TPU v7x, 32 devices: a whole 2x2x4 slice. The times are simulated.
32 devices in a mesh: parts: 2 (over y), blk: 4 (over z), chan: 2 (over x), freq: 2 (over core).
Axes of the slice: x: 2, y: 2, z: 4, core: 2. Of those that a mesh axis runs over, the one named last changes fastest.
Arguments:
- records: bfloat16 [128, 2, 512, 1024], P(('parts', 'blk'), None, 'freq', 'chan'), parts along dimension 0, may hold values from -6 to 6
- templates: bfloat16 [4, 2, 512, 1024], P('blk', None, 'freq', 'chan'), may hold values from -0.125 to 0.125
- masks: int32 [4, 4], replicated, may hold values 0 or 1
- offsets: int32 [4], replicated, may hold values from 0 to 1023
Outputs:
- correlation: float32 [4, 128, 1024], P(None, ('parts', 'blk'), ('chan', 'freq')), parts along dimension 1
There are 2 independent parts, one for each index of `parts`. A program takes and returns all parts, laid end to end along the dimension named above; an argument that names none is the same for every part. Nothing has to cross between parts.
All inputs are finite; a program needn't handle non-finite values.
Results may differ from a plain program's by a relative error of at most 0.0003.
Values may be sent and summed in bfloat16 or wider, within the bound.
No kernel may reach another device: no remote copies, remote signals or barrier semaphores. Data moves between devices by JAX's collectives and lax.ppermute only.
A program may use at most 64 MiB of HBM per device.

v0:
```python
import math

import jax
import jax.numpy as jnp
from jax import lax
from jax.sharding import PartitionSpec as P

NSAMP = 1024
BINS = 512


def rotate_spectra(real_part, imag_part, offsets, first_bin):
    count = real_part.shape[2]
    bin_index = first_bin + lax.iota(jnp.int32, count)
    phase = offsets[:, None] * bin_index[None, :] % NSAMP
    angle = 2.0 * math.pi / NSAMP * phase.astype(jnp.float32)
    cosine = jnp.cos(angle)[:, None, :]
    sine_table = jnp.sin(angle)[:, None, :]
    return (
        real_part * cosine - imag_part * sine_table,
        real_part * sine_table + imag_part * cosine,
    )


def inverse_part(rot_real, rot_imag, first_bin, first_lag, lag_count):
    bin_index = first_bin + lax.iota(jnp.int32, rot_real.shape[2])
    lag_index = first_lag + lax.iota(jnp.int32, lag_count)
    phase = bin_index[:, None] * lag_index[None, :] % NSAMP
    angle = 2.0 * math.pi / NSAMP * phase.astype(jnp.float32)
    scale = math.sqrt(2.0 / BINS)
    first = jnp.einsum("twk,kn->ntw", rot_real, jnp.cos(angle), precision=lax.Precision.HIGHEST)
    second = jnp.einsum("twk,kn->ntw", rot_imag, jnp.sin(angle), precision=lax.Precision.HIGHEST)
    return scale * (first - second)


def shards(records, templates, masks, offsets):
    n_chan = lax.axis_size("chan")
    chan_at = lax.axis_index("chan")
    freq_at = lax.axis_index("freq")
    bin_count = records.shape[2]
    first_bin = freq_at * bin_count
    block_count = masks.shape[1] // n_chan
    block_width = records.shape[3] // block_count
    local_masks = lax.dynamic_slice_in_dim(masks, chan_at * block_count, block_count, 1)
    channel_mask = jnp.repeat(local_masks, block_width, axis=1).astype(jnp.bfloat16)
    masked = lax.all_gather(templates, "blk", axis=0, tiled=True) * channel_mask[:, None, None, :]
    products = jnp.einsum("tpkc,wqkc->tpqwk", masked, records, preferred_element_type=jnp.float32)
    real_part = products[:, 0, 0] + products[:, 1, 1]
    imag_part = products[:, 0, 1] - products[:, 1, 0]
    real_part, imag_part = (real_part, imag_part)
    real_part, imag_part = lax.psum((real_part, imag_part), "chan")
    rot_real, rot_imag = rotate_spectra(real_part, imag_part, offsets, first_bin)
    lag_width = NSAMP // n_chan
    partial_lags = inverse_part(rot_real, rot_imag, first_bin, chan_at * lag_width, lag_width)
    partial_lags = jnp.transpose(partial_lags, (1, 2, 0))
    return lax.psum_scatter(partial_lags, "freq", scatter_dimension=2, tiled=True)


def solution(mesh):
    placed = (P(("parts", "blk"), None, "freq", "chan"), P("blk", None, "freq", "chan"), P(), P())
    return jax.shard_map(
        shards,
        mesh=mesh,
        in_specs=placed,
        out_specs=P(None, ("parts", "blk"), ("chan", "freq")),
        check_vma=False,
    )
```

profile of v0, /device:TPU:0, one launch (start us, length us, event | category | flops | bytes accessed | tf_op | source)
XLA Modules:
  0.0 136.6 jit_solution(9435781748407235772)
XLA Ops:
  6.5 0.0 all-gather.2.cloned.1.call-start
  6.5 0.7 all-gather.2.cloned.1.call-update
  7.3 0.0 all-reduce.3.cloned.1.call-start
  7.3 0.8 dynamic-slice_convert_fusion
  8.1 0.1 broadcast_bitcast_fusion
  8.2 49.4 %all-gather.2.cloned.1.call-done = bf16[4,2,256,512]{3,2,1,0:T(8,128)(2,1)} async-done(((bf16[1,2,256,512]{3,2,1,0:T(8,128)(2,1)}), bf16[4,2,256,512]{3,2,1,0:T(8,128)(2,1)}) %all-gather.2.cloned.1.call-update) | async-done | bytes 2097168 | tf_op jit(solution)/shard_map/all_gather | solution.py:46
  57.6 1.7 %multiply_bitcast_fusion = bf16[4,2,256,512,1]{3,2,1,0,4:T(8,128)(2,1)S(1)} fusion(bf16[4,2,256,512]{3,2,1,0:T(8,128)(2,1)} %all-gather.2.cloned.1.call-done, bf16[4,512]{1,0:T(4,128)(2,1)S(1)} %bitcast.28), kind=kLoop, calls=%fused_computation.3 | loop fusion | flops 1048576 | bytes 4198400 | tf_op jit(solution)/shard_map/mul | solution.py:46
  59.3 13.8 %fusion.3 = f32[4,2,2,16,256]{3,0,2,1,4:T(4,128)S(1)} fusion(bf16[16,2,256,512,1]{3,2,1,0,4:T(8,128)(2,1)} %bitcast.29, bf16[4,2,256,512,1]{3,2,1,0,4:T(8,128)(2,1)S(1)} %multiply_bitcast_fusion), kind=kOutput, calls=%fused_computation.4 | convolution fusion | flops 67108864 | bytes 10747904 | tf_op jit(solution)/shard_map/tpkc,wqkc->tpqwk/dot_general | solution.py:47
  73.1 0.0 copy-start
  73.1 1.0 fusion.12
  74.1 0.9 fusion.14
  75.0 0.0 all-reduce.3.cloned.1.call-update
  75.1 0.2 reduce-scatter.2.cloned.1.call-start
  75.3 0.0 copy-done
  75.3 0.1 fusion.28
  75.4 0.1 copy.21
  75.6 0.1 copy.22
  75.7 38.5 %all-reduce.3.cloned.1.call-done = (f32[4,16,256]{1,0,2:T(4,128)}, f32[4,16,256]{1,0,2:T(4,128)}) async-done(((f32[4,16,256]{1,0,2:T(4,128)}, f32[4,16,256]{1,0,2:T(4,128)}), (f32[4,16,256]{1,0,2:T(4,128)}, f32[4,16,256]{1,0,2:T(4,128)})) %all-reduce.3.cloned.1.call-update) | async-done | bytes 131088 | tf_op jit(solution)/shard_map/psum | solution.py:51
  114.2 1.7 %multiply_add_fusion = (f32[4,16,256]{1,0,2:T(4,128)S(1)}, f32[4,16,256]{1,0,2:T(4,128)S(1)}) fusion(f32[4,16,256]{1,0,2:T(4,128)} %get-tuple-element.5, f32[4,16,256]{1,0,2:T(4,128)} %get-tuple-element.6, f32[4,256]{0,1:T(8,128)S(1)} %copy.22, f32[4,256]{0,1:T(8,128)S(1)} %copy.21), kind=kLoop, calls=%fused_computation.27 | loop fusion | flops 98304 | bytes 270336 | tf_op jit(solution)/shard_map/add | solution.py:21
  115.9 2.9 %fusion.16 = f32[4,16,512]{2,1,0:T(8,128)S(1)} fusion(f32[4,16,256]{1,0,2:T(4,128)S(1)} %get-tuple-element.8, s32[512]{0:T(512)S(1)} %iota_add_fusion, s32[256]{0:T(256)S(1)} %iota_add_fusion.1), kind=kOutput, calls=%fused_computation.22 | convolution fusion | flops 102498304 | bytes 199680 | tf_op jit(solution)/shard_map/twk,kn->ntw/dot_general | solution.py:31
  118.8 3.6 %fusion.8 = f32[4,16,512]{2,1,0:T(8,128)} fusion(f32[4,16,512]{2,1,0:T(8,128)S(1)} %fusion.16, f32[4,16,256]{1,0,2:T(4,128)S(1)} %get-tuple-element.7, s32[512]{0:T(512)S(1)} %iota_add_fusion, s32[256]{0:T(256)S(1)} %iota_add_fusion.1), kind=kOutput, calls=%fused_computation.6 | convolution fusion | flops 102563840 | bytes 330752 | tf_op jit(solution)/shard_map/twk,kn->ntw/dot_general | solution.py:32
  122.4 0.0 reduce-scatter.2.cloned.1.call-update
  122.4 7.7 %reduce-scatter.2.cloned.1.call-done = f32[4,16,256]{2,1,0:T(8,128)} async-done(((f32[4,16,512]{2,1,0:T(8,128)}), f32[4,16,256]{2,1,0:T(8,128)}) %reduce-scatter.2.cloned.1.call-update) | async-done | bytes 65552 | tf_op jit(solution)/shard_map/reduce_scatter | solution.py:56
  (3 shorter events, 0.0 us)
Async XLA Ops:
  6.5 51.1 %all-gather.2.cloned.1.call-start = ((), (), s32[]{:S(2)}) async-start(), calls=%async_computation.1 | async-start | bytes 2621440 | tf_op jit(solution)/shard_map/all_gather | solution.py:46
  7.3 106.9 %all-reduce.3.cloned.1.call-start = ((), (), s32[]{:S(2)}) async-start(), calls=%async_computation.3 | async-start | bytes 2097152 | tf_op jit(solution)/shard_map/psum | solution.py:51
  73.1 2.1 %copy-start = (s32[4]{0:T(128)S(1)}, s32[4]{0:T(128)}, u32[]{:S(2)}) copy-start(s32[4]{0:T(128)} %param.7) | copy-start | bytes 52
  75.1 55.0 %reduce-scatter.2.cloned.1.call-start = ((), (), s32[]{:S(2)}) async-start(), calls=%async_computation.2 | async-start | bytes 196608 | tf_op jit(solution)/shard_map/reduce_scatter | solution.py:56
Sparse Core Ops, SparseCore 0:
  8.9 48.6 all-gather.1
  75.2 38.9 all-reduce.2
  122.5 7.5 reduce-scatter.1
where the time goes:
time: 137 us
  waiting for transfers between devices  96.3 us (70%)
  matrix products  20.3 us (15%)
  between operations  13.2 us (10%)
  other arithmetic  6.24 us (5%)
    all_gather x1, waiting for transfers between devices, shards(): lax.all_gather(templates, 'blk', axis=0, tiled=True)  49.4 us
    psum x1, waiting for transfers between devices, shards(): real_part, imag_part = lax.psum((real_part, imag_part), 'chan')  38.5 us
    dot_general x1, matrix products, shards(): jnp.einsum('tpkc,wqkc->tpqwk', masked, records, preferred_element_type=jn...  13.8 us
    reduce_scatter x1, waiting for transfers between devices, shards(): lax.psum_scatter(partial_lags, 'freq', scatter_dimension=2, tiled=True)  7.67 us
    dot_general x1, matrix products, inverse_part(): jnp.einsum('twk,kn->ntw', rot_imag, jnp.sin(angle), precision=lax.Precisi...  3.56 us
    dot_general x1, matrix products, inverse_part(): jnp.einsum('twk,kn->ntw', rot_real, jnp.cos(angle), precision=lax.Precisi...  2.88 us
  transfers between devices with their start and end apart: 3, of which 3 were waited for; matrix products, arithmetic and copies ran while one was open for 1% of the time, Pallas kernels for 0%

commit v1 on v0

v1 whole, which is shorter than its diff:
```python
import functools
import math

import jax
import jax.numpy as jnp
import numpy as np
from jax import lax
from jax.experimental import pallas as pl
from jax.experimental.pallas import tpu as pltpu
from jax.sharding import PartitionSpec as P

NSAMP = 1024
BINS = 512
SUB = 64
FOLD = 256


def lag_tables():
    bins = np.arange(BINS).reshape(-1, SUB)
    angle = 2.0 * math.pi / NSAMP * (bins[..., None] * np.arange(FOLD) % NSAMP)
    table = math.sqrt(2.0 / BINS) * np.concatenate([np.cos(angle), -np.sin(angle)], axis=1)
    table = table.astype(np.float32)
    high = table.astype(jnp.bfloat16)
    low = (table - high.astype(np.float32)).astype(jnp.bfloat16)
    return high, low


def two_halves(values):
    high = values.astype(jnp.bfloat16)
    return high, (values - high.astype(jnp.float32)).astype(jnp.bfloat16)


def product(left, right, contract):
    return lax.dot_general(left, right, ((contract[:1], contract[1:]), ((), ())), preferred_element_type=jnp.float32)


def lags_kernel(plan, n_masks, n_chan, at, records, turn, high, low, *rest):
    d, starts, n_before, others, blocks = plan
    pieces, rest = rest[: len(starts)], rest[len(starts) :]
    before, rest = rest[:n_before], rest[n_before:]
    finished, outs = rest[: len(others)], rest[len(others) :]
    windows, width = records.shape[0], records.shape[3]
    template_at = at[0] ^ d
    lane = lax.broadcasted_iota(jnp.int32, (1, width), 1)
    n_here = n_masks // n_chan
    mask = jnp.zeros((1, width), jnp.float32)
    for b in range(n_here):
        here = at[5 + template_at * n_masks + at[2] * n_here + b]
        mask = jnp.where(lane // (width // n_here) == b, here.astype(jnp.float32), mask)
    mask = mask.astype(jnp.bfloat16)
    row = lax.broadcasted_iota(jnp.int32, (2 * SUB, 2 * SUB), 0)
    lane = lax.broadcasted_iota(jnp.int32, (2 * SUB, 2 * SUB), 1)
    same_bin = row % SUB == lane % SUB
    pairs = windows // 2
    order = [w for v in range(pairs) for w in (v, v + pairs)]
    real_lane = lax.broadcasted_iota(jnp.int32, (windows, 2 * SUB), 1) < SUB
    straight, turned, tables = [], [], []
    for piece, (fixed, moved) in zip(pieces, starts):
        for sub in range(piece.shape[2] // SUB):
            run = fixed // SUB + sub + (at[3] * (moved // SUB) if moved else 0)
            bins = pl.ds(pl.multiple_of(run * SUB, SUB), SUB)
            first, second = (piece[0, part, sub * SUB : (sub + 1) * SUB, :] * mask for part in range(2))
            weights = jnp.concatenate(
                [jnp.concatenate([first, second], axis=1), jnp.concatenate([-second, first], axis=1)], axis=0
            )
            rows = jnp.concatenate(
                [jnp.concatenate([records[w, 0, bins, :], records[w, 1, bins, :]], axis=1) for w in order], axis=0
            )
            every = product(weights, rows, (1, 1))
            every = [jnp.where(same_bin, every[:, v * 2 * SUB : (v + 1) * 2 * SUB], 0.0) for v in range(pairs)]
            real = jnp.concatenate([jnp.sum(e[:SUB], axis=0, keepdims=True) for e in every], axis=0)
            imag = jnp.concatenate([jnp.sum(e[SUB:], axis=0, keepdims=True) for e in every], axis=0)
            real = jnp.concatenate([real, pltpu.roll(real, SUB, 1)], axis=0)
            imag = jnp.concatenate([pltpu.roll(imag, SUB, 1), imag], axis=0)
            spectrum = jnp.where(real_lane, real, imag)
            cosine, sine_table = (turn[template_at, i, pl.ds(run, 1)] for i in range(2))
            spectrum = spectrum * cosine + pltpu.roll(spectrum, SUB, 1) * sine_table
            straight.append(spectrum)
            turned.append(jnp.where(real_lane, 1.0, -1.0) * pltpu.roll(spectrum, SUB, 1))
            tables.append(at[1] + run)
    straight, turned = (jnp.concatenate(s, axis=1) for s in (straight, turned))
    lane = lax.broadcasted_iota(jnp.int32, straight.shape, 1) % 4
    picked = [jnp.where(lane == r, straight, 0.0) for r in range(4)]
    picked += [jnp.where(lane == r, turned, 0.0) for r in (1, 3)]
    rows = jnp.concatenate(picked, axis=0)
    rows_high, rows_low = two_halves(rows)
    table_high, table_low = (jnp.concatenate([t[run] for run in tables], axis=0) for t in (high, low))
    both = product(jnp.concatenate([rows_high, rows_low], axis=0), table_high, (1, 0))
    sums = both[: rows.shape[0]] + both[rows.shape[0] :] + product(rows_high, table_low, (1, 0))
    re0, re1, re2, re3, im1, im3 = (sums[i * windows : (i + 1) * windows] for i in range(6))
    even, odd, even_turned, odd_turned = re0 + re2, re1 + re3, re0 - re2, im1 - im3
    found = jnp.concatenate([even + odd, even_turned - odd_turned, even - odd, even_turned + odd_turned], axis=1)
    for b in before:
        found += b[...]
    if blocks is None:
        outs[0][...] = found
        return
    *outs, lags = outs
    block = lags.shape[2]
    for i, whole in enumerate([other[...] for other in finished] + [found]):
        for n in range(blocks):
            lags[n] = whole[:, n * block : (n + 1) * block]
        for n in range(blocks):
            outs[n][i] = lags[at[4] ^ n]


def template_lags(split, at, held, d, pieces, before=(), others=None, blocks=None):
    records = held[0]
    windows = records.shape[0]
    starts = tuple(start for _, start in pieces)
    plan = (d, starts, len(before), others or (), None if others is None else blocks)
    whole = pl.BlockSpec(memory_space=pltpu.VMEM)
    if others is None:
        out_shape = [jax.ShapeDtypeStruct((windows, NSAMP), jnp.float32)]
        scratch = []
    else:
        block = (windows, NSAMP // blocks)
        out_shape = [jax.ShapeDtypeStruct((len(others) + 1,) + block, jnp.float32)] * blocks
        scratch = [pltpu.VMEM((blocks,) + block, jnp.float32)]
    operands = (*held, *(piece for piece, _ in pieces), *before, *(others or ()))
    return pl.pallas_call(
        functools.partial(lags_kernel, plan, *split),
        in_specs=[pl.BlockSpec(memory_space=pltpu.SMEM)] + [whole] * len(operands),
        out_specs=[whole] * len(out_shape),
        out_shape=out_shape,
        scratch_shapes=scratch,
        compiler_params=pltpu.CompilerParams(vmem_limit_bytes=24 * 2**20),
    )(at, *operands)


def sum_kernel(orders, at, *refs):
    *parts, out = refs
    per = len(parts) // len(orders)
    for g, order in enumerate(orders):
        for i, d in enumerate(order):
            total = parts[g * per][i]
            for part in parts[g * per + 1 : (g + 1) * per]:
                total += part[i]
            out[at[0] ^ d] = total


def partners(n, d):
    return [(i, i ^ d) for i in range(n)]


def after(value, *others):
    return lax.optimization_barrier((value,) + others)[0]


def shards(records, templates, masks, offsets):
    n_blk, n_chan, n_freq, n_parts = (lax.axis_size(a) for a in ("blk", "chan", "freq", "parts"))
    blk_at, chan_at, freq_at, part_at = (lax.axis_index(a) for a in ("blk", "chan", "freq", "parts"))
    windows, _, bin_count, width = records.shape
    runs = bin_count // SUB
    blocks = n_chan * n_freq
    split = (masks.shape[1], n_chan)
    at = jnp.concatenate(
        [
            jnp.stack([blk_at, freq_at * runs, chan_at, part_at, chan_at * n_freq + freq_at]),
            masks.reshape(-1),
        ]
    ).astype(jnp.int32)
    bin_index = (freq_at * bin_count + lax.iota(jnp.int32, bin_count)).reshape(runs, 1, SUB)
    phase = offsets[:, None, None, None] * bin_index % NSAMP
    angle = 2.0 * math.pi / NSAMP * phase.astype(jnp.float32)
    cosine, sine_table = jnp.cos(angle), jnp.sin(angle)
    turn = jnp.stack(
        [jnp.concatenate([cosine, cosine], axis=2), jnp.concatenate([-sine_table, sine_table], axis=2)], axis=1
    ).reshape(offsets.shape[0], 2, runs, 2 * SUB)
    high, low = (jnp.asarray(t) for t in lag_tables())
    held = [pltpu.with_memory_space_constraint(a, pltpu.VMEM) for a in (records, turn, high, low)]

    def exchange(found):
        return [found[0]] + [lax.ppermute(found[n], ("chan", "freq"), partners(blocks, n)) for n in range(1, blocks)]

    half = bin_count // 2
    mine = lax.dynamic_slice_in_dim(templates, part_at * half, half, 2)
    swap = lambda a: lax.ppermute(a, "parts", partners(2, 1))
    far = sorted(range(2, n_blk), key=lambda d: -(d & -d))
    arrived = {d: lax.ppermute(mine, "blk", partners(n_blk, d)) for d in far}
    near = lax.ppermute(templates, "blk", partners(n_blk, 1))
    own = (0, half)
    other = (half, -half)
    found = {0: template_lags(split, at, held, 0, [(templates, (0, 0))])[0]}
    swapped = {}
    last = found[0]
    for d in far:
        swapped[d] = swap(after(arrived[d], last))
        last = template_lags(split, at, held, d, [(arrived[d], own)])[0]
        found[d] = last
    for d in far[:-1]:
        found[d] = template_lags(split, at, held, d, [(swapped[d], other)], before=[found[d]])[0]
    d = far[-1]
    ready = [e for e in found if e != d]
    first = exchange(template_lags(split, at, held, 1, [(near, (0, 0))], others=[found[e] for e in ready], blocks=blocks))
    last = exchange(template_lags(split, at, held, d, [(swapped[d], other)], before=[found[d]], others=[], blocks=blocks))
    return pl.pallas_call(
        functools.partial(sum_kernel, (ready + [1], [d])),
        in_specs=[pl.BlockSpec(memory_space=pltpu.SMEM)] + [pl.BlockSpec(memory_space=pltpu.VMEM)] * (2 * blocks),
        out_specs=pl.BlockSpec(memory_space=pltpu.VMEM),
        out_shape=jax.ShapeDtypeStruct((n_blk, windows, NSAMP // blocks), jnp.float32),
        compiler_params=pltpu.CompilerParams(vmem_limit_bytes=24 * 2**20),
    )(at, *first, *last)


def solution(mesh):
    placed = (P(("parts", "blk"), None, "freq", "chan"), P("blk", None, "freq", "chan"), P(), P())
    return jax.shard_map(
        shards,
        mesh=mesh,
        in_specs=placed,
        out_specs=P(None, ("parts", "blk"), ("chan", "freq")),
        check_vma=False,
    )
```

time: 137 us -> 53.9 us (0.39)
  waiting for transfers between devices: 96.3 us -> 12.2 us
  matrix products: 20.3 us -> 0 us
  Pallas kernels: 0 us -> 18.5 us
  between operations: 13.2 us -> 0.12 us
  starting transfers between devices: 0.26 us -> 13.2 us
  local copies, waits for them, and re-layouts: 0.36 us -> 8.5 us
  other arithmetic: 6.24 us -> 1.04 us
    all_gather x1 -> x0, waiting for transfers between devices: 49.4 us -> none  [shards(): lax.all_gather(templates, 'blk', axis=0, tiled=True)]
    psum x1 -> x0, waiting for transfers between devices: 38.5 us -> none  [shards(): real_part, imag_part = lax.psum((real_part, imag_part), 'chan')]
    dot_general x3 -> x0, matrix products: 20.3 us -> none  [the longest x1 13.8 us: shards(): jnp.einsum('tpkc,wqkc->tpqwk', masked, records, preferred_element_type=jn...]
    pallas_call x0 -> x7, Pallas kernels: none -> 18.5 us  [the longest x6 17.3 us: template_lags(): pl.pallas_call(functools.partial(lags_kernel, plan, *split), in_specs=[pl...]
    ppermute x0 -> x11, starting transfers between devices: none -> 13.2 us  [the longest x2 5.45 us: shards(): arrived = {d: lax.ppermute(mine, 'blk', partners(n_blk, d)) for d in far}]
    ppermute x0 -> x11, waiting for transfers between devices: none -> 12.2 us  [the longest x2 4.39 us: shards(): arrived = {d: lax.ppermute(mine, 'blk', partners(n_blk, d)) for d in far}]
    reduce_scatter x1 -> x0, waiting for transfers between devices: 7.67 us -> none  [shards(): lax.psum_scatter(partial_lags, 'freq', scatter_dimension=2, tiled=True)]
    unnamed x4 -> x9, local copies, waits for them, and re-layouts: 0.09 us -> 6.5 us
  transfers between devices with their start and end apart: 3 -> 11, of which waited for: 3 -> 4; matrix products, arithmetic and copies ran while one was open for 1% -> 4% of each run, Pallas kernels for 0% -> 32%
where the time goes in v1:
time: 53.9 us; the launch traced here: 53.5 us
  Pallas kernels  18.5 us (34%)
  starting transfers between devices  13.2 us (24%)
  waiting for transfers between devices  12.2 us (23%)
  local copies, waits for them, and re-layouts  8.5 us (16%)
  other arithmetic  1.04 us (2%)
    pallas_call x6, Pallas kernels, template_lags(): pl.pallas_call(functools.partial(lags_kernel, plan, *split), in_specs=[pl...  17.3 us
    unnamed x9, local copies, waits for them, and re-layouts  6.5 us
    ppermute x2, starting transfers between devices, shards(): arrived = {d: lax.ppermute(mine, 'blk', partners(n_blk, d)) for d in far}  5.45 us
    ppermute x6, starting transfers between devices, exchange(): lax.ppermute(found[n], ('chan', 'freq'), partners(blocks, n))  5.39 us
    ppermute x2, waiting for transfers between devices, shards(): arrived = {d: lax.ppermute(mine, 'blk', partners(n_blk, d)) for d in far}  4.39 us
    ppermute x2, waiting for transfers between devices, shards(): swap = lambda a: lax.ppermute(a, 'parts', partners(2, 1))  4.32 us
    ppermute x6, waiting for transfers between devices, exchange(): lax.ppermute(found[n], ('chan', 'freq'), partners(blocks, n))  3.51 us
    ppermute x2, starting transfers between devices, shards(): swap = lambda a: lax.ppermute(a, 'parts', partners(2, 1))  2.09 us
  transfers between devices with their start and end apart: 11, of which 4 were waited for; matrix products, arithmetic and copies ran while one was open for 4% of the time, Pallas kernels for 32%

profile of v1, /device:TPU:0, one launch (start us, length us, event | category | flops | bytes accessed | tf_op | source)
XLA Modules:
  0.0 53.5 jit_solution(10847125303213202656)
XLA Ops:
  0.0 1.0 %constant_dynamic-slice_fusion = bf16[1,2,128,512]{3,2,1,0:T(8,128)(2,1)S(1)} fusion(bf16[1,2,256,512]{3,2,1,0:T(8,128)(2,1)} %rest_0_.1, s32[]{:T(128)S(6)} %select_n.27), kind=kLoop, calls=%fused_computation.11 | loop fusion | bytes 524292 | tf_op jit(solution)/shard_map/dynamic_slice | solution.py:177
  1.0 4.1 %collective-permute-start.1 = (bf16[1,2,128,512]{3,2,1,0:T(8,128)(2,1)S(1)}, bf16[1,2,128,512]{3,2,1,0:T(8,128)(2,1)S(1)}, u32[]{:S(2)}, u32[]{:S(2)}) collective-permute-start(bf16[1,2,128,512]{3,2,1,0:T(8,128)(2,1)S(1)} %constant_dynamic-slice_fusion), channel_id=1, source_target_pairs={{0,8},{4,12},{8,0},{12,4},{1,9},{5,13},{9,1},{13,5},{2,10},{6,14},... | collective-permute-start | bytes 786440 | tf_op jit(solution)/shard_map/ppermute | solution.py:180
  5.1 1.3 %collective-permute-start.6 = (bf16[1,2,128,512]{3,2,1,0:T(8,128)(2,1)S(1)}, bf16[1,2,128,512]{3,2,1,0:T(8,128)(2,1)S(1)}, u32[]{:S(2)}, u32[]{:S(2)}) collective-permute-start(bf16[1,2,128,512]{3,2,1,0:T(8,128)(2,1)S(1)} %constant_dynamic-slice_fusion), channel_id=1, source_target_pairs={{0,12},{4,8},{8,4},{12,0},{1,13},{5,9},{9,5},{13,1},{2,14},{6,10},... | collective-permute-start | bytes 786440 | tf_op jit(solution)/shard_map/ppermute | solution.py:180
  6.4 0.2 collective-permute-start
  6.7 1.0 %fusion.5 = (f32[4,4,1,64]{3,2,1,0:T(1,128)S(1)}, f32[4,4,1,64]{3,2,1,0:T(1,128)S(1)}, f32[4,4,1,64]{3,2,1,0:T(1,128)S(1)}) fusion(s32[4,64]{1,0:T(4,128)S(1)} %add_add_fusion, s32[4]{0:T(128)} %param.9), kind=kLoop, calls=%fused_computation.14 | loop fusion | flops 15360 | bytes 13328 | tf_op jit(solution)/shard_map/neg | solution.py:168
  7.7 0.1 stack.29
  7.8 0.1 stack.30
  7.9 0.8 %reshape.84 = s32[16]{0:T(128)S(1)} reshape(s32[4,4]{1,0:T(4,128)} %param.8) | data formatting | bytes 128 | tf_op jit(solution)/shard_map/reshape | solution.py:160
  8.6 0.1 concatenate.10.at
  8.7 0.0 copy-start
  8.7 3.4 %copy-done = bf16[16,2,256,512]{3,2,1,0:T(8,128)(2,1)S(1)} copy-done((bf16[16,2,256,512]{3,2,1,0:T(8,128)(2,1)S(1)}, bf16[16,2,256,512]{3,2,1,0:T(8,128)(2,1)}, u32[]{:S(2)}) %copy-start) | copy-done | bytes 8388632
  12.1 0.0 copy-start.1
  12.1 1.0 %copy-done.1 = bf16[8,128,256]{2,1,0:T(8,128)(2,1)S(1)} copy-done((bf16[8,128,256]{2,1,0:T(8,128)(2,1)S(1)}, bf16[8,128,256]{2,1,0:T(8,128)(2,1)}, u32[]{:S(2)}) %copy-start.1) | copy-done | bytes 524312
  13.2 0.0 copy-start.2
  13.2 1.0 %copy-done.2 = bf16[8,128,256]{2,1,0:T(8,128)(2,1)S(1)} copy-done((bf16[8,128,256]{2,1,0:T(8,128)(2,1)S(1)}, bf16[8,128,256]{2,1,0:T(8,128)(2,1)}, u32[]{:S(2)}) %copy-start.2) | copy-done | bytes 524312
  14.2 0.0 copy-start.3
  14.2 1.0 %copy-done.3 = bf16[1,2,256,512]{3,2,1,0:T(8,128)(2,1)S(1)} copy-done((bf16[1,2,256,512]{3,2,1,0:T(8,128)(2,1)S(1)}, bf16[1,2,256,512]{3,2,1,0:T(8,128)(2,1)}, u32[]{:S(2)}) %copy-start.3) | copy-done | bytes 524312
  15.2 3.8 %shard_map.64.rest_1_ = f32[16,1024]{1,0:T(8,128)S(1)} custom-call(s32[21]{0:T(128)S(1)} %concatenate.10.at, bf16[16,2,256,512]{3,2,1,0:T(8,128)(2,1)S(1)} %copy-done, f32[4,2,4,128]{3,2,1,0:T(4,128)S(1)} %constant_dynamic-update-slice_fusion.turn, bf16[8,128,256]{2,1,0:T(8,128)(2,1)S(1)} %copy-done.1, bf16[8,128,256]{2,1,0:T(8,128)(2,1)S(1)} %copy-done.2, ...), custom_call_target="tpu_custom_call" | custom-call | tf_op jit(solution)/shard_map/pallas_call | solution.py:121
  19.1 4.4 %collective-permute-done.1.rest_0_ = bf16[1,2,128,512]{3,2,1,0:T(8,128)(2,1)S(1)} collective-permute-done((bf16[1,2,128,512]{3,2,1,0:T(8,128)(2,1)S(1)}, bf16[1,2,128,512]{3,2,1,0:T(8,128)(2,1)S(1)}, u32[]{:S(2)}, u32[]{:S(2)}) %collective-permute-start.1) | collective-permute-done | bytes 262176 | tf_op jit(solution)/shard_map/ppermute | solution.py:180
  23.5 1.9 %collective-permute-start.2 = (bf16[1,2,128,512]{3,2,1,0:T(8,128)(2,1)S(1)}, bf16[1,2,128,512]{3,2,1,0:T(8,128)(2,1)S(1)}, u32[]{:S(2)}, u32[]{:S(2)}) collective-permute-start(bf16[1,2,128,512]{3,2,1,0:T(8,128)(2,1)S(1)} %collective-permute-done.1.rest_0_), channel_id=1, source_target_pairs={{0,16},{16,0},{1,17},{17,1},{2,18},{18,2},{3,19},{19,3},{4,20},{20... | collective-permute-start | bytes 786440 | tf_op jit(solution)/shard_map/ppermute | solution.py:178
  25.4 2.4 %shard_map.65.rest_1_ = f32[16,1024]{1,0:T(8,128)S(1)} custom-call(s32[21]{0:T(128)S(1)} %concatenate.10.at, bf16[16,2,256,512]{3,2,1,0:T(8,128)(2,1)S(1)} %copy-done, f32[4,2,4,128]{3,2,1,0:T(4,128)S(1)} %constant_dynamic-update-slice_fusion.turn, bf16[8,128,256]{2,1,0:T(8,128)(2,1)S(1)} %copy-done.1, bf16[8,128,256]{2,1,0:T(8,128)(2,1)S(1)} %copy-done.2, ...), custom_call_target="tpu_custom_call" | custom-call | tf_op jit(solution)/shard_map/pallas_call | solution.py:121
  27.8 0.0 collective-permute-done.6.rest_0_
  27.8 0.2 collective-permute-start.7
  28.0 4.3 %collective-permute-done.2.rest_0_ = bf16[1,2,128,512]{3,2,1,0:T(8,128)(2,1)S(1)} collective-permute-done((bf16[1,2,128,512]{3,2,1,0:T(8,128)(2,1)S(1)}, bf16[1,2,128,512]{3,2,1,0:T(8,128)(2,1)S(1)}, u32[]{:S(2)}, u32[]{:S(2)}) %collective-permute-start.2) | collective-permute-done | bytes 262176 | tf_op jit(solution)/shard_map/ppermute | solution.py:178
  32.3 2.4 %shard_map.66.rest_2_ = f32[16,1024]{1,0:T(8,128)S(1)} custom-call(s32[21]{0:T(128)S(1)} %concatenate.10.at, bf16[16,2,256,512]{3,2,1,0:T(8,128)(2,1)S(1)} %copy-done, f32[4,2,4,128]{3,2,1,0:T(4,128)S(1)} %constant_dynamic-update-slice_fusion.turn, bf16[8,128,256]{2,1,0:T(8,128)(2,1)S(1)} %copy-done.1, bf16[8,128,256]{2,1,0:T(8,128)(2,1)S(1)} %copy-done.2, ...), custom_call_target="tpu_custom_call" | custom-call | tf_op jit(solution)/shard_map/pallas_call | solution.py:121
  34.7 0.0 collective-permute-done.rest_0_
  34.7 3.8 %shard_map.67 = (f32[3,16,256]{2,1,0:T(8,128)S(1)}, f32[3,16,256]{2,1,0:T(8,128)S(1)}, f32[3,16,256]{2,1,0:T(8,128)S(1)}, f32[3,16,256]{2,1,0:T(8,128)S(1)}) custom-call(s32[21]{0:T(128)S(1)} %concatenate.10.at, bf16[16,2,256,512]{3,2,1,0:T(8,128)(2,1)S(1)} %copy-done, f32[4,2,4,128]{3,2,1,0:T(4,128)S(1)} %constant_dynamic-update-slice_fusion.turn, ...), custom_call_target="tpu_custom_call" | custom-call | tf_op jit(solution)/shard_map/pallas_call | solution.py:121
  38.6 0.1 collective-permute-start.3
  38.7 1.7 %collective-permute-start.4 = (f32[3,16,256]{2,1,0:T(8,128)S(1)}, f32[3,16,256]{2,1,0:T(8,128)S(1)}, u32[]{:S(2)}, u32[]{:S(2)}) collective-permute-start(f32[3,16,256]{2,1,0:T(8,128)S(1)} %get-tuple-element.18), channel_id=1, source_target_pairs={{0,2},{1,3},{2,0},{3,1},{4,6},{5,7},{6,4},{7,5},{8,10},{9,11},{10,... | collective-permute-start | bytes 147464 | tf_op jit(solution)/shard_map/ppermute | solution.py:174
  40.4 0.2 collective-permute-start.5
  40.5 2.4 %shard_map.68.rest_1_ = f32[16,1024]{1,0:T(8,128)S(1)} custom-call(s32[21]{0:T(128)S(1)} %concatenate.10.at, bf16[16,2,256,512]{3,2,1,0:T(8,128)(2,1)S(1)} %copy-done, f32[4,2,4,128]{3,2,1,0:T(4,128)S(1)} %constant_dynamic-update-slice_fusion.turn, bf16[8,128,256]{2,1,0:T(8,128)(2,1)S(1)} %copy-done.1, bf16[8,128,256]{2,1,0:T(8,128)(2,1)S(1)} %copy-done.2, ...), custom_call_target="tpu_custom_call" | custom-call | tf_op jit(solution)/shard_map/pallas_call | solution.py:121
  42.9 0.0 collective-permute-done.7.rest_0_
  42.9 2.4 %shard_map.69 = (f32[1,16,256]{2,1,0:T(8,128)S(1)}, f32[1,16,256]{2,1,0:T(8,128)S(1)}, f32[1,16,256]{2,1,0:T(8,128)S(1)}, f32[1,16,256]{2,1,0:T(8,128)S(1)}) custom-call(s32[21]{0:T(128)S(1)} %concatenate.10.at, bf16[16,2,256,512]{3,2,1,0:T(8,128)(2,1)S(1)} %copy-done, f32[4,2,4,128]{3,2,1,0:T(4,128)S(1)} %constant_dynamic-update-slice_fusion.turn, ...), custom_call_target="tpu_custom_call" | custom-call | tf_op jit(solution)/shard_map/pallas_call | solution.py:121
  45.3 1.7 %collective-permute-start.10 = (f32[1,16,256]{2,1,0:T(8,128)S(1)}, f32[1,16,256]{2,1,0:T(8,128)S(1)}, u32[]{:S(2)}, u32[]{:S(2)}) collective-permute-start(f32[1,16,256]{2,1,0:T(8,128)S(1)} %get-tuple-element.24), channel_id=1, source_target_pairs={{0,3},{1,2},{2,1},{3,0},{4,7},{5,6},{6,5},{7,4},{8,11},{9,10},{10,... | collective-permute-start | bytes 49160 | tf_op jit(solution)/shard_map/ppermute | solution.py:174
  47.0 0.2 collective-permute-start.8
  47.2 1.4 %collective-permute-done.10.refs_7_ = f32[1,16,256]{2,1,0:T(8,128)S(1)} collective-permute-done((f32[1,16,256]{2,1,0:T(8,128)S(1)}, f32[1,16,256]{2,1,0:T(8,128)S(1)}, u32[]{:S(2)}, u32[]{:S(2)}) %collective-permute-start.10) | collective-permute-done | bytes 16416 | tf_op jit(solution)/shard_map/ppermute | solution.py:174
  48.6 1.6 %collective-permute-start.9 = (f32[1,16,256]{2,1,0:T(8,128)S(1)}, f32[1,16,256]{2,1,0:T(8,128)S(1)}, u32[]{:S(2)}, u32[]{:S(2)}) collective-permute-start(f32[1,16,256]{2,1,0:T(8,128)S(1)} %get-tuple-element.23), channel_id=1, source_target_pairs={{0,2},{1,3},{2,0},{3,1},{4,6},{5,7},{6,4},{7,5},{8,10},{9,11},{10,... | collective-permute-start | bytes 49160 | tf_op jit(solution)/shard_map/ppermute | solution.py:174
  50.2 0.0 collective-permute-done.8.refs_5_
  50.2 2.1 %collective-permute-done.9.refs_6_ = f32[1,16,256]{2,1,0:T(8,128)S(1)} collective-permute-done((f32[1,16,256]{2,1,0:T(8,128)S(1)}, f32[1,16,256]{2,1,0:T(8,128)S(1)}, u32[]{:S(2)}, u32[]{:S(2)}) %collective-permute-start.9) | collective-permute-done | bytes 16416 | tf_op jit(solution)/shard_map/ppermute | solution.py:174
  52.3 0.0 collective-permute-done.3.refs_1_
  52.3 0.0 collective-permute-done.4.refs_2_
  52.3 0.0 collective-permute-done.5.refs_3_
  52.3 1.2 %shard_map.70 = f32[4,16,256]{2,1,0:T(8,128)} custom-call(s32[21]{0:T(128)S(1)} %concatenate.10.at, f32[3,16,256]{2,1,0:T(8,128)S(1)} %get-tuple-element.16.refs_0_, f32[3,16,256]{2,1,0:T(8,128)S(1)} %collective-permute-done.3.refs_1_, f32[3,16,256]{2,1,0:T(8,128)S(1)} %collective-permute-done.4.refs_2_, f32[3,16,256]{2,1,0:T(8,128)S(1)} %collective-permute-done.5.refs_3_, ...), custom_call_target="tpu_custom_call" | custom-call | tf_op jit(solution)/shard_map/pallas_call | solution.py:197
  (4 shorter events, 0.1 us)
Async XLA Ops:
  1.0 22.5 %collective-permute-start.1 = (bf16[1,2,128,512]{3,2,1,0:T(8,128)(2,1)S(1)}, bf16[1,2,128,512]{3,2,1,0:T(8,128)(2,1)S(1)}, u32[]{:S(2)}, u32[]{:S(2)}) collective-permute-start(bf16[1,2,128,512]{3,2,1,0:T(8,128)(2,1)S(1)} %constant_dynamic-slice_fusion), channel_id=1, source_target_pairs={{0,8},{4,12},{8,0},{12,4},{1,9},{5,13},{9,1},{13,5},{2,10},{6,14},... | collective-permute-start | bytes 786440 | tf_op jit(solution)/shard_map/ppermute | solution.py:180
  5.1 22.7 %collective-permute-start.6 = (bf16[1,2,128,512]{3,2,1,0:T(8,128)(2,1)S(1)}, bf16[1,2,128,512]{3,2,1,0:T(8,128)(2,1)S(1)}, u32[]{:S(2)}, u32[]{:S(2)}) collective-permute-start(bf16[1,2,128,512]{3,2,1,0:T(8,128)(2,1)S(1)} %constant_dynamic-slice_fusion), channel_id=1, source_target_pairs={{0,12},{4,8},{8,4},{12,0},{1,13},{5,9},{9,5},{13,1},{2,14},{6,10},... | collective-permute-start | bytes 786440 | tf_op jit(solution)/shard_map/ppermute | solution.py:180
  6.4 28.3 %collective-permute-start = (bf16[1,2,256,512]{3,2,1,0:T(8,128)(2,1)}, bf16[1,2,256,512]{3,2,1,0:T(8,128)(2,1)S(1)}, u32[]{:S(2)}, u32[]{:S(2)}) collective-permute-start(bf16[1,2,256,512]{3,2,1,0:T(8,128)(2,1)} %rest_0_.1), channel_id=1, source_target_pairs={{0,4},{4,0},{8,12},{12,8},{1,5},{5,1},{9,13},{13,9},{2,6},{6,2},{1... | collective-permute-start | bytes 1572872 | tf_op jit(solution)/shard_map/ppermute | solution.py:181
  8.7 3.4 %copy-start = (bf16[16,2,256,512]{3,2,1,0:T(8,128)(2,1)S(1)}, bf16[16,2,256,512]{3,2,1,0:T(8,128)(2,1)}, u32[]{:S(2)}) copy-start(bf16[16,2,256,512]{3,2,1,0:T(8,128)(2,1)} %records.11) | copy-start | bytes 25165828
  12.1 1.0 %copy-start.1 = (bf16[8,128,256]{2,1,0:T(8,128)(2,1)S(1)}, bf16[8,128,256]{2,1,0:T(8,128)(2,1)}, u32[]{:S(2)}) copy-start(bf16[8,128,256]{2,1,0:T(8,128)(2,1)} %constant.49.clone.high) | copy-start | bytes 1572868
  13.2 1.0 %copy-start.2 = (bf16[8,128,256]{2,1,0:T(8,128)(2,1)S(1)}, bf16[8,128,256]{2,1,0:T(8,128)(2,1)}, u32[]{:S(2)}) copy-start(bf16[8,128,256]{2,1,0:T(8,128)(2,1)} %constant.50.clone.low) | copy-start | bytes 1572868
  14.2 1.0 %copy-start.3 = (bf16[1,2,256,512]{3,2,1,0:T(8,128)(2,1)S(1)}, bf16[1,2,256,512]{3,2,1,0:T(8,128)(2,1)}, u32[]{:S(2)}) copy-start(bf16[1,2,256,512]{3,2,1,0:T(8,128)(2,1)} %rest_0_.1) | copy-start | bytes 1572868
  23.5 8.8 %collective-permute-start.2 = (bf16[1,2,128,512]{3,2,1,0:T(8,128)(2,1)S(1)}, bf16[1,2,128,512]{3,2,1,0:T(8,128)(2,1)S(1)}, u32[]{:S(2)}, u32[]{:S(2)}) collective-permute-start(bf16[1,2,128,512]{3,2,1,0:T(8,128)(2,1)S(1)} %collective-permute-done.1.rest_0_), channel_id=1, source_target_pairs={{0,16},{16,0},{1,17},{17,1},{2,18},{18,2},{3,19},{19,3},{4,20},{20... | collective-permute-start | bytes 786440 | tf_op jit(solution)/shard_map/ppermute | solution.py:178
  27.8 15.2 %collective-permute-start.7 = (bf16[1,2,128,512]{3,2,1,0:T(8,128)(2,1)S(1)}, bf16[1,2,128,512]{3,2,1,0:T(8,128)(2,1)S(1)}, u32[]{:S(2)}, u32[]{:S(2)}) collective-permute-start(bf16[1,2,128,512]{3,2,1,0:T(8,128)(2,1)S(1)} %collective-permute-done.6.rest_0_), channel_id=1, source_target_pairs={{0,16},{16,0},{1,17},{17,1},{2,18},{18,2},{3,19},{19,3},{4,20},{20... | collective-permute-start | bytes 786440 | tf_op jit(solution)/shard_map/ppermute | solution.py:178
  38.6 13.7 %collective-permute-start.3 = (f32[3,16,256]{2,1,0:T(8,128)S(1)}, f32[3,16,256]{2,1,0:T(8,128)S(1)}, u32[]{:S(2)}, u32[]{:S(2)}) collective-permute-start(f32[3,16,256]{2,1,0:T(8,128)S(1)} %get-tuple-element.17), channel_id=1, source_target_pairs={{0,1},{1,0},{2,3},{3,2},{4,5},{5,4},{6,7},{7,6},{8,9},{9,8},{10,11... | collective-permute-start | bytes 147464 | tf_op jit(solution)/shard_map/ppermute | solution.py:174
  38.7 13.7 %collective-permute-start.4 = (f32[3,16,256]{2,1,0:T(8,128)S(1)}, f32[3,16,256]{2,1,0:T(8,128)S(1)}, u32[]{:S(2)}, u32[]{:S(2)}) collective-permute-start(f32[3,16,256]{2,1,0:T(8,128)S(1)} %get-tuple-element.18), channel_id=1, source_target_pairs={{0,2},{1,3},{2,0},{3,1},{4,6},{5,7},{6,4},{7,5},{8,10},{9,11},{10,... | collective-permute-start | bytes 147464 | tf_op jit(solution)/shard_map/ppermute | solution.py:174
  40.4 12.0 %collective-permute-start.5 = (f32[3,16,256]{2,1,0:T(8,128)S(1)}, f32[3,16,256]{2,1,0:T(8,128)S(1)}, u32[]{:S(2)}, u32[]{:S(2)}) collective-permute-start(f32[3,16,256]{2,1,0:T(8,128)S(1)} %get-tuple-element.19), channel_id=1, source_target_pairs={{0,3},{1,2},{2,1},{3,0},{4,7},{5,6},{6,5},{7,4},{8,11},{9,10},{10,... | collective-permute-start | bytes 147464 | tf_op jit(solution)/shard_map/ppermute | solution.py:174
  45.3 3.2 %collective-permute-start.10 = (f32[1,16,256]{2,1,0:T(8,128)S(1)}, f32[1,16,256]{2,1,0:T(8,128)S(1)}, u32[]{:S(2)}, u32[]{:S(2)}) collective-permute-start(f32[1,16,256]{2,1,0:T(8,128)S(1)} %get-tuple-element.24), channel_id=1, source_target_pairs={{0,3},{1,2},{2,1},{3,0},{4,7},{5,6},{6,5},{7,4},{8,11},{9,10},{10,... | collective-permute-start | bytes 49160 | tf_op jit(solution)/shard_map/ppermute | solution.py:174
  47.0 3.2 %collective-permute-start.8 = (f32[1,16,256]{2,1,0:T(8,128)S(1)}, f32[1,16,256]{2,1,0:T(8,128)S(1)}, u32[]{:S(2)}, u32[]{:S(2)}) collective-permute-start(f32[1,16,256]{2,1,0:T(8,128)S(1)} %get-tuple-element.22), channel_id=1, source_target_pairs={{0,1},{1,0},{2,3},{3,2},{4,5},{5,4},{6,7},{7,6},{8,9},{9,8},{10,11... | collective-permute-start | bytes 49160 | tf_op jit(solution)/shard_map/ppermute | solution.py:174
  48.6 3.7 %collective-permute-start.9 = (f32[1,16,256]{2,1,0:T(8,128)S(1)}, f32[1,16,256]{2,1,0:T(8,128)S(1)}, u32[]{:S(2)}, u32[]{:S(2)}) collective-permute-start(f32[1,16,256]{2,1,0:T(8,128)S(1)} %get-tuple-element.23), channel_id=1, source_target_pairs={{0,2},{1,3},{2,0},{3,1},{4,6},{5,7},{6,4},{7,5},{8,10},{9,11},{10,... | collective-permute-start | bytes 49160 | tf_op jit(solution)/shard_map/ppermute | solution.py:174

commit v2 on v0

v2 whole, which is shorter than its diff:
```python
import functools
import math

import jax
import jax.numpy as jnp
import numpy as np
from jax import lax
from jax.experimental import pallas as pl
from jax.experimental.pallas import tpu as pltpu
from jax.sharding import PartitionSpec as P

NSAMP = 1024
BINS = 512
SUB = 64
FOLD = 256
BATCH = 4
VMEM_LIMIT = 24 * 2**20


def lag_tables():
    bins = np.arange(BINS).reshape(-1, SUB)
    angle = 2.0 * math.pi / NSAMP * (bins[..., None] * np.arange(FOLD) % NSAMP)
    table = math.sqrt(2.0 / BINS) * np.concatenate([np.cos(angle), -np.sin(angle)], axis=1)
    table = table.astype(np.float32)
    high = table.astype(jnp.bfloat16)
    low = (table - high.astype(np.float32)).astype(jnp.bfloat16)
    return high, low


def two_halves(values):
    high = values.astype(jnp.bfloat16)
    return high, (values - high.astype(jnp.float32)).astype(jnp.bfloat16)


def product(left, right, contract):
    return lax.dot_general(left, right, ((contract[:1], contract[1:]), ((), ())), preferred_element_type=jnp.float32)


def mask_row(masks, template_at, width):
    here = masks.shape[1] // lax.axis_size("chan")
    first = lax.axis_index("chan") * here
    lane = lax.broadcasted_iota(jnp.int32, (1, width), 1) // (width // here)
    row = jnp.zeros((1, width), jnp.float32)
    for b in range(here):
        row = jnp.where(lane == b, masks[template_at, first + b].astype(jnp.float32), row)
    return row


def run_spectrum(template_at, run, piece, used, records, turn):
    windows, pairs = records.shape[0], records.shape[0] // 2
    bins = pl.ds(pl.multiple_of(run * SUB, SUB), SUB)
    mask = used[template_at].astype(jnp.bfloat16)
    first, second = piece[0] * mask, piece[1] * mask
    weights = jnp.concatenate(
        [jnp.concatenate([first, second], axis=1), jnp.concatenate([-second, first], axis=1)], axis=0
    )
    row = lax.broadcasted_iota(jnp.int32, (2 * SUB, 2 * SUB), 0)
    lane = lax.broadcasted_iota(jnp.int32, (2 * SUB, 2 * SUB), 1)
    same_bin = row % SUB == lane % SUB
    real, imag = [], []
    for v in range(pairs):
        rows = jnp.concatenate(
            [jnp.concatenate([records[w, 0, bins, :], records[w, 1, bins, :]], axis=1) for w in (v, v + pairs)], axis=0
        )
        every = jnp.where(same_bin, product(weights, rows, (1, 1)), 0.0)
        real.append(jnp.sum(every[:SUB], axis=0, keepdims=True))
        imag.append(jnp.sum(every[SUB:], axis=0, keepdims=True))
    real, imag = jnp.concatenate(real, axis=0), jnp.concatenate(imag, axis=0)
    real = jnp.concatenate([real, pltpu.roll(real, SUB, 1)], axis=0)
    imag = jnp.concatenate([pltpu.roll(imag, SUB, 1), imag], axis=0)
    real_lane = lax.broadcasted_iota(jnp.int32, (windows, 2 * SUB), 1) < SUB
    spectrum = jnp.where(real_lane, real, imag)
    cosine, sine_table = (turn[template_at, i, pl.ds(run, 1)] for i in range(2))
    return spectrum * cosine + pltpu.roll(spectrum, SUB, 1) * sine_table


def all_lags(spectra, high, low):
    runs, windows, width = spectra.shape
    real_lane = lax.broadcasted_iota(jnp.int32, (windows, width), 1) < SUB
    sign = jnp.where(real_lane, 1.0, -1.0)
    straight = jnp.concatenate([spectra[r] for r in range(runs)], axis=1)
    turned = jnp.concatenate([sign * pltpu.roll(spectra[r], SUB, 1) for r in range(runs)], axis=1)
    lane = lax.broadcasted_iota(jnp.int32, straight.shape, 1) % 4
    picked = [jnp.where(lane == r, straight, 0.0) for r in range(4)]
    picked += [jnp.where(lane == r, turned, 0.0) for r in (1, 3)]
    rows = jnp.concatenate(picked, axis=0)
    rows_high, rows_low = two_halves(rows)
    table_high, table_low = (jnp.concatenate([t[r] for r in range(runs)], axis=0) for t in (high, low))
    both = product(jnp.concatenate([rows_high, rows_low], axis=0), table_high, (1, 0))
    sums = both[: rows.shape[0]] + both[rows.shape[0] :] + product(rows_high, table_low, (1, 0))
    re0, re1, re2, re3, im1, im3 = (sums[i * windows : (i + 1) * windows] for i in range(6))
    even, odd, even_turned, odd_turned = re0 + re2, re1 + re3, re0 - re2, im1 - im3
    return [even + odd, even_turned - odd_turned, even - odd, even_turned + odd_turned]


def own_kernel(
    masks, offsets, records, templates, high, low, held, turn, used, held_high, held_low, spectra, template, numbers, sems
):
    runs = turn.shape[2]
    first_run = lax.axis_index("freq") * runs
    small = [
        pltpu.make_async_copy(masks, numbers[0], sems.at[0]),
        pltpu.make_async_copy(offsets, numbers[1], sems.at[1]),
    ]
    pieces = [
        pltpu.make_async_copy(values.at[:, :, pl.ds(r * SUB, SUB), :], to.at[:, :, pl.ds(r * SUB, SUB), :], sem)
        for r in range(runs)
        for values, to, sem in (
            (templates, template, sems.at[4 + 2 * r]),
            (records, held, sems.at[5 + 2 * r]),
        )
    ]
    tables = [
        pltpu.make_async_copy(table.at[pl.ds(first_run, runs)], to, sems.at[2 + i])
        for i, (table, to) in enumerate(((high, held_high), (low, held_low)))
    ]
    for copy in small + pieces + tables:
        copy.start()
    for copy in small:
        copy.wait()
    masks, offsets = numbers
    row = lax.broadcasted_iota(jnp.int32, (runs, 2 * SUB), 0)
    lane = lax.broadcasted_iota(jnp.int32, (runs, 2 * SUB), 1)
    bin_index = (first_run + row) * SUB + lane % SUB
    sign = jnp.where(lane < SUB, -1.0, 1.0)
    for t in range(turn.shape[0]):
        phase = offsets[t] * bin_index % NSAMP
        angle = 2.0 * math.pi / NSAMP * phase.astype(jnp.float32)
        turn[t, 0] = jnp.cos(angle)
        turn[t, 1] = jnp.sin(angle) * sign
        used[t] = mask_row(masks, t, held.shape[3])
    template_at = lax.axis_index("blk")
    for r in range(runs):
        for copy in pieces[2 * r : 2 * r + 2]:
            copy.wait()
        piece = template[0, :, r * SUB : (r + 1) * SUB, :]
        spectra[r] = run_spectrum(template_at, r, piece, used, held, turn)
    for copy in tables:
        copy.wait()


def piece_kernel(plan, held, turn, used, high, low, *rest):
    d, moved, whole = plan
    found = []
    if d is not None:
        piece, *rest = rest
        template_at = lax.axis_index("blk") ^ d
        first = lax.axis_index("parts") * moved[1] + moved[0]
        found = [
            run_spectrum(template_at, first + r, piece[0, :, r * SUB : (r + 1) * SUB, :], used, held, turn)
            for r in range(piece.shape[2] // SUB)
        ]
    if whole is None:
        for r, spectrum in enumerate(found):
            rest[0][r] = spectrum
        return
    n_in = sum(len(w) for w in whole)
    before, outs, (spectra, lags) = rest[:n_in], rest[n_in:-2], rest[-2:]
    at = 0
    for i, starts in enumerate(whole):
        for start, step in starts:
            run = lax.axis_index("parts") * step + start
            for r in range(before[at].shape[0]):
                spectra[i, run + r] = before[at][r]
            at += 1
    for r, spectrum in enumerate(found):
        spectra[len(whole) - 1, first + r] = spectrum
    me = lax.axis_index("chan") * lax.axis_size("freq") + lax.axis_index("freq")
    width = lags.shape[2]
    total = spectra.shape[0]
    for begin in range(0, total, BATCH):
        many = min(BATCH, total - begin)
        rows = jnp.concatenate([spectra[begin + i] for i in range(many)], axis=1)
        folded = all_lags(rows, high, low)
        for i in range(many):
            at = slice(i * held.shape[0], (i + 1) * held.shape[0])
            for n in range(len(outs)):
                start = n * width
                lags[n] = folded[start // FOLD][at, start % FOLD : start % FOLD + width]
            for n in range(len(outs)):
                outs[n][begin + i] = lags[me ^ n]


def sum_kernel(orders, *refs):
    *parts, out = refs
    per = len(parts) // len(orders)
    for g, order in enumerate(orders):
        for i, d in enumerate(order):
            total = parts[g * per][i]
            for part in parts[g * per + 1 : (g + 1) * per]:
                total += part[i]
            out[lax.axis_index("blk") ^ d] = total


IN_SMEM = pl.BlockSpec(memory_space=pltpu.SMEM)
IN_VMEM = pl.BlockSpec(memory_space=pltpu.VMEM)
IN_HBM = pl.BlockSpec(memory_space=pltpu.HBM)
PARAMS = pltpu.CompilerParams(vmem_limit_bytes=VMEM_LIMIT)


def in_vmem(values):
    return [pltpu.with_memory_space_constraint(v, pltpu.VMEM) for v in values]


def in_hbm(values):
    return [pltpu.with_memory_space_constraint(v, pltpu.HBM) for v in values]


def own_template(masks, offsets, records, template, high, low):
    windows, _, bin_count, width = records.shape
    runs = bin_count // SUB
    table = (runs,) + high.shape[1:]
    out_shape = [
        pltpu.VMEM(records.shape, records.dtype),
        pltpu.VMEM((offsets.shape[0], 2, runs, 2 * SUB), jnp.float32),
        pltpu.VMEM((offsets.shape[0], 1, width), jnp.float32),
        pltpu.VMEM(table, high.dtype),
        pltpu.VMEM(table, low.dtype),
        pltpu.VMEM((runs, windows, 2 * SUB), jnp.float32),
    ]
    *held, spectra = pl.pallas_call(
        own_kernel,
        in_specs=[IN_HBM] * 6,
        out_specs=[IN_VMEM] * len(out_shape),
        out_shape=out_shape,
        scratch_shapes=[
            pltpu.VMEM(template.shape, template.dtype),
            (pltpu.SMEM(masks.shape, masks.dtype), pltpu.SMEM(offsets.shape, offsets.dtype)),
            pltpu.SemaphoreType.DMA((2 * runs + 4,)),
        ],
        compiler_params=PARAMS,
    )(*in_hbm((masks, offsets, records, template, high, low)))
    return held, spectra


def add_piece(held, d, moved, piece):
    windows = held[0].shape[0]
    return pl.pallas_call(
        functools.partial(piece_kernel, (d, moved, None)),
        in_specs=[IN_VMEM] * 6,
        out_specs=IN_VMEM,
        out_shape=pltpu.VMEM((piece.shape[2] // SUB, windows, 2 * SUB), jnp.float32),
        compiler_params=PARAMS,
    )(*in_vmem(held), *in_vmem([piece]))


def transform(held, whole, blocks):
    return finish(held, None, None, None, whole, blocks)


def finish(held, d, moved, piece, whole, blocks):
    windows, _, bin_count, _ = held[0].shape
    block = (windows, NSAMP // blocks)
    before = [spectra for pieces in whole for spectra, _ in pieces]
    places = tuple(tuple(at for _, at in pieces) for pieces in whole)
    return pl.pallas_call(
        functools.partial(piece_kernel, (d, moved, places)),
        in_specs=[IN_VMEM] * (len(held) + (piece is not None) + len(before)),
        out_specs=[IN_VMEM] * blocks,
        out_shape=[jax.ShapeDtypeStruct((len(whole),) + block, jnp.float32)] * blocks,
        scratch_shapes=[
            pltpu.VMEM((len(whole), bin_count // SUB, windows, 2 * SUB), jnp.float32),
            pltpu.VMEM((blocks,) + block, jnp.float32),
        ],
        compiler_params=PARAMS,
    )(*in_vmem(held), *in_vmem([] if piece is None else [piece]), *in_vmem(before))


def partners(n, d):
    return [(i, i ^ d) for i in range(n)]


def after(value, *others):
    return lax.optimization_barrier((value,) + others)[0]


def shards(records, templates, masks, offsets):
    n_blk, n_chan, n_freq = (lax.axis_size(a) for a in ("blk", "chan", "freq"))
    windows, _, bin_count, _ = records.shape
    runs = bin_count // SUB
    blocks = n_chan * n_freq
    high, low = (jnp.asarray(t) for t in lag_tables())

    def exchange(found):
        return [found[0]] + [lax.ppermute(found[n], ("chan", "freq"), partners(blocks, n)) for n in range(1, blocks)]

    half = bin_count // 2
    mine = lax.dynamic_slice_in_dim(templates, lax.axis_index("parts") * half, half, 2)
    swap = lambda a: lax.ppermute(a, "parts", partners(2, 1))
    far = sorted(range(2, n_blk), key=lambda d: -(d & -d))
    final = far[-1]
    arrived = {far[0]: lax.ppermute(mine, "blk", partners(n_blk, far[0]))}
    near = lax.ppermute(templates, "blk", partners(n_blk, 1))
    held, spectra = own_template(masks, offsets, records, templates, high, low)
    for d in far[1:]:
        arrived[d] = lax.ppermute(after(mine, spectra), "blk", partners(n_blk, d))
    own, other = (0, runs // 2), (runs // 2, -(runs // 2))
    whole = {0: [(spectra, (0, 0))]}
    last = spectra
    for d in far[:-1]:
        swapped = swap(after(arrived[d], last))
        last = add_piece(held, d, own, arrived[d])
        whole[d] = [(last, own), (add_piece(held, d, other, after(swapped, last)), other)]
        last = whole[d][1][0]
    near = after(near, last)
    near_spectra = add_piece(held, 1, (0, 0), near)
    swapped = swap(after(arrived[final], near_spectra))
    late = add_piece(held, final, own, after(arrived[final], near_spectra))
    ready = list(whole)
    first = exchange(transform(held, [whole[d] for d in ready] + [[(after(near_spectra, late), (0, 0))]], blocks))
    second = exchange(finish(held, final, other, swapped, [[(late, own)]], blocks))
    return pl.pallas_call(
        functools.partial(sum_kernel, (ready + [1], [final])),
        in_specs=[IN_VMEM] * (2 * blocks),
        out_specs=IN_VMEM,
        out_shape=jax.ShapeDtypeStruct((n_blk, windows, NSAMP // blocks), jnp.float32),
        compiler_params=PARAMS,
    )(*first, *second)


def solution(mesh):
    placed = (P(("parts", "blk"), None, "freq", "chan"), P("blk", None, "freq", "chan"), P(), P())
    return jax.shard_map(
        shards,
        mesh=mesh,
        in_specs=placed,
        out_specs=P(None, ("parts", "blk"), ("chan", "freq")),
        check_vma=False,
    )
```

time: 137 us -> 44.8 us (0.33)
  waiting for transfers between devices: 96.3 us -> 12.4 us
  matrix products: 20.3 us -> 0 us
  starting transfers between devices: 0.26 us -> 16.4 us
  Pallas kernels: 0 us -> 14.7 us
  between operations: 13.2 us -> 0.05 us
  other arithmetic: 6.24 us -> 0 us
    all_gather x1 -> x0, waiting for transfers between devices: 49.4 us -> none  [shards(): lax.all_gather(templates, 'blk', axis=0, tiled=True)]
    psum x1 -> x0, waiting for transfers between devices: 38.5 us -> none  [shards(): real_part, imag_part = lax.psum((real_part, imag_part), 'chan')]
    dot_general x3 -> x0, matrix products: 20.3 us -> none  [the longest x1 13.8 us: shards(): jnp.einsum('tpkc,wqkc->tpqwk', masked, records, preferred_element_type=jn...]
    ppermute x0 -> x11, starting transfers between devices: none -> 16.4 us  [the longest x6 4.13 us: exchange(): lax.ppermute(found[n], ('chan', 'freq'), partners(blocks, n))]
    pallas_call x0 -> x8, Pallas kernels: none -> 14.7 us  [the longest x4 6.69 us: add_piece(): pl.pallas_call(functools.partial(piece_kernel, (d, moved, None)), in_spec...]
    ppermute x0 -> x11, waiting for transfers between devices: none -> 12.4 us  [the longest x1 5.23 us: shards(): arrived = {far[0]: lax.ppermute(mine, 'blk', partners(n_blk, far[0]))}]
    reduce_scatter x1 -> x0, waiting for transfers between devices: 7.67 us -> none  [shards(): lax.psum_scatter(partial_lags, 'freq', scatter_dimension=2, tiled=True)]
    add x4 -> x0, other arithmetic: 2.67 us -> none  [the longest x1 1.73 us: rotate_spectra(): real_part * sine_table + imag_part * cosine]
  transfers between devices with their start and end apart: 3 -> 11, of which waited for: 3 -> 6; matrix products, arithmetic and copies ran while one was open for 1% -> 0% of each run, Pallas kernels for 0% -> 32%
where the time goes in v2:
time: 44.8 us; the launch traced here: 44.5 us
  starting transfers between devices  16.4 us (37%)
  Pallas kernels  14.7 us (33%)
  waiting for transfers between devices  12.4 us (28%)
  local copies, waits for them, and re-layouts  0.97 us (2%)
    pallas_call x4, Pallas kernels, add_piece(): pl.pallas_call(functools.partial(piece_kernel, (d, moved, None)), in_spec...  6.69 us
    ppermute x1, waiting for transfers between devices, shards(): arrived = {far[0]: lax.ppermute(mine, 'blk', partners(n_blk, far[0]))}  5.23 us
    pallas_call x1, Pallas kernels, own_template(): pl.pallas_call(own_kernel, in_specs=[IN_HBM] * 6, out_specs=[IN_VMEM] * l...  5.21 us
    ppermute x6, starting transfers between devices, exchange(): lax.ppermute(found[n], ('chan', 'freq'), partners(blocks, n))  4.13 us
    ppermute x1, starting transfers between devices, shards(): arrived = {far[0]: lax.ppermute(mine, 'blk', partners(n_blk, far[0]))}  4.1 us
    ppermute x1, starting transfers between devices, shards(): arrived[d] = lax.ppermute(after(mine, spectra), 'blk', partners(n_blk, d))  3.49 us
    ppermute x6, waiting for transfers between devices, exchange(): lax.ppermute(found[n], ('chan', 'freq'), partners(blocks, n))  3.19 us
    ppermute x2, starting transfers between devices, shards(): swap = lambda a: lax.ppermute(a, 'parts', partners(2, 1))  3.09 us
  transfers between devices with their start and end apart: 11, of which 6 were waited for; matrix products, arithmetic and copies ran while one was open for 0% of the time, Pallas kernels for 32%

profile of v2, /device:TPU:0, one launch (start us, length us, event | category | flops | bytes accessed | tf_op | source)
XLA Modules:
  0.0 44.5 jit_solution(11463266709788479375)
XLA Ops:
  0.0 1.0 %constant_dynamic-slice_fusion = bf16[1,2,128,512]{3,2,1,0:T(8,128)(2,1)S(1)} fusion(bf16[1,2,256,512]{3,2,1,0:T(8,128)(2,1)} %templates.1, s32[]{:T(128)S(6)} %select_n.3), kind=kLoop, calls=%fused_computation | loop fusion | bytes 524292 | tf_op jit(solution)/shard_map/dynamic_slice | solution.py:288
  1.0 4.1 %collective-permute-start = (bf16[1,2,128,512]{3,2,1,0:T(8,128)(2,1)S(1)}, bf16[1,2,128,512]{3,2,1,0:T(8,128)(2,1)S(1)}, u32[]{:S(2)}, u32[]{:S(2)}) collective-permute-start(bf16[1,2,128,512]{3,2,1,0:T(8,128)(2,1)S(1)} %constant_dynamic-slice_fusion), channel_id=1, source_target_pairs={{0,8},{4,12},{8,0},{12,4},{1,9},{5,13},{9,1},{13,5},{2,10},{6,14},... | collective-permute-start | bytes 786440 | tf_op jit(solution)/shard_map/ppermute | solution.py:292
  5.1 1.6 %collective-permute-start.2 = (bf16[1,2,256,512]{3,2,1,0:T(8,128)(2,1)}, bf16[1,2,256,512]{3,2,1,0:T(8,128)(2,1)S(1)}, u32[]{:S(2)}, u32[]{:S(2)}) collective-permute-start(bf16[1,2,256,512]{3,2,1,0:T(8,128)(2,1)} %templates.1), channel_id=1, source_target_pairs={{0,4},{4,0},{8,12},{12,8},{1,5},{5,1},{9,13},{13,9},{2,6},{6,2},{1... | collective-permute-start | bytes 1572872 | tf_op jit(solution)/shard_map/ppermute | solution.py:293
  6.7 5.2 %shard_map.64 = (bf16[16,2,256,512]{3,2,1,0:T(8,128)(2,1)S(1)}, f32[4,2,4,128]{3,2,1,0:T(4,128)S(1)}, f32[4,1,512]{2,1,0:T(1,128)S(1)}, bf16[4,128,256]{2,1,0:T(...) custom-call(s32[4,4]{1,0:T(4,128)} %masks.1, s32[4]{0:T(128)} %offsets.1, ...), custom_call_target="tpu_custom_call" | custom-call | tf_op jit(solution)/shard_map/pallas_call | solution.py:221
  11.9 5.2 %collective-permute-done.rest_0_ = bf16[1,2,128,512]{3,2,1,0:T(8,128)(2,1)S(1)} collective-permute-done((bf16[1,2,128,512]{3,2,1,0:T(8,128)(2,1)S(1)}, bf16[1,2,128,512]{3,2,1,0:T(8,128)(2,1)S(1)}, u32[]{:S(2)}, u32[]{:S(2)}) %collective-permute-start) | collective-permute-done | bytes 262176 | tf_op jit(solution)/shard_map/ppermute | solution.py:292
  17.1 1.6 %collective-permute-start.1 = (bf16[1,2,128,512]{3,2,1,0:T(8,128)(2,1)S(1)}, bf16[1,2,128,512]{3,2,1,0:T(8,128)(2,1)S(1)}, u32[]{:S(2)}, u32[]{:S(2)}) collective-permute-start(bf16[1,2,128,512]{3,2,1,0:T(8,128)(2,1)S(1)} %collective-permute-done.rest_0_), channel_id=1, source_target_pairs={{0,16},{16,0},{1,17},{17,1},{2,18},{18,2},{3,19},{19,3},{4,20},{20... | collective-permute-start | bytes 786440 | tf_op jit(solution)/shard_map/ppermute | solution.py:289
  18.7 3.5 %collective-permute-start.3 = (bf16[1,2,128,512]{3,2,1,0:T(8,128)(2,1)S(1)}, bf16[1,2,128,512]{3,2,1,0:T(8,128)(2,1)S(1)}, u32[]{:S(2)}, u32[]{:S(2)}) collective-permute-start(bf16[1,2,128,512]{3,2,1,0:T(8,128)(2,1)S(1)} %constant_dynamic-slice_fusion), channel_id=1, source_target_pairs={{0,12},{4,8},{8,4},{12,0},{1,13},{5,9},{9,5},{13,1},{2,14},{6,10},... | collective-permute-start | bytes 786440 | tf_op jit(solution)/shard_map/ppermute | solution.py:296
  22.2 1.4 %shard_map.65.rest_1_ = f32[2,16,128]{2,1,0:T(8,128)S(1)} custom-call(bf16[16,2,256,512]{3,2,1,0:T(8,128)(2,1)S(1)} %get-tuple-element.25.held, f32[4,2,4,128]{3,2,1,0:T(4,128)S(1)} %get-tuple-element.26.turn, f32[4,1,512]{2,1,0:T(1,128)S(1)} %get-tuple-element.27.used, bf16[4,128,256]{2,1,0:T(8,128)(2,1)S(1)} %get-tuple-element.28.high, ...), custom_call_target="tpu_custom_call" | custom-call | tf_op jit(solution)/shard_map/pallas_call | solution.py:238
  23.6 1.0 %collective-permute-done.1.rest_0_ = bf16[1,2,128,512]{3,2,1,0:T(8,128)(2,1)S(1)} collective-permute-done((bf16[1,2,128,512]{3,2,1,0:T(8,128)(2,1)S(1)}, bf16[1,2,128,512]{3,2,1,0:T(8,128)(2,1)S(1)}, u32[]{:S(2)}, u32[]{:S(2)}) %collective-permute-start.1) | collective-permute-done | bytes 262176 | tf_op jit(solution)/shard_map/ppermute | solution.py:289
  24.5 1.4 %shard_map.66.rest_2_ = f32[2,16,128]{2,1,0:T(8,128)S(1)} custom-call(bf16[16,2,256,512]{3,2,1,0:T(8,128)(2,1)S(1)} %get-tuple-element.25.held, f32[4,2,4,128]{3,2,1,0:T(4,128)S(1)} %get-tuple-element.26.turn, f32[4,1,512]{2,1,0:T(1,128)S(1)} %get-tuple-element.27.used, bf16[4,128,256]{2,1,0:T(8,128)(2,1)S(1)} %get-tuple-element.28.high, ...), custom_call_target="tpu_custom_call" | custom-call | tf_op jit(solution)/shard_map/pallas_call | solution.py:238
  25.9 0.0 collective-permute-done.2.rest_0_
  25.9 2.5 %shard_map.67.rest_3_ = f32[4,16,128]{2,1,0:T(8,128)S(1)} custom-call(bf16[16,2,256,512]{3,2,1,0:T(8,128)(2,1)S(1)} %get-tuple-element.25.held, f32[4,2,4,128]{3,2,1,0:T(4,128)S(1)} %get-tuple-element.26.turn, f32[4,1,512]{2,1,0:T(1,128)S(1)} %get-tuple-element.27.used, bf16[4,128,256]{2,1,0:T(8,128)(2,1)S(1)} %get-tuple-element.28.high, ...), custom_call_target="tpu_custom_call" | custom-call | tf_op jit(solution)/shard_map/pallas_call | solution.py:238
  28.4 1.0 %collective-permute-done.3.rest_0_ = bf16[1,2,128,512]{3,2,1,0:T(8,128)(2,1)S(1)} collective-permute-done((bf16[1,2,128,512]{3,2,1,0:T(8,128)(2,1)S(1)}, bf16[1,2,128,512]{3,2,1,0:T(8,128)(2,1)S(1)}, u32[]{:S(2)}, u32[]{:S(2)}) %collective-permute-start.3) | collective-permute-done | bytes 262176 | tf_op jit(solution)/shard_map/ppermute | solution.py:296
  29.4 1.5 %collective-permute-start.7 = (bf16[1,2,128,512]{3,2,1,0:T(8,128)(2,1)S(1)}, bf16[1,2,128,512]{3,2,1,0:T(8,128)(2,1)S(1)}, u32[]{:S(2)}, u32[]{:S(2)}) collective-permute-start(bf16[1,2,128,512]{3,2,1,0:T(8,128)(2,1)S(1)} %collective-permute-done.3.rest_0_), channel_id=1, source_target_pairs={{0,16},{16,0},{1,17},{17,1},{2,18},{18,2},{3,19},{19,3},{4,20},{20... | collective-permute-start | bytes 786440 | tf_op jit(solution)/shard_map/ppermute | solution.py:289
  31.0 1.4 %shard_map.68.rest_1_ = f32[2,16,128]{2,1,0:T(8,128)S(1)} custom-call(bf16[16,2,256,512]{3,2,1,0:T(8,128)(2,1)S(1)} %get-tuple-element.25.held, f32[4,2,4,128]{3,2,1,0:T(4,128)S(1)} %get-tuple-element.26.turn, f32[4,1,512]{2,1,0:T(1,128)S(1)} %get-tuple-element.27.used, bf16[4,128,256]{2,1,0:T(8,128)(2,1)S(1)} %get-tuple-element.28.high, ...), custom_call_target="tpu_custom_call" | custom-call | tf_op jit(solution)/shard_map/pallas_call | solution.py:238
  32.4 0.5 %shard_map.69 = (f32[3,16,256]{2,1,0:T(8,128)S(1)}, f32[3,16,256]{2,1,0:T(8,128)S(1)}, f32[3,16,256]{2,1,0:T(8,128)S(1)}, f32[3,16,256]{2,1,0:T(8,128)S(1)}) custom-call(bf16[16,2,256,512]{3,2,1,0:T(8,128)(2,1)S(1)} %get-tuple-element.25.held, f32[4,2,4,128]{3,2,1,0:T(4,128)S(1)} %get-tuple-element.26.turn, f32[4,1,512]{2,1,0:T(1,128)S(1)} %get-tuple-element.27.used, ...), custom_call_target="tpu_custom_call" | custom-call | tf_op jit(solution)/shard_map/pallas_call | solution.py:256
  32.8 0.1 collective-permute-start.4
  32.9 1.5 %collective-permute-start.5 = (f32[3,16,256]{2,1,0:T(8,128)S(1)}, f32[3,16,256]{2,1,0:T(8,128)S(1)}, u32[]{:S(2)}, u32[]{:S(2)}) collective-permute-start(f32[3,16,256]{2,1,0:T(8,128)S(1)} %get-tuple-element.39), channel_id=1, source_target_pairs={{0,2},{1,3},{2,0},{3,1},{4,6},{5,7},{6,4},{7,5},{8,10},{9,11},{10,... | collective-permute-start | bytes 147464 | tf_op jit(solution)/shard_map/ppermute | solution.py:285
  34.5 0.3 collective-permute-start.6
  34.8 2.0 %collective-permute-done.7.rest_0_ = bf16[1,2,128,512]{3,2,1,0:T(8,128)(2,1)S(1)} collective-permute-done((bf16[1,2,128,512]{3,2,1,0:T(8,128)(2,1)S(1)}, bf16[1,2,128,512]{3,2,1,0:T(8,128)(2,1)S(1)}, u32[]{:S(2)}, u32[]{:S(2)}) %collective-permute-start.7) | collective-permute-done | bytes 262176 | tf_op jit(solution)/shard_map/ppermute | solution.py:289
  36.7 1.7 %shard_map.70 = (f32[1,16,256]{2,1,0:T(8,128)S(1)}, f32[1,16,256]{2,1,0:T(8,128)S(1)}, f32[1,16,256]{2,1,0:T(8,128)S(1)}, f32[1,16,256]{2,1,0:T(8,128)S(1)}) custom-call(bf16[16,2,256,512]{3,2,1,0:T(8,128)(2,1)S(1)} %get-tuple-element.25.held, f32[4,2,4,128]{3,2,1,0:T(4,128)S(1)} %get-tuple-element.26.turn, f32[4,1,512]{2,1,0:T(1,128)S(1)} %get-tuple-element.27.used, ...), custom_call_target="tpu_custom_call" | custom-call | tf_op jit(solution)/shard_map/pallas_call | solution.py:256
  38.4 0.1 collective-permute-start.10
  38.5 1.6 %collective-permute-start.8 = (f32[1,16,256]{2,1,0:T(8,128)S(1)}, f32[1,16,256]{2,1,0:T(8,128)S(1)}, u32[]{:S(2)}, u32[]{:S(2)}) collective-permute-start(f32[1,16,256]{2,1,0:T(8,128)S(1)} %get-tuple-element.42), channel_id=1, source_target_pairs={{0,1},{1,0},{2,3},{3,2},{4,5},{5,4},{6,7},{7,6},{8,9},{9,8},{10,11... | collective-permute-start | bytes 49160 | tf_op jit(solution)/shard_map/ppermute | solution.py:285
  40.1 0.0 collective-permute-done.4.refs_1_
  40.1 0.5 %collective-permute-start.9 = (f32[1,16,256]{2,1,0:T(8,128)S(1)}, f32[1,16,256]{2,1,0:T(8,128)S(1)}, u32[]{:S(2)}, u32[]{:S(2)}) collective-permute-start(f32[1,16,256]{2,1,0:T(8,128)S(1)} %get-tuple-element.43), channel_id=1, source_target_pairs={{0,2},{1,3},{2,0},{3,1},{4,6},{5,7},{6,4},{7,5},{8,10},{9,11},{10,... | collective-permute-start | bytes 49160 | tf_op jit(solution)/shard_map/ppermute | solution.py:285
  40.7 0.0 collective-permute-done.5.refs_2_
  40.7 0.0 collective-permute-done.6.refs_3_
  40.7 1.1 %collective-permute-done.10.refs_7_ = f32[1,16,256]{2,1,0:T(8,128)S(1)} collective-permute-done((f32[1,16,256]{2,1,0:T(8,128)S(1)}, f32[1,16,256]{2,1,0:T(8,128)S(1)}, u32[]{:S(2)}, u32[]{:S(2)}) %collective-permute-start.10) | collective-permute-done | bytes 16416 | tf_op jit(solution)/shard_map/ppermute | solution.py:285
  41.8 0.0 collective-permute-done.8.refs_5_
  41.8 2.0 %collective-permute-done.9.refs_6_ = f32[1,16,256]{2,1,0:T(8,128)S(1)} collective-permute-done((f32[1,16,256]{2,1,0:T(8,128)S(1)}, f32[1,16,256]{2,1,0:T(8,128)S(1)}, u32[]{:S(2)}, u32[]{:S(2)}) %collective-permute-start.9) | collective-permute-done | bytes 16416 | tf_op jit(solution)/shard_map/ppermute | solution.py:285
  43.8 0.6 %shard_map.71 = f32[4,16,256]{2,1,0:T(8,128)} custom-call(f32[3,16,256]{2,1,0:T(8,128)S(1)} %get-tuple-element.37.refs_0_, f32[3,16,256]{2,1,0:T(8,128)S(1)} %collective-permute-done.4.refs_1_, f32[3,16,256]{2,1,0:T(8,128)S(1)} %collective-permute-done.5.refs_2_, f32[3,16,256]{2,1,0:T(8,128)S(1)} %collective-permute-done.6.refs_3_, ...), custom_call_target="tpu_custom_call" | custom-call | tf_op jit(solution)/shard_map/pallas_call | solution.py:312
Async XLA Ops:
  1.0 16.1 %collective-permute-start = (bf16[1,2,128,512]{3,2,1,0:T(8,128)(2,1)S(1)}, bf16[1,2,128,512]{3,2,1,0:T(8,128)(2,1)S(1)}, u32[]{:S(2)}, u32[]{:S(2)}) collective-permute-start(bf16[1,2,128,512]{3,2,1,0:T(8,128)(2,1)S(1)} %constant_dynamic-slice_fusion), channel_id=1, source_target_pairs={{0,8},{4,12},{8,0},{12,4},{1,9},{5,13},{9,1},{13,5},{2,10},{6,14},... | collective-permute-start | bytes 786440 | tf_op jit(solution)/shard_map/ppermute | solution.py:292
  5.1 20.9 %collective-permute-start.2 = (bf16[1,2,256,512]{3,2,1,0:T(8,128)(2,1)}, bf16[1,2,256,512]{3,2,1,0:T(8,128)(2,1)S(1)}, u32[]{:S(2)}, u32[]{:S(2)}) collective-permute-start(bf16[1,2,256,512]{3,2,1,0:T(8,128)(2,1)} %templates.1), channel_id=1, source_target_pairs={{0,4},{4,0},{8,12},{12,8},{1,5},{5,1},{9,13},{13,9},{2,6},{6,2},{1... | collective-permute-start | bytes 1572872 | tf_op jit(solution)/shard_map/ppermute | solution.py:293
  17.1 7.4 %collective-permute-start.1 = (bf16[1,2,128,512]{3,2,1,0:T(8,128)(2,1)S(1)}, bf16[1,2,128,512]{3,2,1,0:T(8,128)(2,1)S(1)}, u32[]{:S(2)}, u32[]{:S(2)}) collective-permute-start(bf16[1,2,128,512]{3,2,1,0:T(8,128)(2,1)S(1)} %collective-permute-done.rest_0_), channel_id=1, source_target_pairs={{0,16},{16,0},{1,17},{17,1},{2,18},{18,2},{3,19},{19,3},{4,20},{20... | collective-permute-start | bytes 786440 | tf_op jit(solution)/shard_map/ppermute | solution.py:289
  18.7 10.8 %collective-permute-start.3 = (bf16[1,2,128,512]{3,2,1,0:T(8,128)(2,1)S(1)}, bf16[1,2,128,512]{3,2,1,0:T(8,128)(2,1)S(1)}, u32[]{:S(2)}, u32[]{:S(2)}) collective-permute-start(bf16[1,2,128,512]{3,2,1,0:T(8,128)(2,1)S(1)} %constant_dynamic-slice_fusion), channel_id=1, source_target_pairs={{0,12},{4,8},{8,4},{12,0},{1,13},{5,9},{9,5},{13,1},{2,14},{6,10},... | collective-permute-start | bytes 786440 | tf_op jit(solution)/shard_map/ppermute | solution.py:296
  29.4 7.3 %collective-permute-start.7 = (bf16[1,2,128,512]{3,2,1,0:T(8,128)(2,1)S(1)}, bf16[1,2,128,512]{3,2,1,0:T(8,128)(2,1)S(1)}, u32[]{:S(2)}, u32[]{:S(2)}) collective-permute-start(bf16[1,2,128,512]{3,2,1,0:T(8,128)(2,1)S(1)} %collective-permute-done.3.rest_0_), channel_id=1, source_target_pairs={{0,16},{16,0},{1,17},{17,1},{2,18},{18,2},{3,19},{19,3},{4,20},{20... | collective-permute-start | bytes 786440 | tf_op jit(solution)/shard_map/ppermute | solution.py:289
  32.8 7.3 %collective-permute-start.4 = (f32[3,16,256]{2,1,0:T(8,128)S(1)}, f32[3,16,256]{2,1,0:T(8,128)S(1)}, u32[]{:S(2)}, u32[]{:S(2)}) collective-permute-start(f32[3,16,256]{2,1,0:T(8,128)S(1)} %get-tuple-element.38), channel_id=1, source_target_pairs={{0,1},{1,0},{2,3},{3,2},{4,5},{5,4},{6,7},{7,6},{8,9},{9,8},{10,11... | collective-permute-start | bytes 147464 | tf_op jit(solution)/shard_map/ppermute | solution.py:285
  32.9 7.7 %collective-permute-start.5 = (f32[3,16,256]{2,1,0:T(8,128)S(1)}, f32[3,16,256]{2,1,0:T(8,128)S(1)}, u32[]{:S(2)}, u32[]{:S(2)}) collective-permute-start(f32[3,16,256]{2,1,0:T(8,128)S(1)} %get-tuple-element.39), channel_id=1, source_target_pairs={{0,2},{1,3},{2,0},{3,1},{4,6},{5,7},{6,4},{7,5},{8,10},{9,11},{10,... | collective-permute-start | bytes 147464 | tf_op jit(solution)/shard_map/ppermute | solution.py:285
  34.5 6.2 %collective-permute-start.6 = (f32[3,16,256]{2,1,0:T(8,128)S(1)}, f32[3,16,256]{2,1,0:T(8,128)S(1)}, u32[]{:S(2)}, u32[]{:S(2)}) collective-permute-start(f32[3,16,256]{2,1,0:T(8,128)S(1)} %get-tuple-element.40), channel_id=1, source_target_pairs={{0,3},{1,2},{2,1},{3,0},{4,7},{5,6},{6,5},{7,4},{8,11},{9,10},{10,... | collective-permute-start | bytes 147464 | tf_op jit(solution)/shard_map/ppermute | solution.py:285
  38.4 3.4 %collective-permute-start.10 = (f32[1,16,256]{2,1,0:T(8,128)S(1)}, f32[1,16,256]{2,1,0:T(8,128)S(1)}, u32[]{:S(2)}, u32[]{:S(2)}) collective-permute-start(f32[1,16,256]{2,1,0:T(8,128)S(1)} %get-tuple-element.44), channel_id=1, source_target_pairs={{0,3},{1,2},{2,1},{3,0},{4,7},{5,6},{6,5},{7,4},{8,11},{9,10},{10,... | collective-permute-start | bytes 49160 | tf_op jit(solution)/shard_map/ppermute | solution.py:285
  38.5 3.3 %collective-permute-start.8 = (f32[1,16,256]{2,1,0:T(8,128)S(1)}, f32[1,16,256]{2,1,0:T(8,128)S(1)}, u32[]{:S(2)}, u32[]{:S(2)}) collective-permute-start(f32[1,16,256]{2,1,0:T(8,128)S(1)} %get-tuple-element.42), channel_id=1, source_target_pairs={{0,1},{1,0},{2,3},{3,2},{4,5},{5,4},{6,7},{7,6},{8,9},{9,8},{10,11... | collective-permute-start | bytes 49160 | tf_op jit(solution)/shard_map/ppermute | solution.py:285
  40.1 3.7 %collective-permute-start.9 = (f32[1,16,256]{2,1,0:T(8,128)S(1)}, f32[1,16,256]{2,1,0:T(8,128)S(1)}, u32[]{:S(2)}, u32[]{:S(2)}) collective-permute-start(f32[1,16,256]{2,1,0:T(8,128)S(1)} %get-tuple-element.43), channel_id=1, source_target_pairs={{0,2},{1,3},{2,0},{3,1},{4,6},{5,7},{6,4},{7,5},{8,10},{9,11},{10,... | collective-permute-start | bytes 49160 | tf_op jit(solution)/shard_map/ppermute | solution.py:285

commit v3 on v2

--- a/solution.py
+++ b/solution.py
@@ -13,6 +13,7 @@
 BINS = 512
 SUB = 64
 FOLD = 256
+PIECES = 2
 BATCH = 4
 VMEM_LIMIT = 24 * 2**20
 
@@ -94,7 +95,7 @@
 
 
 def own_kernel(
-    masks, offsets, records, templates, high, low, held, turn, used, held_high, held_low, spectra, template, numbers, sems
+    masks, offsets, records, templates, high, low, held, turn, used, held_high, held_low, spectra, theirs, template, numbers, sems
 ):
     runs = turn.shape[2]
     first_run = lax.axis_index("freq") * runs
@@ -114,6 +115,9 @@
         pltpu.make_async_copy(table.at[pl.ds(first_run, runs)], to, sems.at[2 + i])
         for i, (table, to) in enumerate(((high, held_high), (low, held_low)))
     ]
+    half = theirs.shape[2]
+    from_bin = pl.multiple_of((1 - lax.axis_index("parts")) * half, half)
+    tables.append(pltpu.make_async_copy(templates.at[:, :, pl.ds(from_bin, half), :], theirs, sems.at[4 + 2 * runs]))
     for copy in small + pieces + tables:
         copy.start()
     for copy in small:
@@ -217,8 +221,9 @@
         pltpu.VMEM(table, high.dtype),
         pltpu.VMEM(table, low.dtype),
         pltpu.VMEM((runs, windows, 2 * SUB), jnp.float32),
+        pltpu.VMEM((1, 2, bin_count // 2, width), template.dtype),
     ]
-    *held, spectra = pl.pallas_call(
+    *held, spectra, theirs = pl.pallas_call(
         own_kernel,
         in_specs=[IN_HBM] * 6,
         out_specs=[IN_VMEM] * len(out_shape),
@@ -226,11 +231,11 @@
         scratch_shapes=[
             pltpu.VMEM(template.shape, template.dtype),
             (pltpu.SMEM(masks.shape, masks.dtype), pltpu.SMEM(offsets.shape, offsets.dtype)),
-            pltpu.SemaphoreType.DMA((2 * runs + 4,)),
+            pltpu.SemaphoreType.DMA((2 * runs + 5,)),
         ],
         compiler_params=PARAMS,
     )(*in_hbm((masks, offsets, records, template, high, low)))
-    return held, spectra
+    return held, spectra, theirs
 
 
 def add_piece(held, d, moved, piece):
@@ -266,56 +271,134 @@
     )(*in_vmem(held), *in_vmem([] if piece is None else [piece]), *in_vmem(before))
 
 
+def cut_kernel(template, *rest):
+    *outs, sems = rest
+    at = lax.axis_index("parts") * sum(out.shape[2] for out in outs)
+    copies = []
+    for i, out in enumerate(outs):
+        bins = pl.ds(pl.multiple_of(at, SUB), out.shape[2])
+        copies.append(pltpu.make_async_copy(template.at[:, :, bins, :], out, sems.at[i]))
+        at += out.shape[2]
+    for copy in copies:
+        copy.start()
+    for copy in copies:
+        copy.wait()
+
+
+def cut(template, count):
+    shape = template.shape[:2] + (template.shape[2] // (2 * count),) + template.shape[3:]
+    return pl.pallas_call(
+        cut_kernel,
+        in_specs=[IN_HBM],
+        out_specs=[IN_VMEM] * count,
+        out_shape=[pltpu.VMEM(shape, template.dtype)] * count,
+        scratch_shapes=[pltpu.SemaphoreType.DMA((count,))],
+        compiler_params=PARAMS,
+    )(*in_hbm([template]))
+
+
+def join_kernel(count, *refs):
+    *pieces, out = refs
+    width = pieces[0].shape[2]
+    for i in range(count):
+        out[:, :, i * width : (i + 1) * width, :] = pieces[i][...]
+    if len(pieces) > count:
+
+        @pl.when((lax.axis_index("blk") + 1) & 2 != 0)
+        def _():
+            out[...] = pieces[count][...]
+
+
+def join(pieces, *middle):
+    one = pieces[0]
+    shape = one.shape[:2] + (len(pieces) * one.shape[2],) + one.shape[3:]
+    operands = in_vmem([*pieces, *middle])
+    return pl.pallas_call(
+        functools.partial(join_kernel, len(pieces)),
+        in_specs=[IN_VMEM] * len(operands),
+        out_specs=IN_VMEM,
+        out_shape=pltpu.VMEM(shape, one.dtype),
+        compiler_params=PARAMS,
+    )(*operands)
+
+
 def partners(n, d):
     return [(i, i ^ d) for i in range(n)]
 
 
 def after(value, *others):
     return lax.optimization_barrier((value,) + others)[0]
+
+
+def swap(piece):
+    return lax.ppermute(piece, "parts", partners(2, 1))
+
+
+def any_line(held, spectra, templates, mine, exchange, transform_of, finish_of):
+    n_blk, runs = lax.axis_size("blk"), held[0].shape[2] // SUB
+    own, other = (0, runs // 2), (runs // 2, -(runs // 2))
+    far = range(2, n_blk)
+    whole = {0: [(spectra, (0, 0))]}
+    last = spectra
+    for d in far:
+        arrived = lax.ppermute(after(mine, last), "blk", partners(n_blk, d))
+        swapped = swap(arrived)
+        last = add_piece(held, d, own, arrived)
+        whole[d] = [(last, own), (add_piece(held, d, other, swapped), other)]
+    near = lax.ppermute(templates, "blk", partners(n_blk, 1))
+    order = list(whole)
+    first = exchange(transform_of([whole[d] for d in order]))
+    return (order, [1]), first + exchange(finish_of(1, (0, 0), near, [[]]))
+
+
+def line_of_four(held, spectra, mine, theirs, arrived, near, exchange, transform_of, finish_of):
+    runs = held[0].shape[2] // SUB
+    own, other = (0, runs // 2), (runs // 2, -(runs // 2))
+    arrived = [after(a, spectra) for a in arrived]
+    middle = lax.ppermute(after(mine, spectra), "blk", [(0, 0), (1, 2), (2, 1), (3, 3)])
+    ends = [lax.ppermute(a, "blk", partners(4, 1)) for a in arrived]
+    arrived = join(arrived)
+    swapped = swap(arrived)
+    second = add_piece(held, 2, own, arrived)
+    near_first = add_piece(held, 1, own, after(near, second))
+    near = lax.ppermute(after(theirs, near_first), "blk", partners(4, 1))
+    third = join(ends, middle)
+    third_swapped = swap(third)
+    third_first = add_piece(held, 3, own, third)
+    second_rest = add_piece(held, 2, other, swapped)
+    first = exchange(transform_of([[(spectra, (0, 0))], [(second, own), (second_rest, other)]]))
+    near_rest = add_piece(held, 1, other, near)
+    whole = [[(near_first, own), (near_rest, other)], [(third_first, own)]]
+    return ([0, 2], [1, 3]), first + exchange(finish_of(3, other, third_swapped, whole))
 
 
 def shards(records, templates, masks, offsets):
     n_blk, n_chan, n_freq = (lax.axis_size(a) for a in ("blk", "chan", "freq"))
     windows, _, bin_count, _ = records.shape
-    runs = bin_count // SUB
     blocks = n_chan * n_freq
     high, low = (jnp.asarray(t) for t in lag_tables())
 
     def exchange(found):
         return [found[0]] + [lax.ppermute(found[n], ("chan", "freq"), partners(blocks, n)) for n in range(1, blocks)]
 
-    half = bin_count // 2
-    mine = lax.dynamic_slice_in_dim(templates, lax.axis_index("parts") * half, half, 2)
-    swap = lambda a: lax.ppermute(a, "parts", partners(2, 1))
-    far = sorted(range(2, n_blk), key=lambda d: -(d & -d))
-    final = far[-1]
-    arrived = {far[0]: lax.ppermute(mine, "blk", partners(n_blk, far[0]))}
-    near = lax.ppermute(templates, "blk", partners(n_blk, 1))
-    held, spectra = own_template(masks, offsets, records, templates, high, low)
-    for d in far[1:]:
-        arrived[d] = lax.ppermute(after(mine, spectra), "blk", partners(n_blk, d))
-    own, other = (0, runs // 2), (runs // 2, -(runs // 2))
-    whole = {0: [(spectra, (0, 0))]}
-    last = spectra
-    for d in far[:-1]:
-        swapped = swap(after(arrived[d], last))
-        last = add_piece(held, d, own, arrived[d])
-        whole[d] = [(last, own), (add_piece(held, d, other, after(swapped, last)), other)]
-        last = whole[d][1][0]
-    near = after(near, last)
-    near_spectra = add_piece(held, 1, (0, 0), near)
-    swapped = swap(after(arrived[final], near_spectra))
-    late = add_piece(held, final, own, after(arrived[final], near_spectra))
-    ready = list(whole)
-    first = exchange(transform(held, [whole[d] for d in ready] + [[(after(near_spectra, late), (0, 0))]], blocks))
-    second = exchange(finish(held, final, other, swapped, [[(late, own)]], blocks))
+    pieces = cut(templates, PIECES)
+    if n_blk == 4:
+        arrived = [lax.ppermute(piece, "blk", partners(n_blk, 2)) for piece in pieces]
+        mine = join(pieces)
+        near = lax.ppermute(mine, "blk", partners(n_blk, 1))
+    held, spectra, theirs = own_template(masks, offsets, records, templates, high, low)
+    after_all = (exchange, lambda whole: transform(held, whole, blocks), lambda *w: finish(held, *w, blocks))
+    if n_blk == 4:
+        orders, parts = line_of_four(held, spectra, mine, theirs, arrived, near, *after_all)
+    else:
+        orders, parts = any_line(held, spectra, templates, join(pieces), *after_all)
     return pl.pallas_call(
-        functools.partial(sum_kernel, (ready + [1], [final])),
-        in_specs=[IN_VMEM] * (2 * blocks),
+        functools.partial(sum_kernel, orders),
+        in_specs=[IN_VMEM] * len(parts),
         out_specs=IN_VMEM,
         out_shape=jax.ShapeDtypeStruct((n_blk, windows, NSAMP // blocks), jnp.float32),
         compiler_params=PARAMS,
-    )(*first, *second)
+    )(*parts)
 
 
 def solution(mesh):

time: 44.8 us -> 41.4 us (0.924)
  waiting for transfers between devices: 12.4 us -> 6.82 us
  starting transfers between devices: 16.4 us -> 18.2 us
  Pallas kernels: 14.7 us -> 16.1 us
  local copies, waits for them, and re-layouts: 0.97 us -> 0 us
    ppermute x5 -> x9, waiting for transfers between devices: 9.19 us -> 3.3 us  [the longest x2 3.28 us: shards(): lax.ppermute(piece, 'blk', partners(n_blk, 2))]
    ppermute x5 -> x9, starting transfers between devices: 12.3 us -> 14.4 us  [the longest x2 4.44 us: shards(): lax.ppermute(piece, 'blk', partners(n_blk, 2))]
    pallas_call x1 -> x5, Pallas kernels: 0.65 us -> 1.69 us  [the longest x1 0.98 us: cut(): pl.pallas_call(cut_kernel, in_specs=[IN_HBM], out_specs=[IN_VMEM] * count...]
    dynamic_slice x1 -> x0, local copies, waits for them, and re-layouts: 0.97 us -> none  [shards(): lax.dynamic_slice_in_dim(templates, lax.axis_index('parts') * half, half, 2)]
    pallas_call x4 -> x5, Pallas kernels: 6.69 us -> 7.01 us  [add_piece(): pl.pallas_call(functools.partial(piece_kernel, (d, moved, None)), in_spec...]
  transfers between devices with their start and end apart: 11 -> 15, of which waited for: 6 -> 3; matrix products, arithmetic and copies ran while one was open for 0% -> 0% of each run, Pallas kernels for 32% -> 35%
where the time goes in v3:
time: 41.4 us; the launch traced here: 41.2 us
  starting transfers between devices  18.2 us (44%)
  Pallas kernels  16.1 us (39%)
  waiting for transfers between devices  6.82 us (16%)
    pallas_call x5, Pallas kernels, add_piece(): pl.pallas_call(functools.partial(piece_kernel, (d, moved, None)), in_spec...  7.01 us
    pallas_call x1, Pallas kernels, own_template(): pl.pallas_call(own_kernel, in_specs=[IN_HBM] * 6, out_specs=[IN_VMEM] * l...  5.22 us
    ppermute x2, starting transfers between devices, shards(): lax.ppermute(piece, 'blk', partners(n_blk, 2))  4.44 us
    ppermute x6, starting transfers between devices, exchange(): lax.ppermute(found[n], ('chan', 'freq'), partners(blocks, n))  3.84 us
    ppermute x6, waiting for transfers between devices, exchange(): lax.ppermute(found[n], ('chan', 'freq'), partners(blocks, n))  3.52 us
    ppermute x2, waiting for transfers between devices, shards(): lax.ppermute(piece, 'blk', partners(n_blk, 2))  3.28 us
    ppermute x2, starting transfers between devices, swap(): return lax.ppermute(piece, 'parts', partners(2, 1))  3.13 us
    ppermute x2, starting transfers between devices, line_of_four(): ends = [lax.ppermute(a, 'blk', partners(4, 1)) for a in arrived]  2.53 us
  transfers between devices with their start and end apart: 15, of which 3 were waited for; matrix products, arithmetic and copies ran while one was open for 0% of the time, Pallas kernels for 35%

profile of v3, /device:TPU:0, one launch (start us, length us, event | category | flops | bytes accessed | tf_op | source)
XLA Modules:
  0.0 41.2 jit_solution(7944409664657521569)
XLA Ops:
  0.0 1.0 %shard_map.65 = (bf16[1,2,64,512]{3,2,1,0:T(8,128)(2,1)S(1)}, bf16[1,2,64,512]{3,2,1,0:T(8,128)(2,1)S(1)}) custom-call(bf16[1,2,256,512]{3,2,1,0:T(8,128)(2,1)} %template.1), custom_call_target="tpu_custom_call" | custom-call | tf_op jit(solution)/shard_map/pallas_call | solution.py:290
  1.0 4.1 %collective-permute-start = (bf16[1,2,64,512]{3,2,1,0:T(8,128)(2,1)S(1)}, bf16[1,2,64,512]{3,2,1,0:T(8,128)(2,1)S(1)}, u32[]{:S(2)}, u32[]{:S(2)}) collective-permute-start(bf16[1,2,64,512]{3,2,1,0:T(8,128)(2,1)S(1)} %get-tuple-element.33.refs_0_), channel_id=1, source_target_pairs={{0,8},{4,12},{8,0},{12,4},{1,9},{5,13},{9,1},{13,5},{2,10},{6,14},... | collective-permute-start | bytes 393224 | tf_op jit(solution)/shard_map/ppermute | solution.py:386
  5.1 1.6 %collective-permute-start.10 = (bf16[1,2,128,512]{3,2,1,0:T(8,128)(2,1)S(1)}, bf16[1,2,128,512]{3,2,1,0:T(8,128)(2,1)S(1)}, u32[]{:S(2)}, u32[]{:S(2)}) collective-permute-start(bf16[1,2,128,512]{3,2,1,0:T(8,128)(2,1)S(1)} %shard_map.70), channel_id=1, source_target_pairs={{0,4},{4,0},{8,12},{12,8},{1,5},{5,1},{9,13},{13,9},{2,6},{6,2},{1... | collective-permute-start | bytes 786440 | tf_op jit(solution)/shard_map/ppermute | solution.py:388
  6.8 0.3 collective-permute-start.1
  7.1 5.2 %shard_map.64 = (bf16[16,2,256,512]{3,2,1,0:T(8,128)(2,1)S(1)}, f32[4,2,4,128]{3,2,1,0:T(4,128)S(1)}, f32[4,1,512]{2,1,0:T(1,128)S(1)}, bf16[4,128,256]{2,1,0:T(...) custom-call(s32[4,4]{1,0:T(4,128)} %masks.1, ...), custom_call_target="tpu_custom_call" | custom-call | tf_op jit(solution)/shard_map/pallas_call | solution.py:226
  12.3 0.7 %collective-permute-start.8 = (bf16[1,2,128,512]{3,2,1,0:T(8,128)(2,1)S(1)}, bf16[1,2,128,512]{3,2,1,0:T(8,128)(2,1)S(1)}, u32[]{:S(2)}, u32[]{:S(2)}) collective-permute-start(bf16[1,2,128,512]{3,2,1,0:T(8,128)(2,1)S(1)} %shard_map.70), channel_id=1, source_target_pairs={{0,0},{4,8},{8,4},{12,12},{1,1},{5,9},{9,5},{13,13},{2,2},{6,10},{... | collective-permute-start | bytes 786440 | tf_op jit(solution)/shard_map/ppermute | solution.py:358
  13.0 0.0 collective-permute-done.refs_0_
  13.0 3.3 %collective-permute-done.1.refs_1_ = bf16[1,2,64,512]{3,2,1,0:T(8,128)(2,1)S(1)} collective-permute-done((bf16[1,2,64,512]{3,2,1,0:T(8,128)(2,1)S(1)}, bf16[1,2,64,512]{3,2,1,0:T(8,128)(2,1)S(1)}, u32[]{:S(2)}, u32[]{:S(2)}) %collective-permute-start.1) | collective-permute-done | bytes 131104 | tf_op jit(solution)/shard_map/ppermute | solution.py:386
  16.3 2.5 %collective-permute-start.6 = (bf16[1,2,64,512]{3,2,1,0:T(8,128)(2,1)S(1)}, bf16[1,2,64,512]{3,2,1,0:T(8,128)(2,1)S(1)}, u32[]{:S(2)}, u32[]{:S(2)}) collective-permute-start(bf16[1,2,64,512]{3,2,1,0:T(8,128)(2,1)S(1)} %collective-permute-done.refs_0_), channel_id=1, source_target_pairs={{0,4},{4,0},{8,12},{12,8},{1,5},{5,1},{9,13},{13,9},{2,6},{6,2},{1... | collective-permute-start | bytes 393224 | tf_op jit(solution)/shard_map/ppermute | solution.py:359
  18.8 0.0 collective-permute-start.7
  18.8 1.6 %collective-permute-start.2 = (bf16[1,2,128,512]{3,2,1,0:T(8,128)(2,1)S(1)}, bf16[1,2,128,512]{3,2,1,0:T(8,128)(2,1)S(1)}, u32[]{:S(2)}, u32[]{:S(2)}) collective-permute-start(bf16[1,2,128,512]{3,2,1,0:T(8,128)(2,1)S(1)} %shard_map.66.rest_0_), channel_id=1, source_target_pairs={{0,16},{16,0},{1,17},{17,1},{2,18},{18,2},{3,19},{19,3},{4,20},{20... | collective-permute-start | bytes 786440 | tf_op jit(solution)/shard_map/ppermute | solution.py:334
  20.4 1.4 %shard_map.67.rest_1_ = f32[2,16,128]{2,1,0:T(8,128)S(1)} custom-call(bf16[16,2,256,512]{3,2,1,0:T(8,128)(2,1)S(1)} %get-tuple-element.27.held, f32[4,2,4,128]{3,2,1,0:T(4,128)S(1)} %get-tuple-element.28.turn, f32[4,1,512]{2,1,0:T(1,128)S(1)} %get-tuple-element.29.used, bf16[4,128,256]{2,1,0:T(8,128)(2,1)S(1)} %get-tuple-element.30.high, ...), custom_call_target="tpu_custom_call" | custom-call | tf_op jit(solution)/shard_map/pallas_call | solution.py:243
  21.8 0.0 collective-permute-done.10.rest_0_
  21.8 1.4 %shard_map.72.rest_1_ = f32[2,16,128]{2,1,0:T(8,128)S(1)} custom-call(bf16[16,2,256,512]{3,2,1,0:T(8,128)(2,1)S(1)} %get-tuple-element.27.held, f32[4,2,4,128]{3,2,1,0:T(4,128)S(1)} %get-tuple-element.28.turn, f32[4,1,512]{2,1,0:T(1,128)S(1)} %get-tuple-element.29.used, bf16[4,128,256]{2,1,0:T(8,128)(2,1)S(1)} %get-tuple-element.30.high, ...), custom_call_target="tpu_custom_call" | custom-call | tf_op jit(solution)/shard_map/pallas_call | solution.py:243
  23.2 2.0 %collective-permute-start.11 = (bf16[1,2,128,512]{3,2,1,0:T(8,128)(2,1)S(1)}, bf16[1,2,128,512]{3,2,1,0:T(8,128)(2,1)S(1)}, u32[]{:S(2)}, u32[]{:S(2)}) collective-permute-start(bf16[1,2,128,512]{3,2,1,0:T(8,128)(2,1)S(1)} %get-tuple-element.44), channel_id=1, source_target_pairs={{0,4},{4,0},{8,12},{12,8},{1,5},{5,1},{9,13},{13,9},{2,6},{6,2},{1... | collective-permute-start | bytes 786440 | tf_op jit(solution)/shard_map/ppermute | solution.py:364
  25.2 0.0 collective-permute-done.6.refs_0_
  25.2 0.0 collective-permute-done.7.refs_1_
  25.2 0.0 collective-permute-done.8.refs_2_
  25.3 1.5 %collective-permute-start.9 = (bf16[1,2,128,512]{3,2,1,0:T(8,128)(2,1)S(1)}, bf16[1,2,128,512]{3,2,1,0:T(8,128)(2,1)S(1)}, u32[]{:S(2)}, u32[]{:S(2)}) collective-permute-start(bf16[1,2,128,512]{3,2,1,0:T(8,128)(2,1)S(1)} %shard_map.71.rest_0_), channel_id=1, source_target_pairs={{0,16},{16,0},{1,17},{17,1},{2,18},{18,2},{3,19},{19,3},{4,20},{20... | collective-permute-start | bytes 786440 | tf_op jit(solution)/shard_map/ppermute | solution.py:334
  26.8 0.0 collective-permute-done.2.rest_0_
  26.8 1.4 %shard_map.68.rest_2_ = f32[2,16,128]{2,1,0:T(8,128)S(1)} custom-call(bf16[16,2,256,512]{3,2,1,0:T(8,128)(2,1)S(1)} %get-tuple-element.27.held, f32[4,2,4,128]{3,2,1,0:T(4,128)S(1)} %get-tuple-element.28.turn, f32[4,1,512]{2,1,0:T(1,128)S(1)} %get-tuple-element.29.used, bf16[4,128,256]{2,1,0:T(8,128)(2,1)S(1)} %get-tuple-element.30.high, ...), custom_call_target="tpu_custom_call" | custom-call | tf_op jit(solution)/shard_map/pallas_call | solution.py:243
  28.2 0.4 shard_map.69
  28.6 0.1 collective-permute-start.3
  28.7 1.4 %shard_map.74.rest_3_ = f32[2,16,128]{2,1,0:T(8,128)S(1)} custom-call(bf16[16,2,256,512]{3,2,1,0:T(8,128)(2,1)S(1)} %get-tuple-element.27.held, f32[4,2,4,128]{3,2,1,0:T(4,128)S(1)} %get-tuple-element.28.turn, f32[4,1,512]{2,1,0:T(1,128)S(1)} %get-tuple-element.29.used, bf16[4,128,256]{2,1,0:T(8,128)(2,1)S(1)} %get-tuple-element.30.high, ...), custom_call_target="tpu_custom_call" | custom-call | tf_op jit(solution)/shard_map/pallas_call | solution.py:243
  30.1 1.5 %collective-permute-start.4 = (f32[2,16,256]{2,1,0:T(8,128)S(1)}, f32[2,16,256]{2,1,0:T(8,128)S(1)}, u32[]{:S(2)}, u32[]{:S(2)}) collective-permute-start(f32[2,16,256]{2,1,0:T(8,128)S(1)} %get-tuple-element.39), channel_id=1, source_target_pairs={{0,2},{1,3},{2,0},{3,1},{4,6},{5,7},{6,4},{7,5},{8,10},{9,11},{10,... | collective-permute-start | bytes 98312 | tf_op jit(solution)/shard_map/ppermute | solution.py:382
  31.6 0.3 collective-permute-start.5
  31.9 0.0 collective-permute-done.11.rest_0_
  31.9 1.4 %shard_map.73.rest_2_ = f32[2,16,128]{2,1,0:T(8,128)S(1)} custom-call(bf16[16,2,256,512]{3,2,1,0:T(8,128)(2,1)S(1)} %get-tuple-element.27.held, f32[4,2,4,128]{3,2,1,0:T(4,128)S(1)} %get-tuple-element.28.turn, f32[4,1,512]{2,1,0:T(1,128)S(1)} %get-tuple-element.29.used, bf16[4,128,256]{2,1,0:T(8,128)(2,1)S(1)} %get-tuple-element.30.high, ...), custom_call_target="tpu_custom_call" | custom-call | tf_op jit(solution)/shard_map/pallas_call | solution.py:243
  33.3 0.0 collective-permute-done.9.rest_0_
  33.3 1.8 %shard_map.75 = (f32[2,16,256]{2,1,0:T(8,128)S(1)}, f32[2,16,256]{2,1,0:T(8,128)S(1)}, f32[2,16,256]{2,1,0:T(8,128)S(1)}, f32[2,16,256]{2,1,0:T(8,128)S(1)}) custom-call(bf16[16,2,256,512]{3,2,1,0:T(8,128)(2,1)S(1)} %get-tuple-element.27.held, f32[4,2,4,128]{3,2,1,0:T(4,128)S(1)} %get-tuple-element.28.turn, f32[4,1,512]{2,1,0:T(1,128)S(1)} %get-tuple-element.29.used, ...), custom_call_target="tpu_custom_call" | custom-call | tf_op jit(solution)/shard_map/pallas_call | solution.py:261
  35.1 0.4 collective-permute-start.12
  35.5 1.5 %collective-permute-start.13 = (f32[2,16,256]{2,1,0:T(8,128)S(1)}, f32[2,16,256]{2,1,0:T(8,128)S(1)}, u32[]{:S(2)}, u32[]{:S(2)}) collective-permute-start(f32[2,16,256]{2,1,0:T(8,128)S(1)} %get-tuple-element.47), channel_id=1, source_target_pairs={{0,2},{1,3},{2,0},{3,1},{4,6},{5,7},{6,4},{7,5},{8,10},{9,11},{10,... | collective-permute-start | bytes 98312 | tf_op jit(solution)/shard_map/ppermute | solution.py:382
  37.0 0.0 collective-permute-done.3.refs_1_
  37.0 0.1 collective-permute-start.14
  37.0 0.0 collective-permute-done.4.refs_2_
  37.0 0.0 collective-permute-done.5.refs_3_
  37.0 0.0 collective-permute-done.12.refs_5_
  37.1 2.3 %collective-permute-done.13.refs_6_ = f32[2,16,256]{2,1,0:T(8,128)S(1)} collective-permute-done((f32[2,16,256]{2,1,0:T(8,128)S(1)}, f32[2,16,256]{2,1,0:T(8,128)S(1)}, u32[]{:S(2)}, u32[]{:S(2)}) %collective-permute-start.13) | collective-permute-done | bytes 32800 | tf_op jit(solution)/shard_map/ppermute | solution.py:382
  39.4 1.2 %collective-permute-done.14.refs_7_ = f32[2,16,256]{2,1,0:T(8,128)S(1)} collective-permute-done((f32[2,16,256]{2,1,0:T(8,128)S(1)}, f32[2,16,256]{2,1,0:T(8,128)S(1)}, u32[]{:S(2)}, u32[]{:S(2)}) %collective-permute-start.14) | collective-permute-done | bytes 32800 | tf_op jit(solution)/shard_map/ppermute | solution.py:382
  40.6 0.6 %shard_map.76 = f32[4,16,256]{2,1,0:T(8,128)} custom-call(f32[2,16,256]{2,1,0:T(8,128)S(1)} %get-tuple-element.37.refs_0_, f32[2,16,256]{2,1,0:T(8,128)S(1)} %collective-permute-done.3.refs_1_, f32[2,16,256]{2,1,0:T(8,128)S(1)} %collective-permute-done.4.refs_2_, f32[2,16,256]{2,1,0:T(8,128)S(1)} %collective-permute-done.5.refs_3_, ...), custom_call_target="tpu_custom_call" | custom-call | tf_op jit(solution)/shard_map/pallas_call | solution.py:395
  (3 shorter events, 0.1 us)
Async XLA Ops:
  1.0 12.0 %collective-permute-start = (bf16[1,2,64,512]{3,2,1,0:T(8,128)(2,1)S(1)}, bf16[1,2,64,512]{3,2,1,0:T(8,128)(2,1)S(1)}, u32[]{:S(2)}, u32[]{:S(2)}) collective-permute-start(bf16[1,2,64,512]{3,2,1,0:T(8,128)(2,1)S(1)} %get-tuple-element.33.refs_0_), channel_id=1, source_target_pairs={{0,8},{4,12},{8,0},{12,4},{1,9},{5,13},{9,1},{13,5},{2,10},{6,14},... | collective-permute-start | bytes 393224 | tf_op jit(solution)/shard_map/ppermute | solution.py:386
  5.1 16.7 %collective-permute-start.10 = (bf16[1,2,128,512]{3,2,1,0:T(8,128)(2,1)S(1)}, bf16[1,2,128,512]{3,2,1,0:T(8,128)(2,1)S(1)}, u32[]{:S(2)}, u32[]{:S(2)}) collective-permute-start(bf16[1,2,128,512]{3,2,1,0:T(8,128)(2,1)S(1)} %shard_map.70), channel_id=1, source_target_pairs={{0,4},{4,0},{8,12},{12,8},{1,5},{5,1},{9,13},{13,9},{2,6},{6,2},{1... | collective-permute-start | bytes 786440 | tf_op jit(solution)/shard_map/ppermute | solution.py:388
  6.8 9.5 %collective-permute-start.1 = (bf16[1,2,64,512]{3,2,1,0:T(8,128)(2,1)S(1)}, bf16[1,2,64,512]{3,2,1,0:T(8,128)(2,1)S(1)}, u32[]{:S(2)}, u32[]{:S(2)}) collective-permute-start(bf16[1,2,64,512]{3,2,1,0:T(8,128)(2,1)S(1)} %get-tuple-element.35.refs_1_), channel_id=1, source_target_pairs={{0,8},{4,12},{8,0},{12,4},{1,9},{5,13},{9,1},{13,5},{2,10},{6,14},... | collective-permute-start | bytes 393224 | tf_op jit(solution)/shard_map/ppermute | solution.py:386
  12.3 12.9 %collective-permute-start.8 = (bf16[1,2,128,512]{3,2,1,0:T(8,128)(2,1)S(1)}, bf16[1,2,128,512]{3,2,1,0:T(8,128)(2,1)S(1)}, u32[]{:S(2)}, u32[]{:S(2)}) collective-permute-start(bf16[1,2,128,512]{3,2,1,0:T(8,128)(2,1)S(1)} %shard_map.70), channel_id=1, source_target_pairs={{0,0},{4,8},{8,4},{12,12},{1,1},{5,9},{9,5},{13,13},{2,2},{6,10},{... | collective-permute-start | bytes 786440 | tf_op jit(solution)/shard_map/ppermute | solution.py:358
  16.3 8.9 %collective-permute-start.6 = (bf16[1,2,64,512]{3,2,1,0:T(8,128)(2,1)S(1)}, bf16[1,2,64,512]{3,2,1,0:T(8,128)(2,1)S(1)}, u32[]{:S(2)}, u32[]{:S(2)}) collective-permute-start(bf16[1,2,64,512]{3,2,1,0:T(8,128)(2,1)S(1)} %collective-permute-done.refs_0_), channel_id=1, source_target_pairs={{0,4},{4,0},{8,12},{12,8},{1,5},{5,1},{9,13},{13,9},{2,6},{6,2},{1... | collective-permute-start | bytes 393224 | tf_op jit(solution)/shard_map/ppermute | solution.py:359
  18.8 6.4 %collective-permute-start.7 = (bf16[1,2,64,512]{3,2,1,0:T(8,128)(2,1)S(1)}, bf16[1,2,64,512]{3,2,1,0:T(8,128)(2,1)S(1)}, u32[]{:S(2)}, u32[]{:S(2)}) collective-permute-start(bf16[1,2,64,512]{3,2,1,0:T(8,128)(2,1)S(1)} %collective-permute-done.1.refs_1_), channel_id=1, source_target_pairs={{0,4},{4,0},{8,12},{12,8},{1,5},{5,1},{9,13},{13,9},{2,6},{6,2},{1... | collective-permute-start | bytes 393224 | tf_op jit(solution)/shard_map/ppermute | solution.py:359
  18.8 8.0 %collective-permute-start.2 = (bf16[1,2,128,512]{3,2,1,0:T(8,128)(2,1)S(1)}, bf16[1,2,128,512]{3,2,1,0:T(8,128)(2,1)S(1)}, u32[]{:S(2)}, u32[]{:S(2)}) collective-permute-start(bf16[1,2,128,512]{3,2,1,0:T(8,128)(2,1)S(1)} %shard_map.66.rest_0_), channel_id=1, source_target_pairs={{0,16},{16,0},{1,17},{17,1},{2,18},{18,2},{3,19},{19,3},{4,20},{20... | collective-permute-start | bytes 786440 | tf_op jit(solution)/shard_map/ppermute | solution.py:334
  23.2 8.7 %collective-permute-start.11 = (bf16[1,2,128,512]{3,2,1,0:T(8,128)(2,1)S(1)}, bf16[1,2,128,512]{3,2,1,0:T(8,128)(2,1)S(1)}, u32[]{:S(2)}, u32[]{:S(2)}) collective-permute-start(bf16[1,2,128,512]{3,2,1,0:T(8,128)(2,1)S(1)} %get-tuple-element.44), channel_id=1, source_target_pairs={{0,4},{4,0},{8,12},{12,8},{1,5},{5,1},{9,13},{13,9},{2,6},{6,2},{1... | collective-permute-start | bytes 786440 | tf_op jit(solution)/shard_map/ppermute | solution.py:364
  25.3 8.1 %collective-permute-start.9 = (bf16[1,2,128,512]{3,2,1,0:T(8,128)(2,1)S(1)}, bf16[1,2,128,512]{3,2,1,0:T(8,128)(2,1)S(1)}, u32[]{:S(2)}, u32[]{:S(2)}) collective-permute-start(bf16[1,2,128,512]{3,2,1,0:T(8,128)(2,1)S(1)} %shard_map.71.rest_0_), channel_id=1, source_target_pairs={{0,16},{16,0},{1,17},{17,1},{2,18},{18,2},{3,19},{19,3},{4,20},{20... | collective-permute-start | bytes 786440 | tf_op jit(solution)/shard_map/ppermute | solution.py:334
  28.6 8.4 %collective-permute-start.3 = (f32[2,16,256]{2,1,0:T(8,128)S(1)}, f32[2,16,256]{2,1,0:T(8,128)S(1)}, u32[]{:S(2)}, u32[]{:S(2)}) collective-permute-start(f32[2,16,256]{2,1,0:T(8,128)S(1)} %get-tuple-element.38), channel_id=1, source_target_pairs={{0,1},{1,0},{2,3},{3,2},{4,5},{5,4},{6,7},{7,6},{8,9},{9,8},{10,11... | collective-permute-start | bytes 98312 | tf_op jit(solution)/shard_map/ppermute | solution.py:382
  30.1 7.0 %collective-permute-start.4 = (f32[2,16,256]{2,1,0:T(8,128)S(1)}, f32[2,16,256]{2,1,0:T(8,128)S(1)}, u32[]{:S(2)}, u32[]{:S(2)}) collective-permute-start(f32[2,16,256]{2,1,0:T(8,128)S(1)} %get-tuple-element.39), channel_id=1, source_target_pairs={{0,2},{1,3},{2,0},{3,1},{4,6},{5,7},{6,4},{7,5},{8,10},{9,11},{10,... | collective-permute-start | bytes 98312 | tf_op jit(solution)/shard_map/ppermute | solution.py:382
  31.6 5.5 %collective-permute-start.5 = (f32[2,16,256]{2,1,0:T(8,128)S(1)}, f32[2,16,256]{2,1,0:T(8,128)S(1)}, u32[]{:S(2)}, u32[]{:S(2)}) collective-permute-start(f32[2,16,256]{2,1,0:T(8,128)S(1)} %get-tuple-element.40), channel_id=1, source_target_pairs={{0,3},{1,2},{2,1},{3,0},{4,7},{5,6},{6,5},{7,4},{8,11},{9,10},{10,... | collective-permute-start | bytes 98312 | tf_op jit(solution)/shard_map/ppermute | solution.py:382
  35.1 1.9 %collective-permute-start.12 = (f32[2,16,256]{2,1,0:T(8,128)S(1)}, f32[2,16,256]{2,1,0:T(8,128)S(1)}, u32[]{:S(2)}, u32[]{:S(2)}) collective-permute-start(f32[2,16,256]{2,1,0:T(8,128)S(1)} %get-tuple-element.46), channel_id=1, source_target_pairs={{0,1},{1,0},{2,3},{3,2},{4,5},{5,4},{6,7},{7,6},{8,9},{9,8},{10,11... | collective-permute-start | bytes 98312 | tf_op jit(solution)/shard_map/ppermute | solution.py:382
  35.5 3.9 %collective-permute-start.13 = (f32[2,16,256]{2,1,0:T(8,128)S(1)}, f32[2,16,256]{2,1,0:T(8,128)S(1)}, u32[]{:S(2)}, u32[]{:S(2)}) collective-permute-start(f32[2,16,256]{2,1,0:T(8,128)S(1)} %get-tuple-element.47), channel_id=1, source_target_pairs={{0,2},{1,3},{2,0},{3,1},{4,6},{5,7},{6,4},{7,5},{8,10},{9,11},{10,... | collective-permute-start | bytes 98312 | tf_op jit(solution)/shard_map/ppermute | solution.py:382
  37.0 3.6 %collective-permute-start.14 = (f32[2,16,256]{2,1,0:T(8,128)S(1)}, f32[2,16,256]{2,1,0:T(8,128)S(1)}, u32[]{:S(2)}, u32[]{:S(2)}) collective-permute-start(f32[2,16,256]{2,1,0:T(8,128)S(1)} %get-tuple-element.48), channel_id=1, source_target_pairs={{0,3},{1,2},{2,1},{3,0},{4,7},{5,6},{6,5},{7,4},{8,11},{9,10},{10,... | collective-permute-start | bytes 98312 | tf_op jit(solution)/shard_map/ppermute | solution.py:382

commit v4 on v3

v4 whole, which is shorter than its diff:
```python
import functools
import math

import jax
import jax.numpy as jnp
import numpy as np
from jax import lax
from jax.experimental import pallas as pl
from jax.experimental.pallas import tpu as pltpu
from jax.sharding import PartitionSpec as P

NSAMP = 1024
BINS = 512
GROUP = 16
HALF = 128
RUN = 64
FOLD = 256
PIECES = 1
BATCH = 4
VMEM_LIMIT = 24 * 2**20


def lag_tables():
    bins = np.arange(BINS).reshape(-1, HALF)
    angle = 2.0 * math.pi / NSAMP * (bins[..., None] * np.arange(FOLD) % NSAMP)
    table = math.sqrt(2.0 / BINS) * np.concatenate([np.cos(angle), -np.sin(angle)], axis=1)
    table = table.astype(np.float32)
    high = table.astype(jnp.bfloat16)
    low = (table - high.astype(np.float32)).astype(jnp.bfloat16)
    return high, low


def two_halves(values):
    high = values.astype(jnp.bfloat16)
    return high, (values - high.astype(jnp.float32)).astype(jnp.bfloat16)


def product(left, right, contract):
    return lax.dot_general(left, right, ((contract[:1], contract[1:]), ((), ())), preferred_element_type=jnp.float32)


def mask_row(masks, template_at, width):
    here = masks.shape[1] // lax.axis_size("chan")
    first = lax.axis_index("chan") * here
    lane = lax.broadcasted_iota(jnp.int32, (1, width), 1) // (width // here)
    row = jnp.zeros((1, width), jnp.float32)
    for b in range(here):
        row = jnp.where(lane == b, masks[template_at, first + b].astype(jnp.float32), row)
    return row


def block_transpose(values):
    row = lax.broadcasted_iota(jnp.int32, values.shape, 0)
    place = lax.broadcasted_iota(jnp.int32, values.shape, 1) // GROUP
    for bit in (1, 2, 4):
        up = pltpu.roll(pltpu.roll(values, 8 - bit, 0), bit * GROUP, 1)
        down = pltpu.roll(pltpu.roll(values, bit, 0), 8 * GROUP - bit * GROUP, 1)
        moved = jnp.where(row & bit == 0, up, down)
        values = jnp.where(row & bit == place & bit, values, moved)
    return values


def group_rows(records, half, g):
    bins = pl.ds(pl.multiple_of(half * HALF + g * GROUP, GROUP), GROUP)
    return jnp.concatenate(
        [jnp.concatenate([records[w, 0, bins, :], records[w, 1, bins, :]], axis=1) for w in range(records.shape[0])],
        axis=0,
    )


def flip_kernel(records, out):
    for g in range(HALF // GROUP):
        out[g] = group_rows(records, 1 - lax.axis_index("parts"), g).T


def half_spectra(entries, half, records, turn, used, ready=None, flipped=None):
    windows = records.shape[0]
    masks = [used[template_at].astype(jnp.bfloat16) for template_at, _ in entries]
    row = lax.broadcasted_iota(jnp.int32, (2 * GROUP * len(entries), windows * GROUP), 0)
    lane = lax.broadcasted_iota(jnp.int32, (2 * GROUP * len(entries), windows * GROUP), 1)
    same_bin = row % GROUP == lane % GROUP
    sums = [[] for _ in range(2 * len(entries))]
    for g in range(HALF // GROUP):
        if ready is not None:
            ready(g)
        weights = []
        for (_, pieces), mask in zip(entries, masks):
            piece = pieces[g * GROUP // pieces[0].shape[2]]
            start = g * GROUP % piece.shape[2]
            first, second = (piece[0, part, start : start + GROUP, :] * mask for part in range(2))
            weights.append(jnp.concatenate([first, second], axis=1))
            weights.append(jnp.concatenate([-second, first], axis=1))
        weights = jnp.concatenate(weights, axis=0)
        if flipped is None:
            every = product(weights, group_rows(records, half, g), (1, 1))
        else:
            every = product(weights, flipped[g], (1, 0))
        every = jnp.where(same_bin, every, 0.0)
        for i, found in enumerate(sums):
            found.append(jnp.sum(every[i * GROUP : (i + 1) * GROUP], axis=0, keepdims=True))
    wide = 8 * GROUP
    turned = []
    for i, (template_at, _) in enumerate(entries):
        real, imag = (
            jnp.concatenate(
                [block_transpose(found[:, at : at + wide]) for at in range(0, windows * GROUP, wide)], axis=0
            )
            for found in (jnp.concatenate(sums[2 * i + part], axis=0) for part in range(2))
        )
        cosine, sine_table = (turn[template_at, part, pl.ds(half, 1)] for part in range(2))
        turned.append((real * cosine - imag * sine_table, real * sine_table + imag * cosine))
    return turned


def all_lags(parts, high, low):
    windows = parts[0][0].shape[0]
    straight = jnp.concatenate([v for real, imag in parts for v in (real, imag)], axis=1)
    turned = jnp.concatenate([v for real, imag in parts for v in (imag, -real)], axis=1)
    lane = lax.broadcasted_iota(jnp.int32, straight.shape, 1) % 4
    picked = [jnp.where(lane == r, straight, 0.0) for r in range(4)]
    picked += [jnp.where(lane == r, turned, 0.0) for r in (1, 3)]
    rows = jnp.concatenate(picked, axis=0)
    rows_high, rows_low = two_halves(rows)
    table_high, table_low = (jnp.concatenate([t[r] for r in range(len(parts))], axis=0) for t in (high, low))
    both = product(jnp.concatenate([rows_high, rows_low], axis=0), table_high, (1, 0))
    sums = both[: rows.shape[0]] + both[rows.shape[0] :] + product(rows_high, table_low, (1, 0))
    re0, re1, re2, re3, im1, im3 = (sums[i * windows : (i + 1) * windows] for i in range(6))
    even, odd, even_turned, odd_turned = re0 + re2, re1 + re3, re0 - re2, im1 - im3
    return [even + odd, even_turned - odd_turned, even - odd, even_turned + odd_turned]


def own_kernel(
    masks, offsets, records, templates, high, low, held, turn, used, held_high, held_low, spectra, theirs, rest, template, numbers, sems
):
    halves = turn.shape[2]
    runs = records.shape[2] // RUN
    first_half = lax.axis_index("freq") * halves
    small = [
        pltpu.make_async_copy(masks, numbers[0], sems.at[0]),
        pltpu.make_async_copy(offsets, numbers[1], sems.at[1]),
    ]
    pieces = [
        pltpu.make_async_copy(values.at[:, :, pl.ds(r * RUN, RUN), :], to.at[:, :, pl.ds(r * RUN, RUN), :], sem)
        for r in range(runs)
        for values, to, sem in (
            (templates, template, sems.at[5 + 2 * r]),
            (records, held, sems.at[6 + 2 * r]),
        )
        if r < HALF // RUN or to is held
    ]
    tables = [
        pltpu.make_async_copy(table.at[pl.ds(first_half, halves)], to, sems.at[2 + i])
        for i, (table, to) in enumerate(((high, held_high), (low, held_low)))
    ]
    from_bin = pl.multiple_of((1 - lax.axis_index("parts")) * HALF, HALF)
    tables.append(pltpu.make_async_copy(templates.at[:, :, pl.ds(from_bin, HALF), :], theirs, sems.at[4]))
    tables.append(pltpu.make_async_copy(templates.at[:, :, pl.ds(HALF, rest.shape[2]), :], rest, sems.at[5 + 2 * runs]))
    for copy in small + pieces + tables:
        copy.start()
    for copy in small:
        copy.wait()
    masks, offsets = numbers
    row = lax.broadcasted_iota(jnp.int32, (halves, HALF), 0)
    lane = lax.broadcasted_iota(jnp.int32, (halves, HALF), 1)
    bin_index = (first_half + row) * HALF + lane
    for t in range(turn.shape[0]):
        phase = offsets[t] * bin_index % NSAMP
        angle = 2.0 * math.pi / NSAMP * phase.astype(jnp.float32)
        turn[t, 0] = jnp.cos(angle)
        turn[t, 1] = jnp.sin(angle)
        used[t] = mask_row(masks, t, held.shape[3])
    template_at = lax.axis_index("blk")

    def ready(g):
        if g * GROUP % RUN == 0:
            at = 2 * g * GROUP // RUN
            for copy in pieces[at : at + 2]:
                copy.wait()

    ((spectra[0], spectra[1]),) = half_spectra([(template_at, [template])], 0, held, turn, used, ready)
    for copy in pieces[2 * HALF // RUN :] + tables:
        copy.wait()


def pieces_kernel(plan, held, turn, used, *refs):
    ds, counts, own = plan
    *refs, out = refs
    entries = []
    for d, count in zip(ds, counts):
        entries.append((lax.axis_index("blk") ^ d, refs[:count]))
        refs = refs[count:]
    found = half_spectra(entries, lax.axis_index("parts") if own else 1, held, turn, used)
    for i, (real, imag) in enumerate(found):
        out[i, 0] = real
        out[i, 1] = imag


def lags_kernel(plan, held, turn, used, high, low, flipped, *refs):
    ds, counts, n_whole = plan
    *refs, spectra, lags = refs
    outs = refs[-lags.shape[0] :]
    whole, early, refs = refs[: 2 * n_whole], refs[2 * n_whole], refs[2 * n_whole + 1 : -lags.shape[0]]
    part = lax.axis_index("parts")
    entries = []
    for d, count in zip(ds, counts):
        entries.append((lax.axis_index("blk") ^ d, refs[:count]))
        refs = refs[count:]
    for i in range(n_whole):
        spectra[i, 0] = whole[2 * i][...]
        spectra[i, 1] = whole[2 * i + 1][0]
    found = half_spectra(entries, 1 - part, held, turn, used, flipped=flipped)
    for i, (real, imag) in enumerate(found):
        spectra[n_whole + i, part] = early[i]
        spectra[n_whole + i, 1 - part, 0] = real
        spectra[n_whole + i, 1 - part, 1] = imag
    me = lax.axis_index("chan") * lax.axis_size("freq") + lax.axis_index("freq")
    blocks, windows, width = lags.shape
    total, halves = spectra.shape[:2]
    parts = [
        tuple(jnp.concatenate([spectra[i, h, part] for i in range(total)], axis=0) for part in range(2))
        for h in range(halves)
    ]
    folded = all_lags(parts, high, low)
    for i in range(total):
        at = slice(i * windows, (i + 1) * windows)
        for n in range(blocks):
            start = n * width
            lags[n] = folded[start // FOLD][at, start % FOLD : start % FOLD + width]
        for n in range(blocks):
            outs[n][i] = lags[me ^ n]


def sum_kernel(orders, *refs):
    *parts, out = refs
    per = len(parts) // len(orders)
    for g, order in enumerate(orders):
        for i, d in enumerate(order):
            total = parts[g * per][i]
            for part in parts[g * per + 1 : (g + 1) * per]:
                total += part[i]
            out[lax.axis_index("blk") ^ d] = total


IN_VMEM = pl.BlockSpec(memory_space=pltpu.VMEM)
IN_HBM = pl.BlockSpec(memory_space=pltpu.HBM)
PARAMS = pltpu.CompilerParams(vmem_limit_bytes=VMEM_LIMIT)


def in_vmem(values):
    return [pltpu.with_memory_space_constraint(v, pltpu.VMEM) for v in values]


def in_hbm(values):
    return [pltpu.with_memory_space_constraint(v, pltpu.HBM) for v in values]


def own_template(masks, offsets, records, template, high, low):
    windows, _, bin_count, width = records.shape
    halves = bin_count // HALF
    table = (halves,) + high.shape[1:]
    out_shape = [
        pltpu.VMEM(records.shape, records.dtype),
        pltpu.VMEM((offsets.shape[0], 2, halves, HALF), jnp.float32),
        pltpu.VMEM((offsets.shape[0], 1, width), jnp.float32),
        pltpu.VMEM(table, high.dtype),
        pltpu.VMEM(table, low.dtype),
        pltpu.VMEM((2, windows, HALF), jnp.float32),
        pltpu.VMEM((1, 2, HALF, width), template.dtype),
        pltpu.VMEM((1, 2, bin_count - HALF, width), template.dtype),
    ]
    *held, spectra, theirs, rest = pl.pallas_call(
        own_kernel,
        in_specs=[IN_HBM] * 6,
        out_specs=[IN_VMEM] * len(out_shape),
        out_shape=out_shape,
        scratch_shapes=[
            pltpu.VMEM((1, 2, HALF, width), template.dtype),
            (pltpu.SMEM(masks.shape, masks.dtype), pltpu.SMEM(offsets.shape, offsets.dtype)),
            pltpu.SemaphoreType.DMA((2 * (bin_count // RUN) + 6,)),
        ],
        compiler_params=PARAMS,
    )(*in_hbm((masks, offsets, records, template, high, low)))
    return held, spectra, theirs, rest


def early_half(held, entries, own=True):
    windows = held[0].shape[0]
    plan = (tuple(d for d, _ in entries), tuple(len(pieces) for _, pieces in entries), own)
    operands = in_vmem([*held[:3], *(piece for _, pieces in entries for piece in pieces)])
    return pl.pallas_call(
        functools.partial(pieces_kernel, plan),
        in_specs=[IN_VMEM] * len(operands),
        out_specs=IN_VMEM,
        out_shape=pltpu.VMEM((len(entries), 2, windows, HALF), jnp.float32),
        compiler_params=PARAMS,
    )(*operands)


def flip(held):
    windows, _, _, width = held[0].shape
    return pl.pallas_call(
        flip_kernel,
        in_specs=[IN_VMEM],
        out_specs=IN_VMEM,
        out_shape=pltpu.VMEM((HALF // GROUP, 2 * width, windows * GROUP), held[0].dtype),
        compiler_params=PARAMS,
    )(*in_vmem(held[:1]))


def lag_blocks(held, flipped, early, entries, whole, blocks):
    windows = held[0].shape[0]
    halves = held[0].shape[2] // HALF
    count = len(whole) + len(entries)
    block = (windows, NSAMP // blocks)
    plan = (tuple(d for d, _ in entries), tuple(len(pieces) for _, pieces in entries), len(whole))
    operands = in_vmem([*held, flipped, *(half for pair in whole for half in pair), early, *(piece for _, pieces in entries for piece in pieces)])
    return pl.pallas_call(
        functools.partial(lags_kernel, plan),
        in_specs=[IN_VMEM] * len(operands),
        out_specs=[IN_VMEM] * blocks,
        out_shape=[jax.ShapeDtypeStruct((count,) + block, jnp.float32)] * blocks,
        scratch_shapes=[
            pltpu.VMEM((count, halves, 2, windows, HALF), jnp.float32),
            pltpu.VMEM((blocks,) + block, jnp.float32),
        ],
        compiler_params=PARAMS,
    )(*operands)


def cut_kernel(template, *rest):
    *outs, sems = rest
    at = lax.axis_index("parts") * sum(out.shape[2] for out in outs)
    copies = []
    for i, out in enumerate(outs):
        bins = pl.ds(pl.multiple_of(at, GROUP), out.shape[2])
        copies.append(pltpu.make_async_copy(template.at[:, :, bins, :], out, sems.at[i]))
        at += out.shape[2]
    for copy in copies:
        copy.start()
    for copy in copies:
        copy.wait()


def cut(template, count):
    shape = template.shape[:2] + (template.shape[2] // (2 * count),) + template.shape[3:]
    return pl.pallas_call(
        cut_kernel,
        in_specs=[IN_HBM],
        out_specs=[IN_VMEM] * count,
        out_shape=[pltpu.VMEM(shape, template.dtype)] * count,
        scratch_shapes=[pltpu.SemaphoreType.DMA((count,))],
        compiler_params=PARAMS,
    )(*in_hbm([template]))


def join_kernel(count, *refs):
    *pieces, out = refs
    width = pieces[0].shape[2]
    for i in range(count):
        out[:, :, i * width : (i + 1) * width, :] = pieces[i][...]
    if len(pieces) > count:

        @pl.when((lax.axis_index("blk") + 1) & 2 != 0)
        def _():
            out[...] = pieces[count][...]


def join(pieces, *middle):
    one = pieces[0]
    shape = one.shape[:2] + (len(pieces) * one.shape[2],) + one.shape[3:]
    operands = in_vmem([*pieces, *middle])
    return pl.pallas_call(
        functools.partial(join_kernel, len(pieces)),
        in_specs=[IN_VMEM] * len(operands),
        out_specs=IN_VMEM,
        out_shape=pltpu.VMEM(shape, one.dtype),
        compiler_params=PARAMS,
    )(*operands)


def partners(n, d):
    return [(i, i ^ d) for i in range(n)]


def after(value, *others):
    return lax.optimization_barrier((value,) + others)[0]


def swap(piece):
    return lax.ppermute(piece, "parts", partners(2, 1))


def any_line(held, mine, own, exchange, lags_of):
    n_blk = lax.axis_size("blk")
    orders, parts = [], []
    for begin in range(1, n_blk, BATCH):
        order = range(begin, min(begin + BATCH, n_blk))
        arrived = [lax.ppermute(mine, "blk", partners(n_blk, d)) for d in order]
        early = early_half(held, [(d, [a]) for d, a in zip(order, arrived)])
        whole = [own] if begin == 1 else []
        parts += exchange(lags_of(early, [(d, [swap(a)]) for d, a in zip(order, arrived)], whole))
        orders.append((0,) * len(whole) + tuple(order))
    return orders, parts


def line_of_four(held, mine, theirs, arrived, near, rest, spectra, flipped, exchange, lags_of):
    own = (spectra, early_half(held, [(0, [rest])], False))
    middle = lax.ppermute(after(mine, spectra), "blk", [(0, 0), (1, 2), (2, 1), (3, 3)])
    arrived = [after(a, own[1], flipped) for a in arrived]
    ends = [lax.ppermute(a, "blk", partners(4, 1)) for a in arrived]
    swapped = swap(join([after(arrived[0], near), *arrived[1:]]))
    third = join(ends, middle)
    third_swapped = swap(third)
    near_rest = lax.ppermute(after(theirs, third), "blk", partners(4, 1))
    early = early_half(held, [(1, [near]), (2, arrived), (3, [third])])
    parts = exchange(lags_of(early, [(1, [near_rest]), (2, [swapped]), (3, [third_swapped])], [own]))
    return [(0, 1, 2, 3)], parts


def shards(records, templates, masks, offsets):
    n_blk, n_chan, n_freq = (lax.axis_size(a) for a in ("blk", "chan", "freq"))
    windows = records.shape[0]
    blocks = n_chan * n_freq
    high, low = (jnp.asarray(t) for t in lag_tables())

    def exchange(found):
        return [found[0]] + [lax.ppermute(found[n], ("chan", "freq"), partners(blocks, n)) for n in range(1, blocks)]

    pieces = cut(templates, PIECES)
    mine = join(pieces)
    if n_blk == 4:
        arrived = [lax.ppermute(piece, "blk", partners(n_blk, 2)) for piece in pieces]
        near = lax.ppermute(mine, "blk", partners(n_blk, 1))
    held, spectra, theirs, rest = own_template(masks, offsets, records, templates, high, low)
    flipped = flip(held)
    after_all = (exchange, lambda *found: lag_blocks(held, flipped, *found, blocks))
    if n_blk == 4:
        orders, parts = line_of_four(held, mine, theirs, arrived, near, rest, spectra, flipped, *after_all)
    else:
        own = (spectra, early_half(held, [(0, [rest])], False))
        orders, parts = any_line(held, mine, own, *after_all)
    return pl.pallas_call(
        functools.partial(sum_kernel, orders),
        in_specs=[IN_VMEM] * len(parts),
        out_specs=IN_VMEM,
        out_shape=jax.ShapeDtypeStruct((n_blk, windows, NSAMP // blocks), jnp.float32),
        compiler_params=PARAMS,
    )(*parts)


def solution(mesh):
    placed = (P(("parts", "blk"), None, "freq", "chan"), P("blk", None, "freq", "chan"), P(), P())
    return jax.shard_map(
        shards,
        mesh=mesh,
        in_specs=placed,
        out_specs=P(None, ("parts", "blk"), ("chan", "freq")),
        check_vma=False,
    )
```

time: 41.4 us -> 40.9 us (0.988)
  waiting for transfers between devices: 6.82 us -> 16.1 us
  starting transfers between devices: 18.2 us -> 13.3 us
  Pallas kernels: 16.1 us -> 11.3 us
    ppermute x2 -> x1, waiting for transfers between devices: 0.01 us -> 4.7 us  [line_of_four(): ends = [lax.ppermute(a, 'blk', partners(4, 1)) for a in arrived]]
    pallas_call x7 -> x4, Pallas kernels: 9.16 us -> 5.82 us  [the longest x2 3.16 us: early_half(): pl.pallas_call(functools.partial(pieces_kernel, plan), in_specs=[IN_VMEM]...]
    ppermute x2 -> x1, starting transfers between devices: 2.53 us -> 0.01 us  [line_of_four(): ends = [lax.ppermute(a, 'blk', partners(4, 1)) for a in arrived]]
    ppermute x1, waiting for transfers between devices: 0.01 us -> 2.31 us  [line_of_four(): near_rest = lax.ppermute(after(theirs, third), 'blk', partners(4, 1))]
    ppermute x6 -> x3, starting transfers between devices: 3.84 us -> 1.93 us  [exchange(): lax.ppermute(found[n], ('chan', 'freq'), partners(blocks, n))]
    ppermute x2, waiting for transfers between devices: 0.01 us -> 1.46 us  [swap(): return lax.ppermute(piece, 'parts', partners(2, 1))]
    pallas_call x1, Pallas kernels: 5.22 us -> 3.87 us  [own_template(): pl.pallas_call(own_kernel, in_specs=[IN_HBM] * 6, out_specs=[IN_VMEM] * l...]
    ppermute x2 -> x1, waiting for transfers between devices: 3.28 us -> 3.89 us  [shards(): lax.ppermute(piece, 'blk', partners(n_blk, 2))]
  transfers between devices with their start and end apart: 15 -> 10, of which waited for: 3 -> 6; matrix products, arithmetic and copies ran while one was open for 0% -> 0% of each run, Pallas kernels for 35% -> 20%
where the time goes in v4:
time: 40.9 us; the launch traced here: 40.8 us
  waiting for transfers between devices  16.1 us (39%)
  starting transfers between devices  13.3 us (33%)
  Pallas kernels  11.3 us (28%)
    ppermute x1, waiting for transfers between devices, line_of_four(): ends = [lax.ppermute(a, 'blk', partners(4, 1)) for a in arrived]  4.7 us
    ppermute x1, starting transfers between devices, shards(): lax.ppermute(piece, 'blk', partners(n_blk, 2))  4.1 us
    ppermute x1, waiting for transfers between devices, shards(): lax.ppermute(piece, 'blk', partners(n_blk, 2))  3.89 us
    pallas_call x1, Pallas kernels, own_template(): pl.pallas_call(own_kernel, in_specs=[IN_HBM] * 6, out_specs=[IN_VMEM] * l...  3.87 us
    ppermute x3, waiting for transfers between devices, exchange(): lax.ppermute(found[n], ('chan', 'freq'), partners(blocks, n))  3.69 us
    ppermute x2, starting transfers between devices, swap(): return lax.ppermute(piece, 'parts', partners(2, 1))  3.45 us
    pallas_call x2, Pallas kernels, early_half(): pl.pallas_call(functools.partial(pieces_kernel, plan), in_specs=[IN_VMEM]...  3.16 us
    ppermute x1, waiting for transfers between devices, line_of_four(): near_rest = lax.ppermute(after(theirs, third), 'blk', partners(4, 1))  2.31 us
  transfers between devices with their start and end apart: 10, of which 6 were waited for; matrix products, arithmetic and copies ran while one was open for 0% of the time, Pallas kernels for 20%

profile of v4, /device:TPU:0, one launch (start us, length us, event | category | flops | bytes accessed | tf_op | source)
XLA Modules:
  0.0 40.8 jit_solution(7705976330657347514)
XLA Ops:
  0.0 1.0 %shard_map.67.refs_0_ = bf16[1,2,128,512]{3,2,1,0:T(8,128)(2,1)S(1)} custom-call(bf16[1,2,256,512]{3,2,1,0:T(8,128)(2,1)} %template.1), custom_call_target="tpu_custom_call" | custom-call | tf_op jit(solution)/shard_map/pallas_call | solution.py:346
  1.0 4.1 %collective-permute-start.1 = (bf16[1,2,128,512]{3,2,1,0:T(8,128)(2,1)S(1)}, bf16[1,2,128,512]{3,2,1,0:T(8,128)(2,1)S(1)}, u32[]{:S(2)}, u32[]{:S(2)}) collective-permute-start(bf16[1,2,128,512]{3,2,1,0:T(8,128)(2,1)S(1)} %shard_map.67.refs_0_), channel_id=1, source_target_pairs={{0,8},{4,12},{8,0},{12,4},{1,9},{5,13},{9,1},{13,5},{2,10},{6,14},... | collective-permute-start | bytes 786440 | tf_op jit(solution)/shard_map/ppermute | solution.py:432
  5.1 1.6 %collective-permute-start = (bf16[1,2,128,512]{3,2,1,0:T(8,128)(2,1)S(1)}, bf16[1,2,128,512]{3,2,1,0:T(8,128)(2,1)S(1)}, u32[]{:S(2)}, u32[]{:S(2)}) collective-permute-start(bf16[1,2,128,512]{3,2,1,0:T(8,128)(2,1)S(1)} %shard_map.68), channel_id=1, source_target_pairs={{0,4},{4,0},{8,12},{12,8},{1,5},{5,1},{9,13},{13,9},{2,6},{6,2},{1... | collective-permute-start | bytes 786440 | tf_op jit(solution)/shard_map/ppermute | solution.py:433
  6.7 3.9 %shard_map.64 = (bf16[16,2,256,512]{3,2,1,0:T(8,128)(2,1)S(1)}, f32[4,2,2,128]{3,2,1,0:T(2,128)S(1)}, f32[4,1,512]{2,1,0:T(1,128)S(1)}, bf16[2,256,256]{2,1,0:T(...) custom-call(s32[4,4]{1,0:T(4,128)} %masks.1, ...), custom_call_target="tpu_custom_call" | custom-call | tf_op jit(solution)/shard_map/pallas_call | solution.py:271
  10.6 0.7 %collective-permute-start.3 = (bf16[1,2,128,512]{3,2,1,0:T(8,128)(2,1)S(1)}, bf16[1,2,128,512]{3,2,1,0:T(8,128)(2,1)S(1)}, u32[]{:S(2)}, u32[]{:S(2)}) collective-permute-start(bf16[1,2,128,512]{3,2,1,0:T(8,128)(2,1)S(1)} %shard_map.68), channel_id=1, source_target_pairs={{0,0},{4,8},{8,4},{12,12},{1,1},{5,9},{9,5},{13,13},{2,2},{6,10},{... | collective-permute-start | bytes 786440 | tf_op jit(solution)/shard_map/ppermute | solution.py:408
  11.3 1.1 %shard_map.65.flipped = bf16[8,1024,256]{2,1,0:T(8,128)(2,1)S(1)} custom-call(bf16[16,2,256,512]{3,2,1,0:T(8,128)(2,1)S(1)} %get-tuple-element.21.records.held), custom_call_target="tpu_custom_call" | custom-call | tf_op jit(solution)/shard_map/pallas_call | solution.py:301
  12.4 1.5 %shard_map.66.refs_1_ = f32[1,2,16,128]{3,2,1,0:T(8,128)S(1)} custom-call(bf16[16,2,256,512]{3,2,1,0:T(8,128)(2,1)S(1)} %get-tuple-element.21.records.held, f32[4,2,2,128]{3,2,1,0:T(2,128)S(1)} %get-tuple-element.22.turn, f32[4,1,512]{2,1,0:T(1,128)S(1)} %get-tuple-element.23.used, bf16[1,2,128,512]{3,2,1,0:T(8,128)(2,1)S(1)} %get-tuple-element.27.refs_0_), custom_call_target="tpu_custom_call" | custom-call | tf_op jit(solution)/shard_map/pallas_call | solution.py:290
  14.0 3.9 %collective-permute-done.1.refs_1_.refs_0_ = bf16[1,2,128,512]{3,2,1,0:T(8,128)(2,1)S(1)} collective-permute-done((bf16[1,2,128,512]{3,2,1,0:T(8,128)(2,1)S(1)}, bf16[1,2,128,512]{3,2,1,0:T(8,128)(2,1)S(1)}, u32[]{:S(2)}, u32[]{:S(2)}) %collective-permute-start.1) | collective-permute-done | bytes 262176 | tf_op jit(solution)/shard_map/ppermute | solution.py:432
  17.9 0.0 collective-permute-start.2
  17.9 0.0 collective-permute-done.refs_0_
  17.9 1.9 %collective-permute-start.5 = (bf16[1,2,128,512]{3,2,1,0:T(8,128)(2,1)S(1)}, bf16[1,2,128,512]{3,2,1,0:T(8,128)(2,1)S(1)}, u32[]{:S(2)}, u32[]{:S(2)}) collective-permute-start(bf16[1,2,128,512]{3,2,1,0:T(8,128)(2,1)S(1)} %shard_map.71), channel_id=1, source_target_pairs={{0,16},{16,0},{1,17},{17,1},{2,18},{18,2},{3,19},{19,3},{4,20},{20... | collective-permute-start | bytes 786440 | tf_op jit(solution)/shard_map/ppermute | solution.py:390
  19.8 0.0 collective-permute-done.3.refs_1_
  19.8 4.7 %collective-permute-done.2.refs_0_ = bf16[1,2,128,512]{3,2,1,0:T(8,128)(2,1)S(1)} collective-permute-done((bf16[1,2,128,512]{3,2,1,0:T(8,128)(2,1)S(1)}, bf16[1,2,128,512]{3,2,1,0:T(8,128)(2,1)S(1)}, u32[]{:S(2)}, u32[]{:S(2)}) %collective-permute-start.2) | collective-permute-done | bytes 262176 | tf_op jit(solution)/shard_map/ppermute | solution.py:410
  24.6 1.5 %collective-permute-start.4 = (bf16[1,2,128,512]{3,2,1,0:T(8,128)(2,1)S(1)}, bf16[1,2,128,512]{3,2,1,0:T(8,128)(2,1)S(1)}, u32[]{:S(2)}, u32[]{:S(2)}) collective-permute-start(bf16[1,2,128,512]{3,2,1,0:T(8,128)(2,1)S(1)} %get-tuple-element.31), channel_id=1, source_target_pairs={{0,4},{4,0},{8,12},{12,8},{1,5},{5,1},{9,13},{13,9},{2,6},{6,2},{1... | collective-permute-start | bytes 786440 | tf_op jit(solution)/shard_map/ppermute | solution.py:414
  26.0 1.5 %collective-permute-start.6 = (bf16[1,2,128,512]{3,2,1,0:T(8,128)(2,1)S(1)}, bf16[1,2,128,512]{3,2,1,0:T(8,128)(2,1)S(1)}, u32[]{:S(2)}, u32[]{:S(2)}) collective-permute-start(bf16[1,2,128,512]{3,2,1,0:T(8,128)(2,1)S(1)} %shard_map.69.refs_2_), channel_id=1, source_target_pairs={{0,16},{16,0},{1,17},{17,1},{2,18},{18,2},{3,19},{19,3},{4,20},{20... | collective-permute-start | bytes 786440 | tf_op jit(solution)/shard_map/ppermute | solution.py:390
  27.6 1.6 %shard_map.70.refs_2_ = f32[3,2,16,128]{3,2,1,0:T(8,128)S(1)} custom-call(bf16[16,2,256,512]{3,2,1,0:T(8,128)(2,1)S(1)} %get-tuple-element.21.records.held, f32[4,2,2,128]{3,2,1,0:T(2,128)S(1)} %get-tuple-element.22.turn, f32[4,1,512]{2,1,0:T(1,128)S(1)} %get-tuple-element.23.used, bf16[1,2,128,512]{3,2,1,0:T(8,128)(2,1)S(1)} %collective-permute-done.refs_0_, ...), custom_call_target="tpu_custom_call" | custom-call | tf_op jit(solution)/shard_map/pallas_call | solution.py:290
  29.2 0.0 collective-permute-done.5.refs_4_
  29.2 2.3 %collective-permute-done.4.refs_3_ = bf16[1,2,128,512]{3,2,1,0:T(8,128)(2,1)S(1)} collective-permute-done((bf16[1,2,128,512]{3,2,1,0:T(8,128)(2,1)S(1)}, bf16[1,2,128,512]{3,2,1,0:T(8,128)(2,1)S(1)}, u32[]{:S(2)}, u32[]{:S(2)}) %collective-permute-start.4) | collective-permute-done | bytes 262176 | tf_op jit(solution)/shard_map/ppermute | solution.py:414
  31.5 1.5 %collective-permute-done.6.refs_5_ = bf16[1,2,128,512]{3,2,1,0:T(8,128)(2,1)S(1)} collective-permute-done((bf16[1,2,128,512]{3,2,1,0:T(8,128)(2,1)S(1)}, bf16[1,2,128,512]{3,2,1,0:T(8,128)(2,1)S(1)}, u32[]{:S(2)}, u32[]{:S(2)}) %collective-permute-start.6) | collective-permute-done | bytes 262176 | tf_op jit(solution)/shard_map/ppermute | solution.py:390
  33.0 1.5 %shard_map.72 = (f32[4,16,256]{2,1,0:T(8,128)S(1)}, f32[4,16,256]{2,1,0:T(8,128)S(1)}, f32[4,16,256]{2,1,0:T(8,128)S(1)}, f32[4,16,256]{2,1,0:T(8,128)S(1)}) custom-call(bf16[16,2,256,512]{3,2,1,0:T(8,128)(2,1)S(1)} %get-tuple-element.21.records.held, f32[4,2,2,128]{3,2,1,0:T(2,128)S(1)} %get-tuple-element.22.turn, f32[4,1,512]{2,1,0:T(1,128)S(1)} %get-tuple-element.23.used, ...), custom_call_target="tpu_custom_call" | custom-call | tf_op jit(solution)/shard_map/pallas_call | solution.py:317
  34.5 0.1 collective-permute-start.7
  34.6 1.2 %collective-permute-start.8 = (f32[4,16,256]{2,1,0:T(8,128)S(1)}, f32[4,16,256]{2,1,0:T(8,128)S(1)}, u32[]{:S(2)}, u32[]{:S(2)}) collective-permute-start(f32[4,16,256]{2,1,0:T(8,128)S(1)} %get-tuple-element.35), channel_id=1, source_target_pairs={{0,2},{1,3},{2,0},{3,1},{4,6},{5,7},{6,4},{7,5},{8,10},{9,11},{10,... | collective-permute-start | bytes 196616 | tf_op jit(solution)/shard_map/ppermute | solution.py:427
  35.7 0.7 %collective-permute-start.9 = (f32[4,16,256]{2,1,0:T(8,128)S(1)}, f32[4,16,256]{2,1,0:T(8,128)S(1)}, u32[]{:S(2)}, u32[]{:S(2)}) collective-permute-start(f32[4,16,256]{2,1,0:T(8,128)S(1)} %get-tuple-element.36), channel_id=1, source_target_pairs={{0,3},{1,2},{2,1},{3,0},{4,7},{5,6},{6,5},{7,4},{8,11},{9,10},{10,... | collective-permute-start | bytes 196616 | tf_op jit(solution)/shard_map/ppermute | solution.py:427
  36.4 0.0 collective-permute-done.7.refs_1_
  36.4 3.0 %collective-permute-done.8.refs_2_ = f32[4,16,256]{2,1,0:T(8,128)S(1)} collective-permute-done((f32[4,16,256]{2,1,0:T(8,128)S(1)}, f32[4,16,256]{2,1,0:T(8,128)S(1)}, u32[]{:S(2)}, u32[]{:S(2)}) %collective-permute-start.8) | collective-permute-done | bytes 65568 | tf_op jit(solution)/shard_map/ppermute | solution.py:427
  39.4 0.7 %collective-permute-done.9.refs_3_ = f32[4,16,256]{2,1,0:T(8,128)S(1)} collective-permute-done((f32[4,16,256]{2,1,0:T(8,128)S(1)}, f32[4,16,256]{2,1,0:T(8,128)S(1)}, u32[]{:S(2)}, u32[]{:S(2)}) %collective-permute-start.9) | collective-permute-done | bytes 65568 | tf_op jit(solution)/shard_map/ppermute | solution.py:427
  40.1 0.6 %shard_map.73 = f32[4,16,256]{2,1,0:T(8,128)} custom-call(f32[4,16,256]{2,1,0:T(8,128)S(1)} %get-tuple-element.33.refs_0_, f32[4,16,256]{2,1,0:T(8,128)S(1)} %collective-permute-done.7.refs_1_, f32[4,16,256]{2,1,0:T(8,128)S(1)} %collective-permute-done.8.refs_2_, f32[4,16,256]{2,1,0:T(8,128)S(1)} %collective-permute-done.9.refs_3_), custom_call_target="tpu_custom_call" | custom-call | tf_op jit(solution)/shard_map/pallas_call | solution.py:442
  (3 shorter events, 0.1 us)
Async XLA Ops:
  1.0 16.9 %collective-permute-start.1 = (bf16[1,2,128,512]{3,2,1,0:T(8,128)(2,1)S(1)}, bf16[1,2,128,512]{3,2,1,0:T(8,128)(2,1)S(1)}, u32[]{:S(2)}, u32[]{:S(2)}) collective-permute-start(bf16[1,2,128,512]{3,2,1,0:T(8,128)(2,1)S(1)} %shard_map.67.refs_0_), channel_id=1, source_target_pairs={{0,8},{4,12},{8,0},{12,4},{1,9},{5,13},{9,1},{13,5},{2,10},{6,14},... | collective-permute-start | bytes 786440 | tf_op jit(solution)/shard_map/ppermute | solution.py:432
  5.1 12.8 %collective-permute-start = (bf16[1,2,128,512]{3,2,1,0:T(8,128)(2,1)S(1)}, bf16[1,2,128,512]{3,2,1,0:T(8,128)(2,1)S(1)}, u32[]{:S(2)}, u32[]{:S(2)}) collective-permute-start(bf16[1,2,128,512]{3,2,1,0:T(8,128)(2,1)S(1)} %shard_map.68), channel_id=1, source_target_pairs={{0,4},{4,0},{8,12},{12,8},{1,5},{5,1},{9,13},{13,9},{2,6},{6,2},{1... | collective-permute-start | bytes 786440 | tf_op jit(solution)/shard_map/ppermute | solution.py:433
  10.6 9.2 %collective-permute-start.3 = (bf16[1,2,128,512]{3,2,1,0:T(8,128)(2,1)S(1)}, bf16[1,2,128,512]{3,2,1,0:T(8,128)(2,1)S(1)}, u32[]{:S(2)}, u32[]{:S(2)}) collective-permute-start(bf16[1,2,128,512]{3,2,1,0:T(8,128)(2,1)S(1)} %shard_map.68), channel_id=1, source_target_pairs={{0,0},{4,8},{8,4},{12,12},{1,1},{5,9},{9,5},{13,13},{2,2},{6,10},{... | collective-permute-start | bytes 786440 | tf_op jit(solution)/shard_map/ppermute | solution.py:408
  17.9 6.7 %collective-permute-start.2 = (bf16[1,2,128,512]{3,2,1,0:T(8,128)(2,1)S(1)}, bf16[1,2,128,512]{3,2,1,0:T(8,128)(2,1)S(1)}, u32[]{:S(2)}, u32[]{:S(2)}) collective-permute-start(bf16[1,2,128,512]{3,2,1,0:T(8,128)(2,1)S(1)} %collective-permute-done.1.refs_1_.refs_0_), channel_id=1, source_target_pairs={{0,4},{4,0},{8,12},{12,8},{1,5},{5,1},{9,13},{13,9},{2,6},{6,2},{1... | collective-permute-start | bytes 786440 | tf_op jit(solution)/shard_map/ppermute | solution.py:410
  17.9 11.3 %collective-permute-start.5 = (bf16[1,2,128,512]{3,2,1,0:T(8,128)(2,1)S(1)}, bf16[1,2,128,512]{3,2,1,0:T(8,128)(2,1)S(1)}, u32[]{:S(2)}, u32[]{:S(2)}) collective-permute-start(bf16[1,2,128,512]{3,2,1,0:T(8,128)(2,1)S(1)} %shard_map.71), channel_id=1, source_target_pairs={{0,16},{16,0},{1,17},{17,1},{2,18},{18,2},{3,19},{19,3},{4,20},{20... | collective-permute-start | bytes 786440 | tf_op jit(solution)/shard_map/ppermute | solution.py:390
  24.6 7.0 %collective-permute-start.4 = (bf16[1,2,128,512]{3,2,1,0:T(8,128)(2,1)S(1)}, bf16[1,2,128,512]{3,2,1,0:T(8,128)(2,1)S(1)}, u32[]{:S(2)}, u32[]{:S(2)}) collective-permute-start(bf16[1,2,128,512]{3,2,1,0:T(8,128)(2,1)S(1)} %get-tuple-element.31), channel_id=1, source_target_pairs={{0,4},{4,0},{8,12},{12,8},{1,5},{5,1},{9,13},{13,9},{2,6},{6,2},{1... | collective-permute-start | bytes 786440 | tf_op jit(solution)/shard_map/ppermute | solution.py:414
  26.0 6.9 %collective-permute-start.6 = (bf16[1,2,128,512]{3,2,1,0:T(8,128)(2,1)S(1)}, bf16[1,2,128,512]{3,2,1,0:T(8,128)(2,1)S(1)}, u32[]{:S(2)}, u32[]{:S(2)}) collective-permute-start(bf16[1,2,128,512]{3,2,1,0:T(8,128)(2,1)S(1)} %shard_map.69.refs_2_), channel_id=1, source_target_pairs={{0,16},{16,0},{1,17},{17,1},{2,18},{18,2},{3,19},{19,3},{4,20},{20... | collective-permute-start | bytes 786440 | tf_op jit(solution)/shard_map/ppermute | solution.py:390
  34.5 1.9 %collective-permute-start.7 = (f32[4,16,256]{2,1,0:T(8,128)S(1)}, f32[4,16,256]{2,1,0:T(8,128)S(1)}, u32[]{:S(2)}, u32[]{:S(2)}) collective-permute-start(f32[4,16,256]{2,1,0:T(8,128)S(1)} %get-tuple-element.34), channel_id=1, source_target_pairs={{0,1},{1,0},{2,3},{3,2},{4,5},{5,4},{6,7},{7,6},{8,9},{9,8},{10,11... | collective-permute-start | bytes 196616 | tf_op jit(solution)/shard_map/ppermute | solution.py:427
  34.6 4.9 %collective-permute-start.8 = (f32[4,16,256]{2,1,0:T(8,128)S(1)}, f32[4,16,256]{2,1,0:T(8,128)S(1)}, u32[]{:S(2)}, u32[]{:S(2)}) collective-permute-start(f32[4,16,256]{2,1,0:T(8,128)S(1)} %get-tuple-element.35), channel_id=1, source_target_pairs={{0,2},{1,3},{2,0},{3,1},{4,6},{5,7},{6,4},{7,5},{8,10},{9,11},{10,... | collective-permute-start | bytes 196616 | tf_op jit(solution)/shard_map/ppermute | solution.py:427
  35.7 4.4 %collective-permute-start.9 = (f32[4,16,256]{2,1,0:T(8,128)S(1)}, f32[4,16,256]{2,1,0:T(8,128)S(1)}, u32[]{:S(2)}, u32[]{:S(2)}) collective-permute-start(f32[4,16,256]{2,1,0:T(8,128)S(1)} %get-tuple-element.36), channel_id=1, source_target_pairs={{0,3},{1,2},{2,1},{3,0},{4,7},{5,6},{6,5},{7,4},{8,11},{9,10},{10,... | collective-permute-start | bytes 196616 | tf_op jit(solution)/shard_map/ppermute | solution.py:427

commit v5 on v4

--- a/solution.py
+++ b/solution.py
@@ -17,6 +17,7 @@
 FOLD = 256
 PIECES = 1
 BATCH = 4
+OWN, OTHER = 2, 3
 VMEM_LIMIT = 24 * 2**20
 
 
@@ -177,42 +178,46 @@
             for copy in pieces[at : at + 2]:
                 copy.wait()
 
-    ((spectra[0], spectra[1]),) = half_spectra([(template_at, [template])], 0, held, turn, used, ready)
+    ((spectra[0, 0], spectra[0, 1]),) = half_spectra([(template_at, [template])], 0, held, turn, used, ready)
     for copy in pieces[2 * HALF // RUN :] + tables:
         copy.wait()
 
 
-def pieces_kernel(plan, held, turn, used, *refs):
-    ds, counts, own = plan
-    *refs, out = refs
+def half_at(place):
+    part = lax.axis_index("parts")
+    return {OWN: part, OTHER: 1 - part}.get(place, place)
+
+
+def entries_of(ds, counts, refs):
     entries = []
     for d, count in zip(ds, counts):
         entries.append((lax.axis_index("blk") ^ d, refs[:count]))
         refs = refs[count:]
-    found = half_spectra(entries, lax.axis_index("parts") if own else 1, held, turn, used)
+    return entries
+
+
+def pieces_kernel(plan, held, turn, used, *refs):
+    ds, counts, place = plan
+    *refs, out = refs
+    found = half_spectra(entries_of(ds, counts, refs), half_at(place), held, turn, used)
     for i, (real, imag) in enumerate(found):
         out[i, 0] = real
         out[i, 1] = imag
 
 
 def lags_kernel(plan, held, turn, used, high, low, flipped, *refs):
-    ds, counts, n_whole = plan
+    ds, counts, known = plan
     *refs, spectra, lags = refs
     outs = refs[-lags.shape[0] :]
-    whole, early, refs = refs[: 2 * n_whole], refs[2 * n_whole], refs[2 * n_whole + 1 : -lags.shape[0]]
-    part = lax.axis_index("parts")
-    entries = []
-    for d, count in zip(ds, counts):
-        entries.append((lax.axis_index("blk") ^ d, refs[:count]))
-        refs = refs[count:]
-    for i in range(n_whole):
-        spectra[i, 0] = whole[2 * i][...]
-        spectra[i, 1] = whole[2 * i + 1][0]
-    found = half_spectra(entries, 1 - part, held, turn, used, flipped=flipped)
+    for ref, (first, place) in zip(refs, known):
+        for i in range(ref.shape[0]):
+            spectra[first + i, half_at(place)] = ref[i]
+    entries = entries_of(ds, counts, refs[len(known) : -lags.shape[0]])
+    found = half_spectra(entries, half_at(OTHER), held, turn, used, flipped=flipped)
     for i, (real, imag) in enumerate(found):
-        spectra[n_whole + i, part] = early[i]
-        spectra[n_whole + i, 1 - part, 0] = real
-        spectra[n_whole + i, 1 - part, 1] = imag
+        at = spectra.shape[0] - len(entries) + i
+        spectra[at, half_at(OTHER), 0] = real
+        spectra[at, half_at(OTHER), 1] = imag
     me = lax.axis_index("chan") * lax.axis_size("freq") + lax.axis_index("freq")
     blocks, windows, width = lags.shape
     total, halves = spectra.shape[:2]
@@ -264,7 +269,7 @@
         pltpu.VMEM((offsets.shape[0], 1, width), jnp.float32),
         pltpu.VMEM(table, high.dtype),
         pltpu.VMEM(table, low.dtype),
-        pltpu.VMEM((2, windows, HALF), jnp.float32),
+        pltpu.VMEM((1, 2, windows, HALF), jnp.float32),
         pltpu.VMEM((1, 2, HALF, width), template.dtype),
         pltpu.VMEM((1, 2, bin_count - HALF, width), template.dtype),
     ]
@@ -283,9 +288,9 @@
     return held, spectra, theirs, rest
 
 
-def early_half(held, entries, own=True):
+def early_half(held, entries, place):
     windows = held[0].shape[0]
-    plan = (tuple(d for d, _ in entries), tuple(len(pieces) for _, pieces in entries), own)
+    plan = (tuple(d for d, _ in entries), tuple(len(pieces) for _, pieces in entries), place)
     operands = in_vmem([*held[:3], *(piece for _, pieces in entries for piece in pieces)])
     return pl.pallas_call(
         functools.partial(pieces_kernel, plan),
@@ -307,13 +312,16 @@
     )(*in_vmem(held[:1]))
 
 
-def lag_blocks(held, flipped, early, entries, whole, blocks):
+def lag_blocks(held, flipped, known, entries, count, blocks):
     windows = held[0].shape[0]
     halves = held[0].shape[2] // HALF
-    count = len(whole) + len(entries)
     block = (windows, NSAMP // blocks)
-    plan = (tuple(d for d, _ in entries), tuple(len(pieces) for _, pieces in entries), len(whole))
-    operands = in_vmem([*held, flipped, *(half for pair in whole for half in pair), early, *(piece for _, pieces in entries for piece in pieces)])
+    plan = (
+        tuple(d for d, _ in entries),
+        tuple(len(pieces) for _, pieces in entries),
+        tuple((first, place) for _, first, place in known),
+    )
+    operands = in_vmem([*held, flipped, *(k[0] for k in known), *(piece for _, pieces in entries for piece in pieces)])
     return pl.pallas_call(
         functools.partial(lags_kernel, plan),
         in_specs=[IN_VMEM] * len(operands),
@@ -390,31 +398,34 @@
     return lax.ppermute(piece, "parts", partners(2, 1))
 
 
-def any_line(held, mine, own, exchange, lags_of):
+def any_line(held, mine, rest, spectra, exchange, lags_of):
     n_blk = lax.axis_size("blk")
     orders, parts = [], []
-    for begin in range(1, n_blk, BATCH):
-        order = range(begin, min(begin + BATCH, n_blk))
-        arrived = [lax.ppermute(mine, "blk", partners(n_blk, d)) for d in order]
-        early = early_half(held, [(d, [a]) for d, a in zip(order, arrived)])
-        whole = [own] if begin == 1 else []
-        parts += exchange(lags_of(early, [(d, [swap(a)]) for d, a in zip(order, arrived)], whole))
-        orders.append((0,) * len(whole) + tuple(order))
+    for begin in range(0, n_blk, BATCH):
+        order = tuple(range(begin, min(begin + BATCH, n_blk)))
+        away = [d for d in order if d]
+        arrived = [lax.ppermute(mine, "blk", partners(n_blk, d)) for d in away]
+        known = [] if begin else [(spectra, 0, 0), (early_half(held, [(0, [rest])], 1), 0, 1)]
+        known.append((early_half(held, [(d, [a]) for d, a in zip(away, arrived)], OWN), len(order) - len(away), OWN))
+        parts += exchange(lags_of(known, [(d, [swap(a)]) for d, a in zip(away, arrived)], len(order)))
+        orders.append(order)
     return orders, parts
 
 
 def line_of_four(held, mine, theirs, arrived, near, rest, spectra, flipped, exchange, lags_of):
-    own = (spectra, early_half(held, [(0, [rest])], False))
     middle = lax.ppermute(after(mine, spectra), "blk", [(0, 0), (1, 2), (2, 1), (3, 3)])
-    arrived = [after(a, own[1], flipped) for a in arrived]
+    arrived = [after(a, flipped) for a in arrived]
     ends = [lax.ppermute(a, "blk", partners(4, 1)) for a in arrived]
-    swapped = swap(join([after(arrived[0], near), *arrived[1:]]))
+    second = join([after(arrived[0], near), *arrived[1:]])
+    swapped = swap(second)
+    pair = early_half(held, [(1, [near]), (2, [second])], OWN)
+    rest_half = early_half(held, [(0, [after(rest, pair)])], 1)
+    near_rest = lax.ppermute(after(theirs, rest_half), "blk", partners(4, 1))
     third = join(ends, middle)
     third_swapped = swap(third)
-    near_rest = lax.ppermute(after(theirs, third), "blk", partners(4, 1))
-    early = early_half(held, [(1, [near]), (2, arrived), (3, [third])])
-    parts = exchange(lags_of(early, [(1, [near_rest]), (2, [swapped]), (3, [third_swapped])], [own]))
-    return [(0, 1, 2, 3)], parts
+    known = [(spectra, 0, 0), (rest_half, 0, 1), (pair, 1, OWN), (early_half(held, [(3, [third])], OWN), 3, OWN)]
+    late = [(1, [near_rest]), (2, [swapped]), (3, [third_swapped])]
+    return [(0, 1, 2, 3)], exchange(lags_of(known, late, 4))
 
 
 def shards(records, templates, masks, offsets):
@@ -437,8 +448,7 @@
     if n_blk == 4:
         orders, parts = line_of_four(held, mine, theirs, arrived, near, rest, spectra, flipped, *after_all)
     else:
-        own = (spectra, early_half(held, [(0, [rest])], False))
-        orders, parts = any_line(held, mine, own, *after_all)
+        orders, parts = any_line(held, mine, rest, spectra, *after_all)
     return pl.pallas_call(
         functools.partial(sum_kernel, orders),
         in_specs=[IN_VMEM] * len(parts),

time: 40.9 us -> 39.6 us (0.968)
  waiting for transfers between devices: 16.1 us -> 12 us
  Pallas kernels: 11.3 us -> 12.9 us
  starting transfers between devices: 13.3 us -> 14.5 us
    ppermute x1, waiting for transfers between devices: 4.7 us -> 0.01 us  [line_of_four(): ends = [lax.ppermute(a, 'blk', partners(4, 1)) for a in arrived]]
    ppermute x1, waiting for transfers between devices: 3.89 us -> 5.43 us  [shards(): lax.ppermute(piece, 'blk', partners(n_blk, 2))]
    pallas_call x2 -> x3, Pallas kernels: 3.16 us -> 4.69 us  [early_half(): pl.pallas_call(functools.partial(pieces_kernel, plan), in_specs=[IN_VMEM]...]
    ppermute x1, waiting for transfers between devices: 2.31 us -> 1.43 us  [line_of_four(): near_rest = lax.ppermute(after(theirs, rest_half), 'blk', partners(4, 1))]
    ppermute x2, starting transfers between devices: 3.45 us -> 4.06 us  [swap(): return lax.ppermute(piece, 'parts', partners(2, 1))]
    ppermute x1, starting transfers between devices: 1.49 us -> 2.04 us  [line_of_four(): near_rest = lax.ppermute(after(theirs, rest_half), 'blk', partners(4, 1))]
  transfers between devices with their start and end apart: 10 -> 10, of which waited for: 6 -> 5; matrix products, arithmetic and copies ran while one was open for 0% -> 0% of each run, Pallas kernels for 20% -> 25%
where the time goes in v5:
time: 39.6 us; the launch traced here: 39.4 us
  starting transfers between devices  14.5 us (37%)
  Pallas kernels  12.9 us (33%)
  waiting for transfers between devices  12 us (30%)
    ppermute x1, waiting for transfers between devices, shards(): lax.ppermute(piece, 'blk', partners(n_blk, 2))  5.43 us
    pallas_call x3, Pallas kernels, early_half(): pl.pallas_call(functools.partial(pieces_kernel, plan), in_specs=[IN_VMEM]...  4.69 us
    ppermute x1, starting transfers between devices, shards(): lax.ppermute(piece, 'blk', partners(n_blk, 2))  4.1 us
    ppermute x2, starting transfers between devices, swap(): return lax.ppermute(piece, 'parts', partners(2, 1))  4.06 us
    pallas_call x1, Pallas kernels, own_template(): pl.pallas_call(own_kernel, in_specs=[IN_HBM] * 6, out_specs=[IN_VMEM] * l...  3.87 us
    ppermute x3, waiting for transfers between devices, exchange(): lax.ppermute(found[n], ('chan', 'freq'), partners(blocks, n))  3.75 us
    ppermute x1, starting transfers between devices, line_of_four(): near_rest = lax.ppermute(after(theirs, rest_half), 'blk', partners(4, 1))  2.04 us
    ppermute x3, starting transfers between devices, exchange(): lax.ppermute(found[n], ('chan', 'freq'), partners(blocks, n))  1.93 us
  transfers between devices with their start and end apart: 10, of which 5 were waited for; matrix products, arithmetic and copies ran while one was open for 0% of the time, Pallas kernels for 25%

profile of v5, /device:TPU:0, one launch (start us, length us, event | category | flops | bytes accessed | tf_op | source)
XLA Modules:
  0.0 39.4 jit_solution(5366295468828723322)
XLA Ops:
  0.0 1.0 %shard_map.66.refs_0_ = bf16[1,2,128,512]{3,2,1,0:T(8,128)(2,1)S(1)} custom-call(bf16[1,2,256,512]{3,2,1,0:T(8,128)(2,1)} %template.1), custom_call_target="tpu_custom_call" | custom-call | tf_op jit(solution)/shard_map/pallas_call | solution.py:354
  1.0 4.1 %collective-permute-start.1 = (bf16[1,2,128,512]{3,2,1,0:T(8,128)(2,1)S(1)}, bf16[1,2,128,512]{3,2,1,0:T(8,128)(2,1)S(1)}, u32[]{:S(2)}, u32[]{:S(2)}) collective-permute-start(bf16[1,2,128,512]{3,2,1,0:T(8,128)(2,1)S(1)} %shard_map.66.refs_0_), channel_id=1, source_target_pairs={{0,8},{4,12},{8,0},{12,4},{1,9},{5,13},{9,1},{13,5},{2,10},{6,14},... | collective-permute-start | bytes 786440 | tf_op jit(solution)/shard_map/ppermute | solution.py:443
  5.1 1.6 %collective-permute-start = (bf16[1,2,128,512]{3,2,1,0:T(8,128)(2,1)S(1)}, bf16[1,2,128,512]{3,2,1,0:T(8,128)(2,1)S(1)}, u32[]{:S(2)}, u32[]{:S(2)}) collective-permute-start(bf16[1,2,128,512]{3,2,1,0:T(8,128)(2,1)S(1)} %shard_map.67), channel_id=1, source_target_pairs={{0,4},{4,0},{8,12},{12,8},{1,5},{5,1},{9,13},{13,9},{2,6},{6,2},{1... | collective-permute-start | bytes 786440 | tf_op jit(solution)/shard_map/ppermute | solution.py:444
  6.7 3.9 %shard_map.64 = (bf16[16,2,256,512]{3,2,1,0:T(8,128)(2,1)S(1)}, f32[4,2,2,128]{3,2,1,0:T(2,128)S(1)}, f32[4,1,512]{2,1,0:T(1,128)S(1)}, bf16[2,256,256]{2,1,0:T(...) custom-call(s32[4,4]{1,0:T(4,128)} %masks.1, ...), custom_call_target="tpu_custom_call" | custom-call | tf_op jit(solution)/shard_map/pallas_call | solution.py:276
  10.6 0.7 %collective-permute-start.3 = (bf16[1,2,128,512]{3,2,1,0:T(8,128)(2,1)S(1)}, bf16[1,2,128,512]{3,2,1,0:T(8,128)(2,1)S(1)}, u32[]{:S(2)}, u32[]{:S(2)}) collective-permute-start(bf16[1,2,128,512]{3,2,1,0:T(8,128)(2,1)S(1)} %shard_map.67), channel_id=1, source_target_pairs={{0,0},{4,8},{8,4},{12,12},{1,1},{5,9},{9,5},{13,13},{2,2},{6,10},{... | collective-permute-start | bytes 786440 | tf_op jit(solution)/shard_map/ppermute | solution.py:416
  11.3 1.1 %shard_map.65.flipped = bf16[8,1024,256]{2,1,0:T(8,128)(2,1)S(1)} custom-call(bf16[16,2,256,512]{3,2,1,0:T(8,128)(2,1)S(1)} %get-tuple-element.22.records.held), custom_call_target="tpu_custom_call" | custom-call | tf_op jit(solution)/shard_map/pallas_call | solution.py:306
  12.4 5.4 %collective-permute-done.1.refs_0_ = bf16[1,2,128,512]{3,2,1,0:T(8,128)(2,1)S(1)} collective-permute-done((bf16[1,2,128,512]{3,2,1,0:T(8,128)(2,1)S(1)}, bf16[1,2,128,512]{3,2,1,0:T(8,128)(2,1)S(1)}, u32[]{:S(2)}, u32[]{:S(2)}) %collective-permute-start.1) | collective-permute-done | bytes 262176 | tf_op jit(solution)/shard_map/ppermute | solution.py:443
  17.9 0.0 collective-permute-start.2
  17.9 0.0 collective-permute-done.refs_0_
  17.9 1.9 %collective-permute-start.5 = (bf16[1,2,128,512]{3,2,1,0:T(8,128)(2,1)S(1)}, bf16[1,2,128,512]{3,2,1,0:T(8,128)(2,1)S(1)}, u32[]{:S(2)}, u32[]{:S(2)}) collective-permute-start(bf16[1,2,128,512]{3,2,1,0:T(8,128)(2,1)S(1)} %shard_map.68.refs_1_), channel_id=1, source_target_pairs={{0,16},{16,0},{1,17},{17,1},{2,18},{18,2},{3,19},{19,3},{4,20},{20... | collective-permute-start | bytes 786440 | tf_op jit(solution)/shard_map/ppermute | solution.py:398
  19.8 1.6 %shard_map.69.refs_2_ = f32[2,2,16,128]{3,2,1,0:T(8,128)S(1)} custom-call(bf16[16,2,256,512]{3,2,1,0:T(8,128)(2,1)S(1)} %get-tuple-element.22.records.held, f32[4,2,2,128]{3,2,1,0:T(2,128)S(1)} %get-tuple-element.23.turn, f32[4,1,512]{2,1,0:T(1,128)S(1)} %get-tuple-element.24.used, bf16[1,2,128,512]{3,2,1,0:T(8,128)(2,1)S(1)} %collective-permute-done.refs_0_, ...), custom_call_target="tpu_custom_call" | custom-call | tf_op jit(solution)/shard_map/pallas_call | solution.py:295
  21.4 1.5 %shard_map.70.refs_1_ = f32[1,2,16,128]{3,2,1,0:T(8,128)S(1)} custom-call(bf16[16,2,256,512]{3,2,1,0:T(8,128)(2,1)S(1)} %get-tuple-element.22.records.held, f32[4,2,2,128]{3,2,1,0:T(2,128)S(1)} %get-tuple-element.23.turn, f32[4,1,512]{2,1,0:T(1,128)S(1)} %get-tuple-element.24.used, bf16[1,2,128,512]{3,2,1,0:T(8,128)(2,1)S(1)} %get-tuple-element.31.refs_0_), custom_call_target="tpu_custom_call" | custom-call | tf_op jit(solution)/shard_map/pallas_call | solution.py:295
  23.0 2.0 %collective-permute-start.4 = (bf16[1,2,128,512]{3,2,1,0:T(8,128)(2,1)S(1)}, bf16[1,2,128,512]{3,2,1,0:T(8,128)(2,1)S(1)}, u32[]{:S(2)}, u32[]{:S(2)}) collective-permute-start(bf16[1,2,128,512]{3,2,1,0:T(8,128)(2,1)S(1)} %get-tuple-element.34), channel_id=1, source_target_pairs={{0,4},{4,0},{8,12},{12,8},{1,5},{5,1},{9,13},{13,9},{2,6},{6,2},{1... | collective-permute-start | bytes 786440 | tf_op jit(solution)/shard_map/ppermute | solution.py:423
  25.0 0.0 collective-permute-done.3.refs_1_
  25.0 0.0 collective-permute-done.2.refs_0_
  25.1 2.1 %collective-permute-start.6 = (bf16[1,2,128,512]{3,2,1,0:T(8,128)(2,1)S(1)}, bf16[1,2,128,512]{3,2,1,0:T(8,128)(2,1)S(1)}, u32[]{:S(2)}, u32[]{:S(2)}) collective-permute-start(bf16[1,2,128,512]{3,2,1,0:T(8,128)(2,1)S(1)} %shard_map.71.refs_0_), channel_id=1, source_target_pairs={{0,16},{16,0},{1,17},{17,1},{2,18},{18,2},{3,19},{19,3},{4,20},{20... | collective-permute-start | bytes 786440 | tf_op jit(solution)/shard_map/ppermute | solution.py:398
  27.2 1.5 %shard_map.72.refs_3_ = f32[1,2,16,128]{3,2,1,0:T(8,128)S(1)} custom-call(bf16[16,2,256,512]{3,2,1,0:T(8,128)(2,1)S(1)} %get-tuple-element.22.records.held, f32[4,2,2,128]{3,2,1,0:T(2,128)S(1)} %get-tuple-element.23.turn, f32[4,1,512]{2,1,0:T(1,128)S(1)} %get-tuple-element.24.used, bf16[1,2,128,512]{3,2,1,0:T(8,128)(2,1)S(1)} %shard_map.71.refs_0_), custom_call_target="tpu_custom_call" | custom-call | tf_op jit(solution)/shard_map/pallas_call | solution.py:295
  28.7 1.4 %collective-permute-done.4.refs_4_ = bf16[1,2,128,512]{3,2,1,0:T(8,128)(2,1)S(1)} collective-permute-done((bf16[1,2,128,512]{3,2,1,0:T(8,128)(2,1)S(1)}, bf16[1,2,128,512]{3,2,1,0:T(8,128)(2,1)S(1)}, u32[]{:S(2)}, u32[]{:S(2)}) %collective-permute-start.4) | collective-permute-done | bytes 262176 | tf_op jit(solution)/shard_map/ppermute | solution.py:423
  30.2 0.0 collective-permute-done.5.refs_5_
  30.2 1.4 %collective-permute-done.6.refs_6_ = bf16[1,2,128,512]{3,2,1,0:T(8,128)(2,1)S(1)} collective-permute-done((bf16[1,2,128,512]{3,2,1,0:T(8,128)(2,1)S(1)}, bf16[1,2,128,512]{3,2,1,0:T(8,128)(2,1)S(1)}, u32[]{:S(2)}, u32[]{:S(2)}) %collective-permute-start.6) | collective-permute-done | bytes 262176 | tf_op jit(solution)/shard_map/ppermute | solution.py:398
  31.5 1.5 %shard_map.73 = (f32[4,16,256]{2,1,0:T(8,128)S(1)}, f32[4,16,256]{2,1,0:T(8,128)S(1)}, f32[4,16,256]{2,1,0:T(8,128)S(1)}, f32[4,16,256]{2,1,0:T(8,128)S(1)}) custom-call(bf16[16,2,256,512]{3,2,1,0:T(8,128)(2,1)S(1)} %get-tuple-element.22.records.held, f32[4,2,2,128]{3,2,1,0:T(2,128)S(1)} %get-tuple-element.23.turn, f32[4,1,512]{2,1,0:T(1,128)S(1)} %get-tuple-element.24.used, ...), custom_call_target="tpu_custom_call" | custom-call | tf_op jit(solution)/shard_map/pallas_call | solution.py:325
  33.0 0.1 collective-permute-start.7
  33.1 1.6 %collective-permute-start.8 = (f32[4,16,256]{2,1,0:T(8,128)S(1)}, f32[4,16,256]{2,1,0:T(8,128)S(1)}, u32[]{:S(2)}, u32[]{:S(2)}) collective-permute-start(f32[4,16,256]{2,1,0:T(8,128)S(1)} %get-tuple-element.37), channel_id=1, source_target_pairs={{0,2},{1,3},{2,0},{3,1},{4,6},{5,7},{6,4},{7,5},{8,10},{9,11},{10,... | collective-permute-start | bytes 196616 | tf_op jit(solution)/shard_map/ppermute | solution.py:438
  34.7 0.3 collective-permute-start.9
  35.0 0.0 collective-permute-done.7.refs_1_
  35.0 2.6 %collective-permute-done.8.refs_2_ = f32[4,16,256]{2,1,0:T(8,128)S(1)} collective-permute-done((f32[4,16,256]{2,1,0:T(8,128)S(1)}, f32[4,16,256]{2,1,0:T(8,128)S(1)}, u32[]{:S(2)}, u32[]{:S(2)}) %collective-permute-start.8) | collective-permute-done | bytes 65568 | tf_op jit(solution)/shard_map/ppermute | solution.py:438
  37.6 1.1 %collective-permute-done.9.refs_3_ = f32[4,16,256]{2,1,0:T(8,128)S(1)} collective-permute-done((f32[4,16,256]{2,1,0:T(8,128)S(1)}, f32[4,16,256]{2,1,0:T(8,128)S(1)}, u32[]{:S(2)}, u32[]{:S(2)}) %collective-permute-start.9) | collective-permute-done | bytes 65568 | tf_op jit(solution)/shard_map/ppermute | solution.py:438
  38.7 0.6 %shard_map.74 = f32[4,16,256]{2,1,0:T(8,128)} custom-call(f32[4,16,256]{2,1,0:T(8,128)S(1)} %get-tuple-element.35.refs_0_, f32[4,16,256]{2,1,0:T(8,128)S(1)} %collective-permute-done.7.refs_1_, f32[4,16,256]{2,1,0:T(8,128)S(1)} %collective-permute-done.8.refs_2_, f32[4,16,256]{2,1,0:T(8,128)S(1)} %collective-permute-done.9.refs_3_), custom_call_target="tpu_custom_call" | custom-call | tf_op jit(solution)/shard_map/pallas_call | solution.py:452
  (3 shorter events, 0.1 us)
Async XLA Ops:
  1.0 16.9 %collective-permute-start.1 = (bf16[1,2,128,512]{3,2,1,0:T(8,128)(2,1)S(1)}, bf16[1,2,128,512]{3,2,1,0:T(8,128)(2,1)S(1)}, u32[]{:S(2)}, u32[]{:S(2)}) collective-permute-start(bf16[1,2,128,512]{3,2,1,0:T(8,128)(2,1)S(1)} %shard_map.66.refs_0_), channel_id=1, source_target_pairs={{0,8},{4,12},{8,0},{12,4},{1,9},{5,13},{9,1},{13,5},{2,10},{6,14},... | collective-permute-start | bytes 786440 | tf_op jit(solution)/shard_map/ppermute | solution.py:443
  5.1 12.8 %collective-permute-start = (bf16[1,2,128,512]{3,2,1,0:T(8,128)(2,1)S(1)}, bf16[1,2,128,512]{3,2,1,0:T(8,128)(2,1)S(1)}, u32[]{:S(2)}, u32[]{:S(2)}) collective-permute-start(bf16[1,2,128,512]{3,2,1,0:T(8,128)(2,1)S(1)} %shard_map.67), channel_id=1, source_target_pairs={{0,4},{4,0},{8,12},{12,8},{1,5},{5,1},{9,13},{13,9},{2,6},{6,2},{1... | collective-permute-start | bytes 786440 | tf_op jit(solution)/shard_map/ppermute | solution.py:444
  10.6 14.4 %collective-permute-start.3 = (bf16[1,2,128,512]{3,2,1,0:T(8,128)(2,1)S(1)}, bf16[1,2,128,512]{3,2,1,0:T(8,128)(2,1)S(1)}, u32[]{:S(2)}, u32[]{:S(2)}) collective-permute-start(bf16[1,2,128,512]{3,2,1,0:T(8,128)(2,1)S(1)} %shard_map.67), channel_id=1, source_target_pairs={{0,0},{4,8},{8,4},{12,12},{1,1},{5,9},{9,5},{13,13},{2,2},{6,10},{... | collective-permute-start | bytes 786440 | tf_op jit(solution)/shard_map/ppermute | solution.py:416
  17.9 7.2 %collective-permute-start.2 = (bf16[1,2,128,512]{3,2,1,0:T(8,128)(2,1)S(1)}, bf16[1,2,128,512]{3,2,1,0:T(8,128)(2,1)S(1)}, u32[]{:S(2)}, u32[]{:S(2)}) collective-permute-start(bf16[1,2,128,512]{3,2,1,0:T(8,128)(2,1)S(1)} %collective-permute-done.1.refs_0_), channel_id=1, source_target_pairs={{0,4},{4,0},{8,12},{12,8},{1,5},{5,1},{9,13},{13,9},{2,6},{6,2},{1... | collective-permute-start | bytes 786440 | tf_op jit(solution)/shard_map/ppermute | solution.py:418
  17.9 12.3 %collective-permute-start.5 = (bf16[1,2,128,512]{3,2,1,0:T(8,128)(2,1)S(1)}, bf16[1,2,128,512]{3,2,1,0:T(8,128)(2,1)S(1)}, u32[]{:S(2)}, u32[]{:S(2)}) collective-permute-start(bf16[1,2,128,512]{3,2,1,0:T(8,128)(2,1)S(1)} %shard_map.68.refs_1_), channel_id=1, source_target_pairs={{0,16},{16,0},{1,17},{17,1},{2,18},{18,2},{3,19},{19,3},{4,20},{20... | collective-permute-start | bytes 786440 | tf_op jit(solution)/shard_map/ppermute | solution.py:398
  23.0 7.2 %collective-permute-start.4 = (bf16[1,2,128,512]{3,2,1,0:T(8,128)(2,1)S(1)}, bf16[1,2,128,512]{3,2,1,0:T(8,128)(2,1)S(1)}, u32[]{:S(2)}, u32[]{:S(2)}) collective-permute-start(bf16[1,2,128,512]{3,2,1,0:T(8,128)(2,1)S(1)} %get-tuple-element.34), channel_id=1, source_target_pairs={{0,4},{4,0},{8,12},{12,8},{1,5},{5,1},{9,13},{13,9},{2,6},{6,2},{1... | collective-permute-start | bytes 786440 | tf_op jit(solution)/shard_map/ppermute | solution.py:423
  25.1 6.5 %collective-permute-start.6 = (bf16[1,2,128,512]{3,2,1,0:T(8,128)(2,1)S(1)}, bf16[1,2,128,512]{3,2,1,0:T(8,128)(2,1)S(1)}, u32[]{:S(2)}, u32[]{:S(2)}) collective-permute-start(bf16[1,2,128,512]{3,2,1,0:T(8,128)(2,1)S(1)} %shard_map.71.refs_0_), channel_id=1, source_target_pairs={{0,16},{16,0},{1,17},{17,1},{2,18},{18,2},{3,19},{19,3},{4,20},{20... | collective-permute-start | bytes 786440 | tf_op jit(solution)/shard_map/ppermute | solution.py:398
  33.0 1.9 %collective-permute-start.7 = (f32[4,16,256]{2,1,0:T(8,128)S(1)}, f32[4,16,256]{2,1,0:T(8,128)S(1)}, u32[]{:S(2)}, u32[]{:S(2)}) collective-permute-start(f32[4,16,256]{2,1,0:T(8,128)S(1)} %get-tuple-element.36), channel_id=1, source_target_pairs={{0,1},{1,0},{2,3},{3,2},{4,5},{5,4},{6,7},{7,6},{8,9},{9,8},{10,11... | collective-permute-start | bytes 196616 | tf_op jit(solution)/shard_map/ppermute | solution.py:438
  33.1 4.5 %collective-permute-start.8 = (f32[4,16,256]{2,1,0:T(8,128)S(1)}, f32[4,16,256]{2,1,0:T(8,128)S(1)}, u32[]{:S(2)}, u32[]{:S(2)}) collective-permute-start(f32[4,16,256]{2,1,0:T(8,128)S(1)} %get-tuple-element.37), channel_id=1, source_target_pairs={{0,2},{1,3},{2,0},{3,1},{4,6},{5,7},{6,4},{7,5},{8,10},{9,11},{10,... | collective-permute-start | bytes 196616 | tf_op jit(solution)/shard_map/ppermute | solution.py:438
  34.7 4.0 %collective-permute-start.9 = (f32[4,16,256]{2,1,0:T(8,128)S(1)}, f32[4,16,256]{2,1,0:T(8,128)S(1)}, u32[]{:S(2)}, u32[]{:S(2)}) collective-permute-start(f32[4,16,256]{2,1,0:T(8,128)S(1)} %get-tuple-element.38), channel_id=1, source_target_pairs={{0,3},{1,2},{2,1},{3,0},{4,7},{5,6},{6,5},{7,4},{8,11},{9,10},{10,... | collective-permute-start | bytes 196616 | tf_op jit(solution)/shard_map/ppermute | solution.py:438

commit v6 on v5

--- a/solution.py
+++ b/solution.py
@@ -113,21 +113,20 @@
     return turned
 
 
-def all_lags(parts, high, low):
-    windows = parts[0][0].shape[0]
-    straight = jnp.concatenate([v for real, imag in parts for v in (real, imag)], axis=1)
-    turned = jnp.concatenate([v for real, imag in parts for v in (imag, -real)], axis=1)
+def half_lags(real, imag, high, low):
+    windows = real.shape[0]
+    straight = jnp.concatenate([real, imag], axis=1)
+    turned = jnp.concatenate([imag, -real], axis=1)
     lane = lax.broadcasted_iota(jnp.int32, straight.shape, 1) % 4
     picked = [jnp.where(lane == r, straight, 0.0) for r in range(4)]
     picked += [jnp.where(lane == r, turned, 0.0) for r in (1, 3)]
     rows = jnp.concatenate(picked, axis=0)
     rows_high, rows_low = two_halves(rows)
-    table_high, table_low = (jnp.concatenate([t[r] for r in range(len(parts))], axis=0) for t in (high, low))
-    both = product(jnp.concatenate([rows_high, rows_low], axis=0), table_high, (1, 0))
-    sums = both[: rows.shape[0]] + both[rows.shape[0] :] + product(rows_high, table_low, (1, 0))
+    both = product(jnp.concatenate([rows_high, rows_low], axis=0), high, (1, 0))
+    sums = both[: rows.shape[0]] + both[rows.shape[0] :] + product(rows_high, low, (1, 0))
     re0, re1, re2, re3, im1, im3 = (sums[i * windows : (i + 1) * windows] for i in range(6))
     even, odd, even_turned, odd_turned = re0 + re2, re1 + re3, re0 - re2, im1 - im3
-    return [even + odd, even_turned - odd_turned, even - odd, even_turned + odd_turned]
+    return jnp.concatenate([even + odd, even_turned - odd_turned, even - odd, even_turned + odd_turned], axis=1)
 
 
 def own_kernel(
@@ -205,32 +204,47 @@
         out[i, 1] = imag
 
 
-def lags_kernel(plan, held, turn, used, high, low, flipped, *refs):
-    ds, counts, known = plan
-    *refs, spectra, lags = refs
-    outs = refs[-lags.shape[0] :]
+def early_lags_kernel(plan, held, turn, used, high, low, *refs):
+    ds, counts, known, whole = plan
+    *refs, out, spectra = refs
     for ref, (first, place) in zip(refs, known):
         for i in range(ref.shape[0]):
             spectra[first + i, half_at(place)] = ref[i]
-    entries = entries_of(ds, counts, refs[len(known) : -lags.shape[0]])
-    found = half_spectra(entries, half_at(OTHER), held, turn, used, flipped=flipped)
+    entries = entries_of(ds, counts, refs[len(known) :])
+    found = half_spectra(entries, half_at(OWN), held, turn, used)
+    total, windows = out.shape[:2]
     for i, (real, imag) in enumerate(found):
-        at = spectra.shape[0] - len(entries) + i
-        spectra[at, half_at(OTHER), 0] = real
-        spectra[at, half_at(OTHER), 1] = imag
+        at = total - len(entries) + i
+        spectra[at, half_at(OWN), 0] = real
+        spectra[at, half_at(OWN), 1] = imag
+    for count, place in ((total, OWN), (whole, OTHER)):
+        half = half_at(place)
+        if count:
+            real, imag = (jnp.concatenate([spectra[i, half, p] for i in range(count)], axis=0) for p in range(2))
+            lags = half_lags(real, imag, high[half], low[half])
+            for i in range(count):
+                add = lags[i * windows : (i + 1) * windows]
+                out[i] = add if place == OWN else out[i] + add
+
+
+def lags_kernel(plan, held, turn, used, high, low, flipped, early, *refs):
+    ds, counts = plan
+    *refs, lags = refs
+    blocks, windows, width = lags.shape
+    outs = refs[-blocks:]
+    entries = entries_of(ds, counts, refs[:-blocks])
+    half = half_at(OTHER)
+    found = half_spectra(entries, half, held, turn, used, flipped=flipped)
+    real, imag = (jnp.concatenate([f[p] for f in found], axis=0) for p in range(2))
+    late = half_lags(real, imag, high[half], low[half])
     me = lax.axis_index("chan") * lax.axis_size("freq") + lax.axis_index("freq")
-    blocks, windows, width = lags.shape
-    total, halves = spectra.shape[:2]
-    parts = [
-        tuple(jnp.concatenate([spectra[i, h, part] for i in range(total)], axis=0) for part in range(2))
-        for h in range(halves)
-    ]
-    folded = all_lags(parts, high, low)
-    for i in range(total):
-        at = slice(i * windows, (i + 1) * windows)
+    whole = early.shape[0] - len(entries)
+    for i in range(early.shape[0]):
         for n in range(blocks):
-            start = n * width
-            lags[n] = folded[start // FOLD][at, start % FOLD : start % FOLD + width]
+            at = slice(n * width, (n + 1) * width)
+            lags[n] = early[i, :, at]
+            if i >= whole:
+                lags[n] += late[(i - whole) * windows : (i - whole + 1) * windows, at]
         for n in range(blocks):
             outs[n][i] = lags[me ^ n]
 
@@ -312,25 +326,36 @@
     )(*in_vmem(held[:1]))
 
 
-def lag_blocks(held, flipped, known, entries, count, blocks):
+def early_lags(held, known, entries, count, whole):
     windows = held[0].shape[0]
-    halves = held[0].shape[2] // HALF
-    block = (windows, NSAMP // blocks)
     plan = (
         tuple(d for d, _ in entries),
         tuple(len(pieces) for _, pieces in entries),
         tuple((first, place) for _, first, place in known),
+        whole,
     )
-    operands = in_vmem([*held, flipped, *(k[0] for k in known), *(piece for _, pieces in entries for piece in pieces)])
+    operands = in_vmem([*held, *(k[0] for k in known), *(piece for _, pieces in entries for piece in pieces)])
+    return pl.pallas_call(
+        functools.partial(early_lags_kernel, plan),
+        in_specs=[IN_VMEM] * len(operands),
+        out_specs=IN_VMEM,
+        out_shape=pltpu.VMEM((count, windows, NSAMP), jnp.float32),
+        scratch_shapes=[pltpu.VMEM((count, held[0].shape[2] // HALF, 2, windows, HALF), jnp.float32)],
+        compiler_params=PARAMS,
+    )(*operands)
+
+
+def lag_blocks(held, flipped, early, entries, blocks):
+    count, windows, _ = early.shape
+    block = (windows, NSAMP // blocks)
+    plan = (tuple(d for d, _ in entries), tuple(len(pieces) for _, pieces in entries))
+    operands = in_vmem([*held, flipped, early, *(piece for _, pieces in entries for piece in pieces)])
     return pl.pallas_call(
         functools.partial(lags_kernel, plan),
         in_specs=[IN_VMEM] * len(operands),
         out_specs=[IN_VMEM] * blocks,
         out_shape=[jax.ShapeDtypeStruct((count,) + block, jnp.float32)] * blocks,
-        scratch_shapes=[
-            pltpu.VMEM((count, halves, 2, windows, HALF), jnp.float32),
-            pltpu.VMEM((blocks,) + block, jnp.float32),
-        ],
+        scratch_shapes=[pltpu.VMEM((blocks,) + block, jnp.float32)],
         compiler_params=PARAMS,
     )(*operands)
 
@@ -406,8 +431,9 @@
         away = [d for d in order if d]
         arrived = [lax.ppermute(mine, "blk", partners(n_blk, d)) for d in away]
         known = [] if begin else [(spectra, 0, 0), (early_half(held, [(0, [rest])], 1), 0, 1)]
-        known.append((early_half(held, [(d, [a]) for d, a in zip(away, arrived)], OWN), len(order) - len(away), OWN))
-        parts += exchange(lags_of(known, [(d, [swap(a)]) for d, a in zip(away, arrived)], len(order)))
+        whole = len(order) - len(away)
+        early = early_lags(held, known, [(d, [a]) for d, a in zip(away, arrived)], len(order), whole)
+        parts += exchange(lags_of(early, [(d, [swap(a)]) for d, a in zip(away, arrived)]))
         orders.append(order)
     return orders, parts
 
@@ -423,9 +449,9 @@
     near_rest = lax.ppermute(after(theirs, rest_half), "blk", partners(4, 1))
     third = join(ends, middle)
     third_swapped = swap(third)
-    known = [(spectra, 0, 0), (rest_half, 0, 1), (pair, 1, OWN), (early_half(held, [(3, [third])], OWN), 3, OWN)]
+    early = early_lags(held, [(spectra, 0, 0), (rest_half, 0, 1), (pair, 1, OWN)], [(3, [third])], 4, 1)
     late = [(1, [near_rest]), (2, [swapped]), (3, [third_swapped])]
-    return [(0, 1, 2, 3)], exchange(lags_of(known, late, 4))
+    return [(0, 1, 2, 3)], exchange(lags_of(early, late))
 
 
 def shards(records, templates, masks, offsets):

time: 39.6 us -> 39.4 us (level)
  waiting for transfers between devices: 12 us -> 11.6 us
    pallas_call x0 -> x1, Pallas kernels: none -> 1.88 us  [early_lags(): pl.pallas_call(functools.partial(early_lags_kernel, plan), in_specs=[IN_V...]
    pallas_call x3 -> x2, Pallas kernels: 4.69 us -> 3.15 us  [early_half(): pl.pallas_call(functools.partial(pieces_kernel, plan), in_specs=[IN_VMEM]...]
  transfers between devices with their start and end apart: 10 -> 10, of which waited for: 5 -> 5; matrix products, arithmetic and copies ran while one was open for 0% -> 0% of each run, Pallas kernels for 25% -> 26%
where the time goes in v6:
time: 39.4 us; the launch traced here: 39.2 us
  starting transfers between devices  14.5 us (37%)
  Pallas kernels  13 us (33%)
  waiting for transfers between devices  11.6 us (29%)
    ppermute x1, waiting for transfers between devices, shards(): lax.ppermute(piece, 'blk', partners(n_blk, 2))  5.43 us
    ppermute x1, starting transfers between devices, shards(): lax.ppermute(piece, 'blk', partners(n_blk, 2))  4.1 us
    ppermute x2, starting transfers between devices, swap(): return lax.ppermute(piece, 'parts', partners(2, 1))  4.06 us
    pallas_call x1, Pallas kernels, own_template(): pl.pallas_call(own_kernel, in_specs=[IN_HBM] * 6, out_specs=[IN_VMEM] * l...  3.87 us
    ppermute x3, waiting for transfers between devices, exchange(): lax.ppermute(found[n], ('chan', 'freq'), partners(blocks, n))  3.74 us
    pallas_call x2, Pallas kernels, early_half(): pl.pallas_call(functools.partial(pieces_kernel, plan), in_specs=[IN_VMEM]...  3.15 us
    ppermute x1, starting transfers between devices, line_of_four(): near_rest = lax.ppermute(after(theirs, rest_half), 'blk', partners(4, 1))  2.04 us
    ppermute x3, starting transfers between devices, exchange(): lax.ppermute(found[n], ('chan', 'freq'), partners(blocks, n))  1.93 us
  transfers between devices with their start and end apart: 10, of which 5 were waited for; matrix products, arithmetic and copies ran while one was open for 0% of the time, Pallas kernels for 26%

profile of v6, /device:TPU:0, one launch (start us, length us, event | category | flops | bytes accessed | tf_op | source)
XLA Modules:
  0.0 39.2 jit_solution(11454769960033420599)
XLA Ops:
  0.0 1.0 %shard_map.66.refs_0_ = bf16[1,2,128,512]{3,2,1,0:T(8,128)(2,1)S(1)} custom-call(bf16[1,2,256,512]{3,2,1,0:T(8,128)(2,1)} %template.1), custom_call_target="tpu_custom_call" | custom-call | tf_op jit(solution)/shard_map/pallas_call | solution.py:379
  1.0 4.1 %collective-permute-start.1 = (bf16[1,2,128,512]{3,2,1,0:T(8,128)(2,1)S(1)}, bf16[1,2,128,512]{3,2,1,0:T(8,128)(2,1)S(1)}, u32[]{:S(2)}, u32[]{:S(2)}) collective-permute-start(bf16[1,2,128,512]{3,2,1,0:T(8,128)(2,1)S(1)} %shard_map.66.refs_0_), channel_id=1, source_target_pairs={{0,8},{4,12},{8,0},{12,4},{1,9},{5,13},{9,1},{13,5},{2,10},{6,14},... | collective-permute-start | bytes 786440 | tf_op jit(solution)/shard_map/ppermute | solution.py:469
  5.1 1.6 %collective-permute-start = (bf16[1,2,128,512]{3,2,1,0:T(8,128)(2,1)S(1)}, bf16[1,2,128,512]{3,2,1,0:T(8,128)(2,1)S(1)}, u32[]{:S(2)}, u32[]{:S(2)}) collective-permute-start(bf16[1,2,128,512]{3,2,1,0:T(8,128)(2,1)S(1)} %shard_map.67), channel_id=1, source_target_pairs={{0,4},{4,0},{8,12},{12,8},{1,5},{5,1},{9,13},{13,9},{2,6},{6,2},{1... | collective-permute-start | bytes 786440 | tf_op jit(solution)/shard_map/ppermute | solution.py:470
  6.7 3.9 %shard_map.64 = (bf16[16,2,256,512]{3,2,1,0:T(8,128)(2,1)S(1)}, f32[4,2,2,128]{3,2,1,0:T(2,128)S(1)}, f32[4,1,512]{2,1,0:T(1,128)S(1)}, bf16[2,256,256]{2,1,0:T(...) custom-call(s32[4,4]{1,0:T(4,128)} %masks.1, ...), custom_call_target="tpu_custom_call" | custom-call | tf_op jit(solution)/shard_map/pallas_call | solution.py:290
  10.6 0.7 %collective-permute-start.3 = (bf16[1,2,128,512]{3,2,1,0:T(8,128)(2,1)S(1)}, bf16[1,2,128,512]{3,2,1,0:T(8,128)(2,1)S(1)}, u32[]{:S(2)}, u32[]{:S(2)}) collective-permute-start(bf16[1,2,128,512]{3,2,1,0:T(8,128)(2,1)S(1)} %shard_map.67), channel_id=1, source_target_pairs={{0,0},{4,8},{8,4},{12,12},{1,1},{5,9},{9,5},{13,13},{2,2},{6,10},{... | collective-permute-start | bytes 786440 | tf_op jit(solution)/shard_map/ppermute | solution.py:442
  11.3 1.1 %shard_map.65.flipped = bf16[8,1024,256]{2,1,0:T(8,128)(2,1)S(1)} custom-call(bf16[16,2,256,512]{3,2,1,0:T(8,128)(2,1)S(1)} %get-tuple-element.22.records.held), custom_call_target="tpu_custom_call" | custom-call | tf_op jit(solution)/shard_map/pallas_call | solution.py:320
  12.4 5.4 %collective-permute-done.1.refs_0_ = bf16[1,2,128,512]{3,2,1,0:T(8,128)(2,1)S(1)} collective-permute-done((bf16[1,2,128,512]{3,2,1,0:T(8,128)(2,1)S(1)}, bf16[1,2,128,512]{3,2,1,0:T(8,128)(2,1)S(1)}, u32[]{:S(2)}, u32[]{:S(2)}) %collective-permute-start.1) | collective-permute-done | bytes 262176 | tf_op jit(solution)/shard_map/ppermute | solution.py:469
  17.9 0.0 collective-permute-start.2
  17.9 0.0 collective-permute-done.refs_0_
  17.9 1.9 %collective-permute-start.5 = (bf16[1,2,128,512]{3,2,1,0:T(8,128)(2,1)S(1)}, bf16[1,2,128,512]{3,2,1,0:T(8,128)(2,1)S(1)}, u32[]{:S(2)}, u32[]{:S(2)}) collective-permute-start(bf16[1,2,128,512]{3,2,1,0:T(8,128)(2,1)S(1)} %shard_map.68.refs_1_), channel_id=1, source_target_pairs={{0,16},{16,0},{1,17},{17,1},{2,18},{18,2},{3,19},{19,3},{4,20},{20... | collective-permute-start | bytes 786440 | tf_op jit(solution)/shard_map/ppermute | solution.py:423
  19.8 1.6 %shard_map.69.refs_2_ = f32[2,2,16,128]{3,2,1,0:T(8,128)S(1)} custom-call(bf16[16,2,256,512]{3,2,1,0:T(8,128)(2,1)S(1)} %get-tuple-element.22.records.held, f32[4,2,2,128]{3,2,1,0:T(2,128)S(1)} %get-tuple-element.23.turn, f32[4,1,512]{2,1,0:T(1,128)S(1)} %get-tuple-element.24.used, bf16[1,2,128,512]{3,2,1,0:T(8,128)(2,1)S(1)} %collective-permute-done.refs_0_, ...), custom_call_target="tpu_custom_call" | custom-call | tf_op jit(solution)/shard_map/pallas_call | solution.py:309
  21.4 1.5 %shard_map.70.refs_1_ = f32[1,2,16,128]{3,2,1,0:T(8,128)S(1)} custom-call(bf16[16,2,256,512]{3,2,1,0:T(8,128)(2,1)S(1)} %get-tuple-element.22.records.held, f32[4,2,2,128]{3,2,1,0:T(2,128)S(1)} %get-tuple-element.23.turn, f32[4,1,512]{2,1,0:T(1,128)S(1)} %get-tuple-element.24.used, bf16[1,2,128,512]{3,2,1,0:T(8,128)(2,1)S(1)} %get-tuple-element.31.refs_0_), custom_call_target="tpu_custom_call" | custom-call | tf_op jit(solution)/shard_map/pallas_call | solution.py:309
  23.0 2.0 %collective-permute-start.4 = (bf16[1,2,128,512]{3,2,1,0:T(8,128)(2,1)S(1)}, bf16[1,2,128,512]{3,2,1,0:T(8,128)(2,1)S(1)}, u32[]{:S(2)}, u32[]{:S(2)}) collective-permute-start(bf16[1,2,128,512]{3,2,1,0:T(8,128)(2,1)S(1)} %get-tuple-element.34), channel_id=1, source_target_pairs={{0,4},{4,0},{8,12},{12,8},{1,5},{5,1},{9,13},{13,9},{2,6},{6,2},{1... | collective-permute-start | bytes 786440 | tf_op jit(solution)/shard_map/ppermute | solution.py:449
  25.0 0.0 collective-permute-done.3.refs_1_
  25.0 0.0 collective-permute-done.2.refs_0_
  25.1 2.1 %collective-permute-start.6 = (bf16[1,2,128,512]{3,2,1,0:T(8,128)(2,1)S(1)}, bf16[1,2,128,512]{3,2,1,0:T(8,128)(2,1)S(1)}, u32[]{:S(2)}, u32[]{:S(2)}) collective-permute-start(bf16[1,2,128,512]{3,2,1,0:T(8,128)(2,1)S(1)} %shard_map.71.refs_3_), channel_id=1, source_target_pairs={{0,16},{16,0},{1,17},{17,1},{2,18},{18,2},{3,19},{19,3},{4,20},{20... | collective-permute-start | bytes 786440 | tf_op jit(solution)/shard_map/ppermute | solution.py:423
  27.2 1.9 %shard_map.72.early = f32[4,16,1024]{2,1,0:T(8,128)S(1)} custom-call(bf16[16,2,256,512]{3,2,1,0:T(8,128)(2,1)S(1)} %get-tuple-element.22.records.held, f32[4,2,2,128]{3,2,1,0:T(2,128)S(1)} %get-tuple-element.23.turn, f32[4,1,512]{2,1,0:T(1,128)S(1)} %get-tuple-element.24.used, bf16[2,256,256]{2,1,0:T(8,128)(2,1)S(1)} %get-tuple-element.25.high, ...), custom_call_target="tpu_custom_call" | custom-call | tf_op jit(solution)/shard_map/pallas_call | solution.py:338
  29.1 1.1 %collective-permute-done.4.refs_0_ = bf16[1,2,128,512]{3,2,1,0:T(8,128)(2,1)S(1)} collective-permute-done((bf16[1,2,128,512]{3,2,1,0:T(8,128)(2,1)S(1)}, bf16[1,2,128,512]{3,2,1,0:T(8,128)(2,1)S(1)}, u32[]{:S(2)}, u32[]{:S(2)}) %collective-permute-start.4) | collective-permute-done | bytes 262176 | tf_op jit(solution)/shard_map/ppermute | solution.py:449
  30.2 0.0 collective-permute-done.5.refs_1_
  30.2 1.4 %collective-permute-done.6.refs_2_ = bf16[1,2,128,512]{3,2,1,0:T(8,128)(2,1)S(1)} collective-permute-done((bf16[1,2,128,512]{3,2,1,0:T(8,128)(2,1)S(1)}, bf16[1,2,128,512]{3,2,1,0:T(8,128)(2,1)S(1)}, u32[]{:S(2)}, u32[]{:S(2)}) %collective-permute-start.6) | collective-permute-done | bytes 262176 | tf_op jit(solution)/shard_map/ppermute | solution.py:423
  31.5 1.3 %shard_map.73 = (f32[4,16,256]{2,1,0:T(8,128)S(1)}, f32[4,16,256]{2,1,0:T(8,128)S(1)}, f32[4,16,256]{2,1,0:T(8,128)S(1)}, f32[4,16,256]{2,1,0:T(8,128)S(1)}) custom-call(bf16[16,2,256,512]{3,2,1,0:T(8,128)(2,1)S(1)} %get-tuple-element.22.records.held, f32[4,2,2,128]{3,2,1,0:T(2,128)S(1)} %get-tuple-element.23.turn, f32[4,1,512]{2,1,0:T(1,128)S(1)} %get-tuple-element.24.used, ...), custom_call_target="tpu_custom_call" | custom-call | tf_op jit(solution)/shard_map/pallas_call | solution.py:353
  32.9 0.1 collective-permute-start.7
  32.9 1.6 %collective-permute-start.8 = (f32[4,16,256]{2,1,0:T(8,128)S(1)}, f32[4,16,256]{2,1,0:T(8,128)S(1)}, u32[]{:S(2)}, u32[]{:S(2)}) collective-permute-start(f32[4,16,256]{2,1,0:T(8,128)S(1)} %get-tuple-element.37), channel_id=1, source_target_pairs={{0,2},{1,3},{2,0},{3,1},{4,6},{5,7},{6,4},{7,5},{8,10},{9,11},{10,... | collective-permute-start | bytes 196616 | tf_op jit(solution)/shard_map/ppermute | solution.py:464
  34.5 0.3 collective-permute-start.9
  34.8 0.0 collective-permute-done.7.refs_1_
  34.8 2.6 %collective-permute-done.8.refs_2_ = f32[4,16,256]{2,1,0:T(8,128)S(1)} collective-permute-done((f32[4,16,256]{2,1,0:T(8,128)S(1)}, f32[4,16,256]{2,1,0:T(8,128)S(1)}, u32[]{:S(2)}, u32[]{:S(2)}) %collective-permute-start.8) | collective-permute-done | bytes 65568 | tf_op jit(solution)/shard_map/ppermute | solution.py:464
  37.4 1.1 %collective-permute-done.9.refs_3_ = f32[4,16,256]{2,1,0:T(8,128)S(1)} collective-permute-done((f32[4,16,256]{2,1,0:T(8,128)S(1)}, f32[4,16,256]{2,1,0:T(8,128)S(1)}, u32[]{:S(2)}, u32[]{:S(2)}) %collective-permute-start.9) | collective-permute-done | bytes 65568 | tf_op jit(solution)/shard_map/ppermute | solution.py:464
  38.5 0.6 %shard_map.74 = f32[4,16,256]{2,1,0:T(8,128)} custom-call(f32[4,16,256]{2,1,0:T(8,128)S(1)} %get-tuple-element.35.refs_0_, f32[4,16,256]{2,1,0:T(8,128)S(1)} %collective-permute-done.7.refs_1_, f32[4,16,256]{2,1,0:T(8,128)S(1)} %collective-permute-done.8.refs_2_, f32[4,16,256]{2,1,0:T(8,128)S(1)} %collective-permute-done.9.refs_3_), custom_call_target="tpu_custom_call" | custom-call | tf_op jit(solution)/shard_map/pallas_call | solution.py:478
  (3 shorter events, 0.1 us)
Async XLA Ops:
  1.0 16.9 %collective-permute-start.1 = (bf16[1,2,128,512]{3,2,1,0:T(8,128)(2,1)S(1)}, bf16[1,2,128,512]{3,2,1,0:T(8,128)(2,1)S(1)}, u32[]{:S(2)}, u32[]{:S(2)}) collective-permute-start(bf16[1,2,128,512]{3,2,1,0:T(8,128)(2,1)S(1)} %shard_map.66.refs_0_), channel_id=1, source_target_pairs={{0,8},{4,12},{8,0},{12,4},{1,9},{5,13},{9,1},{13,5},{2,10},{6,14},... | collective-permute-start | bytes 786440 | tf_op jit(solution)/shard_map/ppermute | solution.py:469
  5.1 12.8 %collective-permute-start = (bf16[1,2,128,512]{3,2,1,0:T(8,128)(2,1)S(1)}, bf16[1,2,128,512]{3,2,1,0:T(8,128)(2,1)S(1)}, u32[]{:S(2)}, u32[]{:S(2)}) collective-permute-start(bf16[1,2,128,512]{3,2,1,0:T(8,128)(2,1)S(1)} %shard_map.67), channel_id=1, source_target_pairs={{0,4},{4,0},{8,12},{12,8},{1,5},{5,1},{9,13},{13,9},{2,6},{6,2},{1... | collective-permute-start | bytes 786440 | tf_op jit(solution)/shard_map/ppermute | solution.py:470
  10.6 14.4 %collective-permute-start.3 = (bf16[1,2,128,512]{3,2,1,0:T(8,128)(2,1)S(1)}, bf16[1,2,128,512]{3,2,1,0:T(8,128)(2,1)S(1)}, u32[]{:S(2)}, u32[]{:S(2)}) collective-permute-start(bf16[1,2,128,512]{3,2,1,0:T(8,128)(2,1)S(1)} %shard_map.67), channel_id=1, source_target_pairs={{0,0},{4,8},{8,4},{12,12},{1,1},{5,9},{9,5},{13,13},{2,2},{6,10},{... | collective-permute-start | bytes 786440 | tf_op jit(solution)/shard_map/ppermute | solution.py:442
  17.9 7.2 %collective-permute-start.2 = (bf16[1,2,128,512]{3,2,1,0:T(8,128)(2,1)S(1)}, bf16[1,2,128,512]{3,2,1,0:T(8,128)(2,1)S(1)}, u32[]{:S(2)}, u32[]{:S(2)}) collective-permute-start(bf16[1,2,128,512]{3,2,1,0:T(8,128)(2,1)S(1)} %collective-permute-done.1.refs_0_), channel_id=1, source_target_pairs={{0,4},{4,0},{8,12},{12,8},{1,5},{5,1},{9,13},{13,9},{2,6},{6,2},{1... | collective-permute-start | bytes 786440 | tf_op jit(solution)/shard_map/ppermute | solution.py:444
  17.9 12.3 %collective-permute-start.5 = (bf16[1,2,128,512]{3,2,1,0:T(8,128)(2,1)S(1)}, bf16[1,2,128,512]{3,2,1,0:T(8,128)(2,1)S(1)}, u32[]{:S(2)}, u32[]{:S(2)}) collective-permute-start(bf16[1,2,128,512]{3,2,1,0:T(8,128)(2,1)S(1)} %shard_map.68.refs_1_), channel_id=1, source_target_pairs={{0,16},{16,0},{1,17},{17,1},{2,18},{18,2},{3,19},{19,3},{4,20},{20... | collective-permute-start | bytes 786440 | tf_op jit(solution)/shard_map/ppermute | solution.py:423
  23.0 7.2 %collective-permute-start.4 = (bf16[1,2,128,512]{3,2,1,0:T(8,128)(2,1)S(1)}, bf16[1,2,128,512]{3,2,1,0:T(8,128)(2,1)S(1)}, u32[]{:S(2)}, u32[]{:S(2)}) collective-permute-start(bf16[1,2,128,512]{3,2,1,0:T(8,128)(2,1)S(1)} %get-tuple-element.34), channel_id=1, source_target_pairs={{0,4},{4,0},{8,12},{12,8},{1,5},{5,1},{9,13},{13,9},{2,6},{6,2},{1... | collective-permute-start | bytes 786440 | tf_op jit(solution)/shard_map/ppermute | solution.py:449
  25.1 6.5 %collective-permute-start.6 = (bf16[1,2,128,512]{3,2,1,0:T(8,128)(2,1)S(1)}, bf16[1,2,128,512]{3,2,1,0:T(8,128)(2,1)S(1)}, u32[]{:S(2)}, u32[]{:S(2)}) collective-permute-start(bf16[1,2,128,512]{3,2,1,0:T(8,128)(2,1)S(1)} %shard_map.71.refs_3_), channel_id=1, source_target_pairs={{0,16},{16,0},{1,17},{17,1},{2,18},{18,2},{3,19},{19,3},{4,20},{20... | collective-permute-start | bytes 786440 | tf_op jit(solution)/shard_map/ppermute | solution.py:423
  32.9 1.9 %collective-permute-start.7 = (f32[4,16,256]{2,1,0:T(8,128)S(1)}, f32[4,16,256]{2,1,0:T(8,128)S(1)}, u32[]{:S(2)}, u32[]{:S(2)}) collective-permute-start(f32[4,16,256]{2,1,0:T(8,128)S(1)} %get-tuple-element.36), channel_id=1, source_target_pairs={{0,1},{1,0},{2,3},{3,2},{4,5},{5,4},{6,7},{7,6},{8,9},{9,8},{10,11... | collective-permute-start | bytes 196616 | tf_op jit(solution)/shard_map/ppermute | solution.py:464
  32.9 4.5 %collective-permute-start.8 = (f32[4,16,256]{2,1,0:T(8,128)S(1)}, f32[4,16,256]{2,1,0:T(8,128)S(1)}, u32[]{:S(2)}, u32[]{:S(2)}) collective-permute-start(f32[4,16,256]{2,1,0:T(8,128)S(1)} %get-tuple-element.37), channel_id=1, source_target_pairs={{0,2},{1,3},{2,0},{3,1},{4,6},{5,7},{6,4},{7,5},{8,10},{9,11},{10,... | collective-permute-start | bytes 196616 | tf_op jit(solution)/shard_map/ppermute | solution.py:464
  34.5 4.0 %collective-permute-start.9 = (f32[4,16,256]{2,1,0:T(8,128)S(1)}, f32[4,16,256]{2,1,0:T(8,128)S(1)}, u32[]{:S(2)}, u32[]{:S(2)}) collective-permute-start(f32[4,16,256]{2,1,0:T(8,128)S(1)} %get-tuple-element.38), channel_id=1, source_target_pairs={{0,3},{1,2},{2,1},{3,0},{4,7},{5,6},{6,5},{7,4},{8,11},{9,10},{10,... | collective-permute-start | bytes 196616 | tf_op jit(solution)/shard_map/ppermute | solution.py:464
